TPU v7x, 32 devices: a whole 2x2x4 slice. The times are simulated.
32 devices in a mesh: dp: 4 (over x, core), mp: 8 (over z, y).
Axes of the slice: x: 2, y: 2, z: 4, core: 2. Of those that a mesh axis runs over, the one named last changes fastest.
Arguments:
- hidden: bfloat16 [1536, 26624], P('dp', 'mp'), may hold values from -6 to 6
- down_weight: bfloat16 [26624, 8192], P('mp', 'dp'), may hold values from -0.0390625 to 0.0390625
- adapter_down: bfloat16 [16, 26624, 64], P('dp', 'mp'), may hold values from -0.0390625 to 0.0390625
- adapter_up: bfloat16 [16, 64, 8192], P('dp', None, 'mp'), may hold values from -0.1875 to 0.1875
- output_grad: bfloat16 [1536, 8192], P('dp', 'mp'), may hold values from -6 to 6
- adapter_per_block: int32 [12], replicated, may hold values from 0 to 15, as said below
- live_rows: int32 [4], replicated, may hold values from 96 to 384, as said below
Outputs:
- layer_out: bfloat16 [1536, 8192], P('dp', 'mp')
- hidden_gradient: bfloat16 [1536, 26624], P('dp', 'mp')
- down_grad: bfloat16 [16, 26624, 64], P('dp', 'mp')
- up_grad: bfloat16 [16, 64, 8192], P('dp', None, 'mp')
Inputs may be any that keep to these rules, and one draw needn't show every extreme that they name: `adapter_per_block`: adapter k is owned by index k // 4 of dp; the 3 blocks of one index of dp use adapters of 3 different owners. `live_rows`: some index of dp has all 384 rows live.
All inputs are finite; a program needn't handle non-finite values.
Results may differ from a plain program's by a relative error of at most 0.0055.
Values may be sent and summed in bfloat16 or wider, within the bound.
No kernel may reach another device: no remote copies, remote signals or barrier semaphores. Data moves between devices by JAX's collectives and lax.ppermute only.
A program may use at most 192 MiB of HBM per device.

v0:
```python
import jax
import jax.numpy as jnp
from jax import lax
from jax.sharding import PartitionSpec as P

BLK = 128


def shards(
    hidden, down_weight, adapter_down, adapter_up, output_grad, adapter_per_block, live_rows
):
    dp_count = lax.axis_size("dp")
    dp_index = lax.axis_index("dp")
    row_count = hidden.shape[0]
    local_unit_index = hidden.shape[1]
    model_local = output_grad.shape[1]
    owned_count = adapter_down.shape[0]
    block_count = row_count // BLK
    id_table = adapter_per_block.reshape(dp_count, block_count)
    own_ids = lax.dynamic_slice_in_dim(id_table, dp_index, 1, 0)[0]
    own_owners = own_ids // owned_count
    live_count = lax.dynamic_slice_in_dim(live_rows, dp_index, 1, 0)[0]
    live_mask = (jnp.arange(row_count, dtype=jnp.int32) < live_count)[:, None]
    masked_grad = jnp.where(live_mask, output_grad, jnp.zeros_like(output_grad))
    source_ids = jnp.arange(dp_count, dtype=jnp.int32)
    local_ids = dp_index * owned_count + jnp.arange(owned_count, dtype=jnp.int32)
    wanted = jnp.sum(
        (id_table[:, :, None] == local_ids[None, None, :]).astype(jnp.int32), axis=1
    ).astype(jnp.bfloat16)
    every_down, every_up = (
        lax.all_gather(adapter_down, "dp", axis=0, tiled=True),
        lax.all_gather(adapter_up, "dp", axis=0, tiled=True),
    )
    all_ids = jnp.arange(owned_count * dp_count, dtype=jnp.int32)
    select = (own_ids[:, None] == all_ids[None, :]).astype(jnp.bfloat16)
    block_down = jnp.einsum(
        "bk,kfr->bfr", select, every_down, preferred_element_type=jnp.float32
    ).astype(jnp.bfloat16)
    block_up = jnp.einsum(
        "bk,krd->brd", select, every_up, preferred_element_type=jnp.float32
    ).astype(jnp.bfloat16)
    hid_blocks = hidden.reshape(block_count, BLK, local_unit_index)
    grad_blocks = masked_grad.reshape(block_count, BLK, model_local)
    down_part = jnp.einsum(
        "btf,bfr->btr", hid_blocks, block_down, preferred_element_type=jnp.float32
    )
    up_part = jnp.einsum("btd,brd->btr", grad_blocks, block_up, preferred_element_type=jnp.float32)
    down_sum, up_sum = lax.psum((down_part, up_part), "mp")
    down_act = down_sum.astype(jnp.bfloat16)
    up_act = up_sum.astype(jnp.bfloat16)
    grad_full = lax.all_gather(masked_grad, "mp", axis=1, tiled=True)
    panel = lax.all_gather(down_weight, "dp", axis=1, tiled=True)
    product = jnp.dot(hidden, panel, preferred_element_type=jnp.float32)
    partial_value = product
    back_sum = lax.dot_general(
        grad_full, panel, (((1,), (1,)), ((), ())), preferred_element_type=jnp.float32
    )
    partial_value, backward = (partial_value, back_sum)
    base_out = lax.psum_scatter(partial_value, "mp", scatter_dimension=1, tiled=True)
    branch = jnp.einsum(
        "btr,brd->btd", down_act, block_up, preferred_element_type=jnp.float32
    ).reshape(row_count, model_local)
    layer_out = jnp.where(live_mask, base_out + branch, jnp.float32(0.0)).astype(jnp.bfloat16)
    side_back = jnp.einsum(
        "btr,bfr->btf", up_act, block_down, preferred_element_type=jnp.float32
    ).reshape(row_count, local_unit_index)
    hidden_gradient = (backward + side_back).astype(jnp.bfloat16)
    term_down = jnp.einsum(
        "btf,btr->bfr", hid_blocks, up_act, preferred_element_type=jnp.float32
    ).astype(jnp.bfloat16)
    term_up = jnp.einsum(
        "btr,btd->brd", down_act, grad_blocks, preferred_element_type=jnp.float32
    ).astype(jnp.bfloat16)
    routing = (source_ids[:, None] == own_owners[None, :]).astype(jnp.bfloat16)
    back_down = jnp.einsum(
        "ob,bfr->ofr", routing, term_down, preferred_element_type=jnp.float32
    ).astype(jnp.bfloat16)
    back_up = jnp.einsum(
        "ob,brd->ord", routing, term_up, preferred_element_type=jnp.float32
    ).astype(jnp.bfloat16)
    arrived_down, arrived_up = (
        lax.all_to_all(back_down, "dp", split_axis=0, concat_axis=0, tiled=True),
        lax.all_to_all(back_up, "dp", split_axis=0, concat_axis=0, tiled=True),
    )
    down_grad = jnp.einsum(
        "sa,sfr->afr", wanted, arrived_down, preferred_element_type=jnp.float32
    ).astype(jnp.bfloat16)
    up_grad = jnp.einsum(
        "sa,srd->ard", wanted, arrived_up, preferred_element_type=jnp.float32
    ).astype(jnp.bfloat16)
    return (layer_out, hidden_gradient, down_grad, up_grad)


def solution(mesh):
    return jax.shard_map(
        shards,
        mesh=mesh,
        in_specs=(
            P("dp", "mp"),
            P("mp", "dp"),
            P("dp", "mp", None),
            P("dp", None, "mp"),
            P("dp", "mp"),
            P(),
            P(),
        ),
        out_specs=(P("dp", "mp"), P("dp", "mp"), P("dp", "mp", None), P("dp", None, "mp")),
        check_vma=False,
    )
```

profile of v0, /device:TPU:0, one launch (start us, length us, event | category | flops | bytes accessed | tf_op | source)
XLA Modules:
  0.0 734.7 jit_solution(8418490207072398446)
XLA Ops:
  7.2 0.7 all-gather.5.cloned.1.call-update
  8.0 0.7 all-gather.9.cloned.1.call-update
  8.7 0.7 all-gather.7.cloned.1.call-update
  10.1 0.6 iota_compare_fusion.2
  10.7 1.0 broadcast_select_fusion
  11.8 323.3 %all-gather.5.cloned.1.call-done = bf16[3328,8192]{1,0:T(8,128)(2,1)} async-done(((bf16[3328,2048]{1,0:T(8,128)(2,1)}), bf16[3328,8192]{1,0:T(8,128)(2,1)}) %all-gather.5.cloned.1.call-update) | async-done | bytes 54525968 | tf_op jit(solution)/shard_map/all_gather | solution.py:52
  335.1 29.1 %fusion.35 = f32[384,8192]{1,0:T(8,128)} fusion(bf16[384,3328]{1,0:T(8,128)(2,1)S(1)} %copy-done, bf16[3328,8192]{1,0:T(8,128)(2,1)} %all-gather.5.cloned.1.call-done), kind=kOutput, calls=%fused_computation.53 | convolution fusion | flops 20937965568 | bytes 69664768 | tf_op jit(solution)/shard_map/dot_general | solution.py:53
  364.2 0.6 copy-done.10
  365.0 3.0 fusion.4
  368.0 0.8 copy-done.5
  369.2 41.1 %all-gather.7.cloned.1.call-done = bf16[16,3328,64]{1,2,0:T(8,128)(2,1)} async-done(((bf16[4,3328,64]{1,2,0:T(8,128)(2,1)}), bf16[16,3328,64]{1,2,0:T(8,128)(2,1)}) %all-gather.7.cloned.1.call-update) | async-done | bytes 6815760 | tf_op jit(solution)/shard_map/all_gather | solution.py:31
  410.3 10.5 %fusion = bf16[3,3328,64]{1,0,2:T(4,128)(2,1)S(1)} fusion(bf16[16,3328,64]{1,2,0:T(8,128)(2,1)} %all-gather.7.cloned.1.call-done, s32[3]{0:T(128)S(1)} %get-tuple-element.23), kind=kOutput, calls=%fused_computation | convolution fusion | flops 20447280 | bytes 8093708 | tf_op jit(solution)/shard_map/bk,kfr->bfr/dot_general | solution.py:36
  420.7 1.2 copy-done.3
  421.9 1.0 convolution_bitcast_fusion
  422.9 42.8 %all-reduce.2 = (bf16[3,128,64]{1,2,0:T(8,128)(2,1)}, bf16[3,128,64]{1,2,0:T(8,128)(2,1)}) all-reduce(f32[3,128,64]{1,2,0:T(8,128)S(1)} %convolution_bitcast_fusion, f32[3,128,64]{1,2,0:T(8,128)S(1)} %fusion.18), channel_id=1, replica_groups=mesh['dp'=4,'mp'=8] {'mp'}, use_global_device_ids=true, to_apply=%region_1.2 | all-reduce | flops 49152 | bytes 294912 | tf_op jit(solution)/shard_map/psum | solution.py:48
  465.7 1.1 convolution_convert_fusion.5
  467.3 1.0 copy.56
  468.2 3.7 all-to-all-start.1
  472.4 1.3 convolution_convert_fusion
  473.7 1.4 copy.52
  475.1 5.4 all-to-all-done.1
  480.5 4.4 all-to-all-start
  485.1 1.6 fusion.16
  486.7 3.2 fusion.12
  490.4 1.0 copy.60
  491.4 15.1 %all-to-all-done = bf16[4,3328,64]{1,2,0:T(8,128)(2,1)} async-done(((bf16[4,3328,64]{1,2,0:T(8,128)(2,1)}), bf16[4,3328,64]{1,2,0:T(8,128)(2,1)}, u32[]{:S(2)}, u32[]{:S(2)}) %all-to-all-start) | async-done | bytes 1703968 | tf_op jit(solution)/shard_map/all_to_all | solution.py:82
  506.5 3.7 convolution_convert_fusion.1
  510.2 1.4 copy.59
  511.5 4.0 all-gather.11.cloned.1.call-done
  515.5 32.2 %fusion.2 = bf16[384,3328]{1,0:T(8,128)(2,1)} fusion(f32[384,3328]{1,0:T(8,128)} %bitcast.48, bf16[384,8192]{1,0:T(8,128)(2,1)} %all-gather.11.cloned.1.call-done, bf16[3328,8192]{1,0:T(8,128)(2,1)} %all-gather.5.cloned.1.call-done), kind=kOutput, calls=%fused_computation.3 | convolution fusion | flops 20940521472 | bytes 68485120 | tf_op jit(solution)/shard_map/dot_general | solution.py:55
  547.8 177.5 %reduce-scatter.2.cloned.1.call-done = f32[384,1024]{1,0:T(8,128)} async-done(((f32[384,8192]{1,0:T(8,128)}), f32[384,1024]{1,0:T(8,128)}) %reduce-scatter.2.cloned.1.call-update) | async-done | bytes 1572880 | tf_op jit(solution)/shard_map/reduce_scatter | solution.py:59
  725.3 2.9 fusion.9
  (39 shorter events, 3.1 us)
Async XLA Ops:
  7.2 328.0 %copy-start = (bf16[384,3328]{1,0:T(8,128)(2,1)S(1)}, bf16[384,3328]{1,0:T(8,128)(2,1)}, u32[]{:S(2)}) copy-start(bf16[384,3328]{1,0:T(8,128)(2,1)} %param.7) | copy-start | bytes 7667716
  7.2 328.0 %all-gather.5.cloned.1.call-start = ((), (), s32[]{:S(2)}) async-start(), calls=%async_computation.3 | async-start | bytes 68157440 | tf_op jit(solution)/shard_map/all_gather | solution.py:52
  7.9 1.6 copy-start.11
  7.9 2.8 copy-start.7
  7.9 357.0 %all-gather.9.cloned.1.call-start = ((), (), s32[]{:S(2)}) async-start(), calls=%async_computation.6 | async-start | bytes 2621440 | tf_op jit(solution)/shard_map/all_gather | solution.py:32
  8.7 401.6 %all-gather.7.cloned.1.call-start = ((), (), s32[]{:S(2)}) async-start(), calls=%async_computation.5 | async-start | bytes 8519680 | tf_op jit(solution)/shard_map/all_gather | solution.py:31
  9.4 506.1 %all-gather.11.cloned.1.call-start = ((), (), s32[]{:S(2)}) async-start(), calls=%async_computation.7 | async-start | bytes 7077888 | tf_op jit(solution)/shard_map/all_gather | solution.py:51
  11.8 713.5 %reduce-scatter.2.cloned.1.call-start = ((), (), s32[]{:S(2)}) async-start(), calls=%async_computation.4 | async-start | bytes 14155776 | tf_op jit(solution)/shard_map/reduce_scatter | solution.py:59
  364.2 0.7 copy-start.10
  364.8 3.9 copy-start.2
  367.9 0.8 copy-start.5
  420.7 1.2 copy-start.3
  465.7 6.2 copy-start.8
  468.2 12.3 %all-to-all-start.1 = ((bf16[4,64,1024]{2,1,0:T(8,128)(2,1)}), bf16[4,64,1024]{2,1,0:T(8,128)(2,1)S(1)}, u32[]{:S(2)}, u32[]{:S(2)}) async-start(bf16[4,64,1024]{2,1,0:T(8,128)(2,1)} %copy.56), calls=%async_computation.2 | async-start | bytes 1048576 | tf_op jit(solution)/shard_map/all_to_all | solution.py:83
  475.1 10.0 %copy-start.6 = (bf16[3,64,1024]{2,0,1:T(4,128)(2,1)S(1)}, bf16[3,64,1024]{2,0,1:T(4,128)(2,1)}, u32[]{:S(2)}) copy-start(bf16[3,64,1024]{2,0,1:T(4,128)(2,1)} %copy-done.5) | copy-start | bytes 1179652
  475.1 10.0 %copy-start.9 = (bf16[3,128,64]{1,2,0:T(8,128)(2,1)S(1)}, bf16[3,128,64]{1,2,0:T(8,128)(2,1)}, u32[]{:S(2)}) copy-start(bf16[3,128,64]{1,2,0:T(8,128)(2,1)} %get-tuple-element.20) | copy-start | bytes 147460
  475.1 11.6 %copy-start.4 = (bf16[3,3328,64]{1,0,2:T(4,128)(2,1)S(1)}, bf16[3,3328,64]{1,0,2:T(4,128)(2,1)}, u32[]{:S(2)}) copy-start(bf16[3,3328,64]{1,0,2:T(4,128)(2,1)} %copy-done.3) | copy-start | bytes 3833860
  480.5 26.0 %all-to-all-start = ((bf16[4,3328,64]{1,2,0:T(8,128)(2,1)}), bf16[4,3328,64]{1,2,0:T(8,128)(2,1)}, u32[]{:S(2)}, u32[]{:S(2)}) async-start(bf16[4,3328,64]{1,2,0:T(8,128)(2,1)} %copy.52), calls=%async_computation.1 | async-start | bytes 3407872 | tf_op jit(solution)/shard_map/all_to_all | solution.py:82
  515.5 212.7 %copy-start.1 = (bf16[384,3328]{1,0:T(8,128)(2,1)S(1)}, bf16[384,3328]{1,0:T(8,128)(2,1)}, u32[]{:S(2)}) copy-start(bf16[384,3328]{1,0:T(8,128)(2,1)} %param.7) | copy-start | bytes 7667716
Sparse Core Ops, SparseCore 0:
  9.6 325.4 all-gather.4
  336.7 22.5 all-gather.8
  360.9 49.3 all-gather.6
  412.9 102.5 all-gather.10
  519.0 206.2 reduce-scatter.1
where the time goes:
time: 735 us
  waiting for transfers between devices  569 us (77%)
  matrix products  88.4 us (12%)
  blocking collectives  42.8 us (6%)
  between operations  13.9 us (2%)
  starting transfers between devices  8.28 us (1%)
  local copies, waits for them, and re-layouts  8.02 us (1%)
    all_gather x1, waiting for transfers between devices, shards(): panel = lax.all_gather(down_weight, 'dp', axis=1, tiled=True)  323 us
    reduce_scatter x1, waiting for transfers between devices, shards(): lax.psum_scatter(partial_value, 'mp', scatter_dimension=1, tiled=True)  178 us
    psum x1, blocking collectives, shards(): down_sum, up_sum = lax.psum((down_part, up_part), 'mp')  42.8 us
    all_gather x1, waiting for transfers between devices, shards(): lax.all_gather(adapter_down, 'dp', axis=0, tiled=True)  41.1 us
    dot_general x1, matrix products, shards(): lax.dot_general(grad_full, panel, (((1,), (1,)), ((), ())), preferred_ele...  32.2 us
    dot_general x1, matrix products, shards(): product = jnp.dot(hidden, panel, preferred_element_type=jnp.float32)  29.1 us
    all_to_all x1, waiting for transfers between devices, shards(): lax.all_to_all(back_down, 'dp', split_axis=0, concat_axis=0, tiled=True)  15.1 us
  transfers between devices with their start and end apart: 7, of which 6 were waited for; matrix products, arithmetic and copies ran while one was open for 13% of the time, Pallas kernels for 0%

commit v1 on v0

v1 whole, which is shorter than its diff:
```python
import functools

import jax
import jax.numpy as jnp
from jax import lax
from jax.experimental import pallas as pl
from jax.experimental.pallas import tpu as pltpu
from jax.sharding import PartitionSpec as P

BLK = 128
F32 = jnp.float32
BF16 = jnp.bfloat16
VMEM_LIMIT = 44 * 1024 * 1024


def forward_kernel(ha_ref, hb_ref, w_ref, a_ref, *refs):
    y_ref, p_ref = refs[-2:]
    w = w_ref[...]
    for index, h_ref in enumerate((ha_ref, hb_ref)):
        y_ref[index, 0] = jnp.dot(h_ref[...], w, preferred_element_type=F32)

    @pl.when(pl.program_id(0) == 0)
    def _():
        a = a_ref[...]
        for index, h_ref in enumerate((ha_ref, hb_ref)):
            p_ref[index] = jnp.dot(h_ref[...], a, preferred_element_type=F32)


def forward_pair(pair, ha, hb, weight, factor, total, n_dp, q):
    rows, units = ha.shape
    cols = weight.shape[1]
    width = cols // q
    tile = min(512, width)
    per = width // tile
    rank = factor.shape[1]
    whole = lambda i: (0, 0)
    in_specs = [
        pl.BlockSpec((rows, units), whole),
        pl.BlockSpec((rows, units), whole),
        pl.BlockSpec((units, tile), lambda i: (0, i)),
        pl.BlockSpec((units, rank), whole),
    ]
    operands = [ha, hb, weight, factor]
    aliases = {}
    if total is not None:
        in_specs.append(pl.BlockSpec(memory_space=pl.ANY))
        operands.append(total)
        aliases = {4: 0}
    return pl.pallas_call(
        forward_kernel,
        grid=(cols // tile,),
        in_specs=in_specs,
        out_specs=[
            pl.BlockSpec((2, 1, rows, tile), lambda i: (pair, i // per, 0, i % per)),
            pl.BlockSpec((2, rows, rank), lambda i: (0, 0, 0)),
        ],
        out_shape=[
            jax.ShapeDtypeStruct((n_dp, q, rows, width), F32),
            jax.ShapeDtypeStruct((2, rows, rank), F32),
        ],
        input_output_aliases=aliases,
        cost_estimate=pl.CostEstimate(
            flops=4 * rows * units * (cols + rank),
            bytes_accessed=2 * units * (cols + rank + 2 * rows) + 8 * rows * cols,
            transcendentals=0,
        ),
        compiler_params=pltpu.CompilerParams(vmem_limit_bytes=VMEM_LIMIT),
        name="forward_pair",
    )(*operands)


def backward_kernel(q, g_ref, u_ref, w_ref, a_ref, z_ref):
    width = g_ref.shape[3]
    turned = (((1,), (1,)), ((), ()))
    acc = lax.dot_general(u_ref[...], a_ref[...], turned, preferred_element_type=F32)
    for h in range(q):
        acc += lax.dot_general(
            g_ref[0, h], w_ref[:, h * width : (h + 1) * width], turned, preferred_element_type=F32
        )
    z_ref[...] = acc.astype(z_ref.dtype)


def backward_part(slot, grads, acts, weight, factor, dtype):
    _, q, rows, width = grads.shape
    units, cols = weight.shape
    rank = factor.shape[1]
    tile = 256 if units % 256 == 0 else units
    return pl.pallas_call(
        functools.partial(backward_kernel, q),
        grid=(units // tile,),
        in_specs=[
            pl.BlockSpec((1, q, rows, width), lambda i: (slot, 0, 0, 0)),
            pl.BlockSpec((rows, rank), lambda i: (0, 0)),
            pl.BlockSpec((tile, cols), lambda i: (i, 0)),
            pl.BlockSpec((tile, rank), lambda i: (i, 0)),
        ],
        out_specs=pl.BlockSpec((rows, tile), lambda i: (0, i)),
        out_shape=jax.ShapeDtypeStruct((rows, units), dtype),
        cost_estimate=pl.CostEstimate(
            flops=2 * rows * units * (cols + rank),
            bytes_accessed=2 * (units + rows) * (cols + rank) + 4 * rows * units,
            transcendentals=0,
        ),
        compiler_params=pltpu.CompilerParams(vmem_limit_bytes=VMEM_LIMIT),
        name="backward_part",
    )(grads, acts, weight, factor)


def shards(
    hidden, down_weight, adapter_down, adapter_up, output_grad, adapter_per_block, live_rows
):
    n_dp = lax.axis_size("dp")
    n_mp = lax.axis_size("mp")
    dp = lax.axis_index("dp")
    mp = lax.axis_index("mp")
    q = n_mp // n_dp
    rows, units = hidden.shape
    width = output_grad.shape[1]
    owned, _, rank = adapter_down.shape
    blocks = rows // BLK
    half = n_mp // 2
    top = rows // 2

    def exchange(value, bit, axis="dp"):
        count = n_dp if axis == "dp" else n_mp
        return lax.ppermute(value, axis, [(i, i ^ bit) for i in range(count)])

    def swap_places(value):
        pairs = [
            (j * n_mp + m, (m // q) * n_mp + j * q + m % q)
            for j in range(n_dp)
            for m in range(n_mp)
        ]
        return lax.ppermute(value, ("dp", "mp"), pairs)

    ring = list(range(0, n_mp, 2)) + list(range(n_mp - 1, 0, -2))
    up_ring = [(ring[i], ring[(i + 1) % n_mp]) for i in range(n_mp)]
    down_ring = [(b, a) for a, b in up_ring]
    place = jnp.where(mp % 2 == 0, mp // 2, n_mp - 1 - mp // 2)

    def ring_slot(offset):
        at = (place + offset) % n_mp
        index = jnp.where(at < half, 2 * at, 2 * (n_mp - 1 - at) + 1)
        return (index // q) ^ dp, index % q

    def onward(value):
        return lax.ppermute(value, "mp", up_ring)

    def backward_on(value):
        return lax.ppermute(value, "mp", down_ring)

    id_table = adapter_per_block.reshape(n_dp, blocks)
    ids_of = [lax.dynamic_index_in_dim(id_table, dp ^ r, 0, False) for r in range(n_dp)]
    my_ids = dp * owned + jnp.arange(owned, dtype=jnp.int32)
    mine = [ids[:, None] == my_ids[None, :] for ids in ids_of]
    live_count = lax.dynamic_index_in_dim(live_rows, dp, 0, False)
    live_mask = (jnp.arange(rows, dtype=jnp.int32) < live_count)[:, None]
    masked_grad = jnp.where(live_mask, output_grad, jnp.zeros_like(output_grad))

    swapped = swap_places(masked_grad)

    hid = {0: hidden}
    bit = 2
    while bit < n_dp:
        for r in list(hid):
            hid[r ^ bit] = exchange(hid[r], bit)
        bit *= 2
    for r in list(hid):
        hid[r ^ 1] = exchange(hid[r], 1)

    def for_partner(r):
        local = jnp.sum(
            jnp.where(mine[r], jnp.arange(owned, dtype=jnp.int32)[None, :], 0), dtype=jnp.int32
        )
        return lax.dynamic_index_in_dim(adapter_up, local, 0, False)

    arrived_up = jnp.stack(
        [for_partner(0)] + [exchange(for_partner(r), r) for r in range(1, n_dp)]
    )
    own_owner = ids_of[0] // owned
    block_up = jnp.stack(
        [
            lax.dynamic_index_in_dim(arrived_up, own_owner[b] ^ dp, 0, False)
            for b in range(blocks)
        ]
    )
    grad_blocks = masked_grad.reshape(blocks, BLK, width)

    def sum_over_mp(value):
        step = 1
        while step < n_mp:
            value = value + exchange(value, step, "mp")
            step *= 2
        return value

    up_act = sum_over_mp(
        jnp.einsum("brd,btd->brt", block_up, grad_blocks, preferred_element_type=F32)
    ).astype(BF16)

    def spread(act, r):
        act = jnp.transpose(act, (0, 2, 1))
        picked = jnp.where(mine[r][:, None, :, None], act[:, :, None, :], jnp.zeros((), BF16))
        return picked.reshape(rows, owned * rank)

    acts = [spread(up_act if r == 0 else exchange(up_act, r), r) for r in range(n_dp)]

    grads = jnp.zeros((n_dp, q, rows, width), BF16)

    def put(grads, offset, value, row):
        group, part = ring_slot(offset)
        return lax.dynamic_update_slice(grads, value[None, None], (group, part, row, 0))

    ahead = behind = swapped
    grads = put(grads, 0, swapped, 0)
    for step in range(1, half):
        ahead = onward(ahead)
        behind = backward_on(behind)
        grads = put(grads, -step, ahead, 0)
        grads = put(grads, step, behind, 0)
    grads = put(grads, half, onward(ahead[:top]), 0)
    grads = put(grads, half, backward_on(behind[top:]), top)

    factor = jnp.transpose(adapter_down, (1, 0, 2)).reshape(units, owned * rank)
    total = None
    down_parts = []
    for pair in range(n_dp // 2):
        total, part = forward_pair(
            pair, hid[2 * pair], hid[2 * pair + 1], down_weight, factor, total, n_dp, q
        )
        down_parts += [part[0], part[1]]

    def pick(part, r):
        part = part.reshape(blocks, BLK, owned, rank)
        part = jnp.sum(jnp.where(mine[r][:, None, :, None], part, F32(0.0)), axis=2)
        return jnp.transpose(part, (0, 2, 1))

    down_sum = pick(down_parts[0], 0)
    for r in range(1, n_dp):
        down_sum = down_sum + exchange(pick(down_parts[r], r), r)
    down_act = sum_over_mp(down_sum).astype(BF16)

    def chunk(offset):
        group, part = ring_slot(offset)
        return lax.dynamic_slice(total, (group, part, 0, 0), (1, 1, rows, width))[0, 0]

    far = chunk(half)
    ahead = onward(far[:top].astype(BF16)).astype(F32)
    behind = backward_on(far[top:].astype(BF16)).astype(F32)
    ahead = jnp.pad(ahead, ((0, rows - top), (0, 0)))
    behind = jnp.pad(behind, ((top, 0), (0, 0)))
    for step in range(half - 1, 0, -1):
        ahead = onward((chunk(step) + ahead).astype(BF16)).astype(F32)
        behind = backward_on((chunk(-step) + behind).astype(BF16)).astype(F32)
    base_out = swap_places((chunk(0) + ahead + behind).astype(BF16))

    branch = jnp.einsum(
        "brt,brd->btd", down_act, block_up, preferred_element_type=F32
    ).reshape(rows, width)
    layer_out = jnp.where(live_mask, base_out.astype(F32) + branch, F32(0.0)).astype(BF16)

    parts = {}
    for r in range(n_dp - 1, -1, -1):
        parts[r] = backward_part(
            r, grads, acts[r], down_weight, factor, BF16 if r % 2 else F32
        )
    bit = 1
    while bit < n_dp:
        for r in [r for r in parts if r & bit]:
            arrived = exchange(parts.pop(r).astype(BF16), bit)
            parts[r ^ bit] = parts[r ^ bit] + arrived.astype(F32)
        bit *= 2
    hidden_gradient = parts[0].astype(BF16)

    down_grad = sum(
        lax.dot_general(
            hid[r], acts[r], (((0,), (0,)), ((), ())), preferred_element_type=F32
        )
        for r in range(n_dp)
    )
    down_grad = jnp.transpose(down_grad.reshape(units, owned, rank), (1, 0, 2)).astype(BF16)

    term_up = jnp.einsum(
        "brt,btd->brd", down_act, grad_blocks, preferred_element_type=F32
    ).astype(BF16)

    def term_for(r):
        chosen = (own_owner == (dp ^ r))[:, None, None]
        return jnp.sum(jnp.where(chosen, term_up, jnp.zeros((), BF16)).astype(F32), axis=0).astype(
            BF16
        )

    up_grad = jnp.zeros((owned, rank, width), F32)
    for r in range(n_dp):
        term = term_for(r)
        if r:
            term = exchange(term, r)
        uses = jnp.any(mine[r], axis=0)[:, None, None]
        up_grad = up_grad + jnp.where(uses, term[None].astype(F32), F32(0.0))
    return layer_out, hidden_gradient, down_grad, up_grad.astype(BF16)


def solution(mesh):
    return jax.shard_map(
        shards,
        mesh=mesh,
        in_specs=(
            P("dp", "mp"),
            P("mp", "dp"),
            P("dp", "mp", None),
            P("dp", None, "mp"),
            P("dp", "mp"),
            P(),
            P(),
        ),
        out_specs=(P("dp", "mp"), P("dp", "mp"), P("dp", "mp", None), P("dp", None, "mp")),
        check_vma=False,
    )
```

time: 735 us -> 428 us (0.58)
  the two profiles are of different devices: /device:TPU:0 before, /device:TPU:2 now
where the time goes in v1:
time: 428 us; the launch traced here: 425 us
  waiting for transfers between devices  172 us (40%)
  Pallas kernels  92.6 us (22%)
  starting transfers between devices  61.8 us (14%)
  local copies, waits for them, and re-layouts  37.8 us (9%)
  other arithmetic  29.4 us (7%)
  matrix products  20.6 us (5%)
  between operations  11.3 us (3%)
    ppermute x24, waiting for transfers between devices, exchange(): return lax.ppermute(value, axis, [(i, i ^ bit) for i in range(count)])  75.6 us
    pallas_call x4, Pallas kernels, backward_part(): pl.pallas_call(functools.partial(backward_kernel, q), grid=(units // tile...  57.5 us
    ppermute x8, waiting for transfers between devices, backward_on(): return lax.ppermute(value, 'mp', down_ring)  48 us
    ppermute x24, starting transfers between devices, exchange(): return lax.ppermute(value, axis, [(i, i ^ bit) for i in range(count)])  40.8 us
    ppermute x2, waiting for transfers between devices, swap_places(): return lax.ppermute(value, ('dp', 'mp'), pairs)  35.3 us
    pallas_call x2, Pallas kernels, forward_pair(): pl.pallas_call(forward_kernel, grid=(cols // tile,), in_specs=in_specs, o...  35.1 us
    dot_general x4, matrix products, shards(): lax.dot_general(hid[r], acts[r], (((0,), (0,)), ((), ())), preferred_elem...  17 us
    ppermute x8, waiting for transfers between devices, onward(): return lax.ppermute(value, 'mp', up_ring)  12.8 us
  transfers between devices with their start and end apart: 42, of which 19 were waited for; matrix products, arithmetic and copies ran while one was open for 18% of the time, Pallas kernels for 22%

profile of v1, /device:TPU:2, one launch (start us, length us, event | category | flops | bytes accessed | tf_op | source)
XLA Modules:
  0.0 425.1 jit_solution(7627408894938404057)
XLA Ops:
  25.5 3.3 collective-permute-done.30
  30.5 4.5 %collective-permute-start.21 = (bf16[384,1024]{1,0:T(8,128)(2,1)}, bf16[384,1024]{1,0:T(8,128)(2,1)}, u32[]{:S(2)}, u32[]{:S(2)}) collective-permute-start(bf16[384,1024]{1,0:T(8,128)(2,1)} %broadcast_select_fusion), channel_id=1, source_target_pairs={{0,0},{1,1},{2,8},{3,9},{4,16},{5,17},{6,24},{7,25},{8,2},{9,3},{1... | collective-permute-start | bytes 2359304 | tf_op jit(solution)/shard_map/ppermute | solution.py:134
  34.9 3.5 collective-permute-start
  42.5 12.1 %collective-permute-done.32 = f32[3,64,128]{2,1,0:T(8,128)} collective-permute-done((f32[3,64,128]{2,1,0:T(8,128)S(1)}, f32[3,64,128]{2,1,0:T(8,128)}, u32[]{:S(2)}, u32[]{:S(2)}) %collective-permute-start.32) | collective-permute-done | bytes 98336 | tf_op jit(solution)/shard_map/ppermute | solution.py:126
  55.4 20.0 %collective-permute-start.35 = (bf16[3,64,128]{2,1,0:T(8,128)(2,1)S(1)}, bf16[3,64,128]{2,1,0:T(8,128)(2,1)S(1)}, u32[]{:S(2)}, u32[]{:S(2)}) collective-permute-start(bf16[3,64,128]{2,1,0:T(8,128)(2,1)S(1)} %add_convert_fusion.4), channel_id=1, source_target_pairs={{0,16},{8,24},{16,0},{24,8},{1,17},{9,25},{17,1},{25,9},{2,18},{10... | collective-permute-start | bytes 147464 | tf_op jit(solution)/shard_map/ppermute | solution.py:126
  75.7 35.2 %collective-permute-done.35 = bf16[3,64,128]{2,1,0:T(8,128)(2,1)S(1)} collective-permute-done((bf16[3,64,128]{2,1,0:T(8,128)(2,1)S(1)}, bf16[3,64,128]{2,1,0:T(8,128)(2,1)S(1)}, u32[]{:S(2)}, u32[]{:S(2)}) %collective-permute-start.35) | collective-permute-done | bytes 49184 | tf_op jit(solution)/shard_map/ppermute | solution.py:126
  112.4 4.5 %fusion.31 = f32[256,3328]{1,0:T(8,128)} fusion(bf16[384,256]{0,1:T(8,128)(2,1)S(1)} %bitcast.148, bf16[384,3328]{1,0:T(8,128)(2,1)} %ha_ref.1), kind=kOutput, calls=%fused_computation.108 | convolution fusion | flops 654311424 | bytes 6160384 | tf_op jit(solution)/shard_map/dot_general | solution.py:275
  119.5 9.6 %collective-permute-done.23 = bf16[384,1024]{1,0:T(8,128)(2,1)} collective-permute-done((bf16[384,1024]{1,0:T(8,128)(2,1)}, bf16[384,1024]{1,0:T(8,128)(2,1)}, u32[]{:S(2)}, u32[]{:S(2)}) %collective-permute-start.23) | collective-permute-done | bytes 786464 | tf_op jit(solution)/shard_map/ppermute | solution.py:150
  135.0 4.0 collective-permute-done.24
  139.5 7.8 %collective-permute-done.25 = bf16[384,1024]{1,0:T(8,128)(2,1)} collective-permute-done((bf16[384,1024]{1,0:T(8,128)(2,1)}, bf16[384,1024]{1,0:T(8,128)(2,1)}, u32[]{:S(2)}, u32[]{:S(2)}) %collective-permute-start.25) | collective-permute-done | bytes 786464 | tf_op jit(solution)/shard_map/ppermute | solution.py:150
  150.4 2.5 copy-done
  152.9 17.6 %forward_pair.2 = (f32[4,2,384,1024]{3,2,1,0:T(8,128)}, f32[2,384,256]{2,1,0:T(8,128)S(1)}) custom-call(bf16[384,3328]{1,0:T(8,128)(2,1)} %ha_ref.1, bf16[384,3328]{1,0:T(8,128)(2,1)} %collective-permute-done.2.hb_ref, bf16[3328,2048]{1,0:T(8,128)(2,1)} %w_ref.11, bf16[3328,256]{1,0:T(8,128)(2,1)S(1)} %copy.36.a_ref), custom_call_target="tpu_custom_call" | custom-call | flops 11777605632 | bytes 26738688 | tf_op jit(solution)/shard_map/forward_pair/pallas_call | solution.py:49
  177.3 3.8 convolution_add_fusion.2
  181.1 4.6 %convolution_add_fusion.1 = f32[256,3328]{1,0:T(8,128)} fusion(f32[256,3328]{1,0:T(8,128)S(1)} %convolution_add_fusion.2, bf16[384,256]{0,1:T(8,128)(2,1)S(1)} %bitcast.153, bf16[384,3328]{1,0:T(8,128)(2,1)} %collective-permute-done.ha_ref), kind=kOutput, calls=%fused_computation.1 | convolution fusion | flops 655163392 | bytes 9568256 | tf_op jit(solution)/shard_map/dot_general | solution.py:275
  194.2 4.1 collective-permute-done.28
  201.5 17.5 %forward_pair.3 = (f32[4,2,384,1024]{3,2,1,0:T(8,128)}, f32[2,384,256]{2,1,0:T(8,128)S(1)}) custom-call(bf16[384,3328]{1,0:T(8,128)(2,1)} %collective-permute-done.ha_ref, bf16[384,3328]{1,0:T(8,128)(2,1)} %collective-permute-done.1.hb_ref, bf16[3328,2048]{1,0:T(8,128)(2,1)} %w_ref.11, ...), custom_call_target="tpu_custom_call", output_to_operand_aliasing={{0}: (4, {})} | custom-call | flops 11777605632 | bytes 26738688 | tf_op jit(solution)/shard_map/forward_pair/pallas_call | solution.py:49
  223.1 15.1 %backward_part.7 = bf16[384,3328]{1,0:T(8,128)(2,1)} custom-call(bf16[4,2,384,1024]{3,2,1,0:T(8,128)(2,1)} %bitcast_dynamic-update-slice_fusion.7.g_ref, bf16[384,256]{1,0:T(8,128)(2,1)S(1)} %copy.52.u_ref, bf16[3328,2048]{1,0:T(8,128)(2,1)} %w_ref.11, bf16[3328,256]{1,0:T(8,128)(2,1)S(1)} %copy.36.a_ref), custom_call_target="tpu_custom_call" | custom-call | flops 5888802816 | bytes 22216704 | tf_op jit(solution)/shard_map/backward_part/pallas_call | solution.py:88
  238.2 2.5 fusion.6
  250.4 4.7 %collective-permute-done.13 = f32[3,64,128]{2,0,1:T(4,128)S(1)} collective-permute-done((f32[3,64,128]{2,0,1:T(4,128)S(1)}, f32[3,64,128]{2,0,1:T(4,128)S(1)}, u32[]{:S(2)}, u32[]{:S(2)}) %collective-permute-start.13) | collective-permute-done | bytes 98336 | tf_op jit(solution)/shard_map/ppermute | solution.py:126
  256.6 4.7 %collective-permute-done.4 = bf16[384,1024]{1,0:T(8,128)(2,1)} collective-permute-done((bf16[384,1024]{1,0:T(8,128)(2,1)}, bf16[384,1024]{1,0:T(8,128)(2,1)}, u32[]{:S(2)}, u32[]{:S(2)}) %collective-permute-start.4) | collective-permute-done | bytes 786464 | tf_op jit(solution)/shard_map/ppermute | solution.py:147
  263.3 14.2 %backward_part.6 = f32[384,3328]{1,0:T(8,128)S(1)} custom-call(bf16[4,2,384,1024]{3,2,1,0:T(8,128)(2,1)} %bitcast_dynamic-update-slice_fusion.7.g_ref, bf16[384,256]{1,0:T(8,128)(2,1)S(1)} %copy.49.u_ref, bf16[3328,2048]{1,0:T(8,128)(2,1)} %w_ref.11, bf16[3328,256]{1,0:T(8,128)(2,1)S(1)} %copy.36.a_ref), custom_call_target="tpu_custom_call" | custom-call | flops 5888802816 | bytes 22216704 | tf_op jit(solution)/shard_map/backward_part/pallas_call | solution.py:88
  279.7 14.0 %backward_part.5 = bf16[384,3328]{1,0:T(8,128)(2,1)S(1)} custom-call(bf16[4,2,384,1024]{3,2,1,0:T(8,128)(2,1)} %bitcast_dynamic-update-slice_fusion.7.g_ref, bf16[384,256]{1,0:T(8,128)(2,1)S(1)} %copy.46.u_ref, bf16[3328,2048]{1,0:T(8,128)(2,1)} %w_ref.11, bf16[3328,256]{1,0:T(8,128)(2,1)S(1)} %copy.36.a_ref), custom_call_target="tpu_custom_call" | custom-call | flops 5888802816 | bytes 22216704 | tf_op jit(solution)/shard_map/backward_part/pallas_call | solution.py:88
  296.0 2.4 fusion.8
  301.3 2.3 collective-permute-start.38
  303.6 15.8 %collective-permute-done.8 = bf16[384,1024]{1,0:T(8,128)(2,1)S(1)} collective-permute-done((bf16[384,1024]{1,0:T(8,128)(2,1)S(1)}, bf16[384,1024]{1,0:T(8,128)(2,1)S(1)}, u32[]{:S(2)}, u32[]{:S(2)}) %collective-permute-start.8) | collective-permute-done | bytes 786464 | tf_op jit(solution)/shard_map/ppermute | solution.py:150
  321.2 14.2 %backward_part.4 = f32[384,3328]{1,0:T(8,128)S(1)} custom-call(bf16[4,2,384,1024]{3,2,1,0:T(8,128)(2,1)} %bitcast_dynamic-update-slice_fusion.7.g_ref, bf16[384,256]{1,0:T(8,128)(2,1)S(1)} %copy.43.u_ref, bf16[3328,2048]{1,0:T(8,128)(2,1)} %w_ref.11, bf16[3328,256]{1,0:T(8,128)(2,1)S(1)} %copy.36.a_ref), custom_call_target="tpu_custom_call" | custom-call | flops 5888802816 | bytes 22216704 | tf_op jit(solution)/shard_map/backward_part/pallas_call | solution.py:88
  337.2 2.3 collective-permute-start.41
  343.6 18.7 %collective-permute-done.41 = bf16[64,1024]{1,0:T(8,128)(2,1)S(1)} collective-permute-done((bf16[64,1024]{1,0:T(8,128)(2,1)S(1)}, bf16[64,1024]{1,0:T(8,128)(2,1)S(1)}, u32[]{:S(2)}, u32[]{:S(2)}) %collective-permute-start.41) | collective-permute-done | bytes 131104 | tf_op jit(solution)/shard_map/ppermute | solution.py:126
  362.3 4.0 fusion
  369.0 13.0 %collective-permute-done.10 = bf16[384,1024]{1,0:T(8,128)(2,1)S(1)} collective-permute-done((bf16[384,1024]{1,0:T(8,128)(2,1)S(1)}, bf16[384,1024]{1,0:T(8,128)(2,1)S(1)}, u32[]{:S(2)}, u32[]{:S(2)}) %collective-permute-start.10) | collective-permute-done | bytes 786464 | tf_op jit(solution)/shard_map/ppermute | solution.py:150
  383.8 2.6 collective-permute-start.11
  388.7 35.3 %collective-permute-done.11 = bf16[384,1024]{1,0:T(8,128)(2,1)S(1)} collective-permute-done((bf16[384,1024]{1,0:T(8,128)(2,1)S(1)}, bf16[384,1024]{1,0:T(8,128)(2,1)S(1)}, u32[]{:S(2)}, u32[]{:S(2)}) %collective-permute-start.11) | collective-permute-done | bytes 786464 | tf_op jit(solution)/shard_map/ppermute | solution.py:134
  (188 shorter events, 93.6 us)
Async XLA Ops:
  30.5 45.2 %collective-permute-start.21 = (bf16[384,1024]{1,0:T(8,128)(2,1)}, bf16[384,1024]{1,0:T(8,128)(2,1)}, u32[]{:S(2)}, u32[]{:S(2)}) collective-permute-start(bf16[384,1024]{1,0:T(8,128)(2,1)} %broadcast_select_fusion), channel_id=1, source_target_pairs={{0,0},{1,1},{2,8},{3,9},{4,16},{5,17},{6,24},{7,25},{8,2},{9,3},{1... | collective-permute-start | bytes 2359304 | tf_op jit(solution)/shard_map/ppermute | solution.py:134
  34.9 115.4 %collective-permute-start = (bf16[384,3328]{1,0:T(8,128)(2,1)}, bf16[384,3328]{1,0:T(8,128)(2,1)}, u32[]{:S(2)}, u32[]{:S(2)}) collective-permute-start(bf16[384,3328]{1,0:T(8,128)(2,1)} %ha_ref.1), channel_id=1, source_target_pairs={{0,16},{8,24},{16,0},{24,8},{1,17},{9,25},{17,1},{25,9},{2,18},{10... | collective-permute-start | bytes 7667720 | tf_op jit(solution)/shard_map/ppermute | solution.py:126
  38.4 114.5 %collective-permute-start.2 = (bf16[384,3328]{1,0:T(8,128)(2,1)}, bf16[384,3328]{1,0:T(8,128)(2,1)}, u32[]{:S(2)}, u32[]{:S(2)}) collective-permute-start(bf16[384,3328]{1,0:T(8,128)(2,1)} %ha_ref.1), channel_id=1, source_target_pairs={{0,8},{8,0},{16,24},{24,16},{1,9},{9,1},{17,25},{25,17},{2,10},{10... | collective-permute-start | bytes 7667720 | tf_op jit(solution)/shard_map/ppermute | solution.py:126
  38.4 16.1 %collective-permute-start.32 = (f32[3,64,128]{2,1,0:T(8,128)S(1)}, f32[3,64,128]{2,1,0:T(8,128)}, u32[]{:S(2)}, u32[]{:S(2)}) collective-permute-start(f32[3,64,128]{2,1,0:T(8,128)S(1)} %add.433), channel_id=1, source_target_pairs={{0,4},{1,5},{2,6},{3,7},{4,0},{5,1},{6,2},{7,3},{8,12},{9,13},{10,... | collective-permute-start | bytes 294920 | tf_op jit(solution)/shard_map/ppermute | solution.py:126
  55.4 55.5 %collective-permute-start.35 = (bf16[3,64,128]{2,1,0:T(8,128)(2,1)S(1)}, bf16[3,64,128]{2,1,0:T(8,128)(2,1)S(1)}, u32[]{:S(2)}, u32[]{:S(2)}) collective-permute-start(bf16[3,64,128]{2,1,0:T(8,128)(2,1)S(1)} %add_convert_fusion.4), channel_id=1, source_target_pairs={{0,16},{8,24},{16,0},{24,8},{1,17},{9,25},{17,1},{25,9},{2,18},{10... | collective-permute-start | bytes 147464 | tf_op jit(solution)/shard_map/ppermute | solution.py:126
  75.4 41.8 %collective-permute-start.36 = (bf16[3,64,128]{2,1,0:T(8,128)(2,1)S(1)}, bf16[3,64,128]{2,1,0:T(8,128)(2,1)S(1)}, u32[]{:S(2)}, u32[]{:S(2)}) collective-permute-start(bf16[3,64,128]{2,1,0:T(8,128)(2,1)S(1)} %add_convert_fusion.4), channel_id=1, source_target_pairs={{0,24},{8,16},{16,8},{24,0},{1,25},{9,17},{17,9},{25,1},{2,26},{10... | collective-permute-start | bytes 147464 | tf_op jit(solution)/shard_map/ppermute | solution.py:126
  75.6 43.2 %collective-permute-start.22 = (bf16[384,1024]{1,0:T(8,128)(2,1)}, bf16[384,1024]{1,0:T(8,128)(2,1)}, u32[]{:S(2)}, u32[]{:S(2)}) collective-permute-start(bf16[384,1024]{1,0:T(8,128)(2,1)} %collective-permute-done.21), channel_id=1, source_target_pairs={{0,2},{2,4},{4,6},{6,7},{7,5},{5,3},{3,1},{1,0},{8,10},{10,12},{12... | collective-permute-start | bytes 2359304 | tf_op jit(solution)/shard_map/ppermute | solution.py:147
  110.9 18.2 %collective-permute-start.23 = (bf16[384,1024]{1,0:T(8,128)(2,1)}, bf16[384,1024]{1,0:T(8,128)(2,1)}, u32[]{:S(2)}, u32[]{:S(2)}) collective-permute-start(bf16[384,1024]{1,0:T(8,128)(2,1)} %collective-permute-done.21), channel_id=1, source_target_pairs={{2,0},{4,2},{6,4},{7,6},{5,7},{3,5},{1,3},{0,1},{10,8},{12,10},{14... | collective-permute-start | bytes 2359304 | tf_op jit(solution)/shard_map/ppermute | solution.py:150
  118.9 20.1 %collective-permute-start.24 = (bf16[384,1024]{1,0:T(8,128)(2,1)}, bf16[384,1024]{1,0:T(8,128)(2,1)}, u32[]{:S(2)}, u32[]{:S(2)}) collective-permute-start(bf16[384,1024]{1,0:T(8,128)(2,1)} %collective-permute-done.22), channel_id=1, source_target_pairs={{0,2},{2,4},{4,6},{6,7},{7,5},{5,3},{3,1},{1,0},{8,10},{10,12},{12... | collective-permute-start | bytes 2359304 | tf_op jit(solution)/shard_map/ppermute | solution.py:147
  129.1 18.2 %collective-permute-start.25 = (bf16[384,1024]{1,0:T(8,128)(2,1)}, bf16[384,1024]{1,0:T(8,128)(2,1)}, u32[]{:S(2)}, u32[]{:S(2)}) collective-permute-start(bf16[384,1024]{1,0:T(8,128)(2,1)} %collective-permute-done.23), channel_id=1, source_target_pairs={{2,0},{4,2},{6,4},{7,6},{5,7},{3,5},{1,3},{0,1},{10,8},{12,10},{14... | collective-permute-start | bytes 2359304 | tf_op jit(solution)/shard_map/ppermute | solution.py:150
  139.0 46.7 %collective-permute-start.26 = (bf16[384,1024]{1,0:T(8,128)(2,1)}, bf16[384,1024]{1,0:T(8,128)(2,1)}, u32[]{:S(2)}, u32[]{:S(2)}) collective-permute-start(bf16[384,1024]{1,0:T(8,128)(2,1)} %collective-permute-done.24), channel_id=1, source_target_pairs={{0,2},{2,4},{4,6},{6,7},{7,5},{5,3},{3,1},{1,0},{8,10},{10,12},{12... | collective-permute-start | bytes 2359304 | tf_op jit(solution)/shard_map/ppermute | solution.py:147
  147.3 40.9 %collective-permute-start.27 = (bf16[384,1024]{1,0:T(8,128)(2,1)}, bf16[384,1024]{1,0:T(8,128)(2,1)}, u32[]{:S(2)}, u32[]{:S(2)}) collective-permute-start(bf16[384,1024]{1,0:T(8,128)(2,1)} %collective-permute-done.25), channel_id=1, source_target_pairs={{2,0},{4,2},{6,4},{7,6},{5,7},{3,5},{1,3},{0,1},{10,8},{12,10},{14... | collective-permute-start | bytes 2359304 | tf_op jit(solution)/shard_map/ppermute | solution.py:150
  150.3 51.1 %collective-permute-start.1 = (bf16[384,3328]{1,0:T(8,128)(2,1)}, bf16[384,3328]{1,0:T(8,128)(2,1)}, u32[]{:S(2)}, u32[]{:S(2)}) collective-permute-start(bf16[384,3328]{1,0:T(8,128)(2,1)} %collective-permute-done.ha_ref), channel_id=1, source_target_pairs={{0,8},{8,0},{16,24},{24,16},{1,9},{9,1},{17,25},{25,17},{2,10},{10... | collective-permute-start | bytes 7667720 | tf_op jit(solution)/shard_map/ppermute | solution.py:126
  174.2 75.8 %collective-permute-start.12 = (f32[3,64,128]{2,0,1:T(4,128)}, f32[3,64,128]{2,0,1:T(4,128)}, u32[]{:S(2)}, u32[]{:S(2)}) collective-permute-start(f32[3,64,128]{2,0,1:T(4,128)} %bitcast.16), channel_id=1, source_target_pairs={{0,8},{8,0},{16,24},{24,16},{1,9},{9,1},{17,25},{25,17},{2,10},{10... | collective-permute-start | bytes 294920 | tf_op jit(solution)/shard_map/ppermute | solution.py:126
  186.7 11.6 %collective-permute-start.28 = (bf16[192,1024]{1,0:T(8,128)(2,1)S(1)}, bf16[192,1024]{1,0:T(8,128)(2,1)S(1)}, u32[]{:S(2)}, u32[]{:S(2)}) collective-permute-start(bf16[192,1024]{1,0:T(8,128)(2,1)S(1)} %slice.50), channel_id=1, source_target_pairs={{0,2},{2,4},{4,6},{6,7},{7,5},{5,3},{3,1},{1,0},{8,10},{10,12},{12... | collective-permute-start | bytes 1179656 | tf_op jit(solution)/shard_map/ppermute | solution.py:147
  221.3 16.8 %collective-permute-start.3 = (bf16[192,1024]{1,0:T(8,128)(2,1)S(1)}, bf16[192,1024]{1,0:T(8,128)(2,1)S(1)}, u32[]{:S(2)}, u32[]{:S(2)}) collective-permute-start(bf16[192,1024]{1,0:T(8,128)(2,1)S(1)} %get-tuple-element.29), channel_id=1, source_target_pairs={{0,2},{2,4},{4,6},{6,7},{7,5},{5,3},{3,1},{1,0},{8,10},{10,12},{12... | collective-permute-start | bytes 1179656 | tf_op jit(solution)/shard_map/ppermute | solution.py:147
  238.1 61.0 %collective-permute-start.37 = (bf16[384,3328]{1,0:T(8,128)(2,1)}, bf16[384,3328]{1,0:T(8,128)(2,1)}, u32[]{:S(2)}, u32[]{:S(2)}) collective-permute-start(bf16[384,3328]{1,0:T(8,128)(2,1)} %backward_part.7), channel_id=1, source_target_pairs={{0,8},{8,0},{16,24},{24,16},{1,9},{9,1},{17,25},{25,17},{2,10},{10... | collective-permute-start | bytes 7667720 | tf_op jit(solution)/shard_map/ppermute | solution.py:126
  240.6 20.7 %collective-permute-start.4 = (bf16[384,1024]{1,0:T(8,128)(2,1)}, bf16[384,1024]{1,0:T(8,128)(2,1)}, u32[]{:S(2)}, u32[]{:S(2)}) collective-permute-start(bf16[384,1024]{1,0:T(8,128)(2,1)} %fusion.6), channel_id=1, source_target_pairs={{0,2},{2,4},{4,6},{6,7},{7,5},{5,3},{3,1},{1,0},{8,10},{10,12},{12... | collective-permute-start | bytes 2359304 | tf_op jit(solution)/shard_map/ppermute | solution.py:147
  256.2 23.3 %collective-permute-start.15 = (f32[3,64,128]{2,0,1:T(4,128)S(1)}, f32[3,64,128]{2,0,1:T(4,128)S(1)}, u32[]{:S(2)}, u32[]{:S(2)}) collective-permute-start(f32[3,64,128]{2,0,1:T(4,128)S(1)} %fusion.14), channel_id=1, source_target_pairs={{0,1},{1,0},{2,3},{3,2},{4,5},{5,4},{6,7},{7,6},{8,9},{9,8},{10,11... | collective-permute-start | bytes 294920 | tf_op jit(solution)/shard_map/ppermute | solution.py:126
  263.2 32.8 %collective-permute-start.5 = (bf16[384,1024]{1,0:T(8,128)(2,1)S(1)}, bf16[384,1024]{1,0:T(8,128)(2,1)S(1)}, u32[]{:S(2)}, u32[]{:S(2)}) collective-permute-start(bf16[384,1024]{1,0:T(8,128)(2,1)S(1)} %fusion.7), channel_id=1, source_target_pairs={{0,2},{2,4},{4,6},{6,7},{7,5},{5,3},{3,1},{1,0},{8,10},{10,12},{12... | collective-permute-start | bytes 2359304 | tf_op jit(solution)/shard_map/ppermute | solution.py:147
  277.5 18.5 %collective-permute-start.7 = (bf16[192,1024]{1,0:T(8,128)(2,1)S(1)}, bf16[192,1024]{1,0:T(8,128)(2,1)S(1)}, u32[]{:S(2)}, u32[]{:S(2)}) collective-permute-start(bf16[192,1024]{1,0:T(8,128)(2,1)S(1)} %copy-done.11), channel_id=1, source_target_pairs={{2,0},{4,2},{6,4},{7,6},{5,7},{3,5},{1,3},{0,1},{10,8},{12,10},{14... | collective-permute-start | bytes 1179656 | tf_op jit(solution)/shard_map/ppermute | solution.py:150
  279.5 14.2 %collective-permute-start.16 = (f32[3,64,128]{2,0,1:T(4,128)S(1)}, f32[3,64,128]{2,0,1:T(4,128)S(1)}, u32[]{:S(2)}, u32[]{:S(2)}) collective-permute-start(f32[3,64,128]{2,0,1:T(4,128)S(1)} %add.421), channel_id=1, source_target_pairs={{0,2},{1,3},{2,0},{3,1},{4,6},{5,7},{6,4},{7,5},{8,10},{9,11},{10,... | collective-permute-start | bytes 294920 | tf_op jit(solution)/shard_map/ppermute | solution.py:126
  293.7 92.7 %collective-permute-start.34 = (bf16[384,3328]{1,0:T(8,128)(2,1)S(1)}, bf16[384,3328]{1,0:T(8,128)(2,1)S(1)}, u32[]{:S(2)}, u32[]{:S(2)}) collective-permute-start(bf16[384,3328]{1,0:T(8,128)(2,1)S(1)} %backward_part.5), channel_id=1, source_target_pairs={{0,8},{8,0},{16,24},{24,16},{1,9},{9,1},{17,25},{25,17},{2,10},{10... | collective-permute-start | bytes 7667720 | tf_op jit(solution)/shard_map/ppermute | solution.py:126
  293.8 41.5 %collective-permute-start.17 = (f32[3,64,128]{2,0,1:T(4,128)S(1)}, f32[3,64,128]{2,0,1:T(4,128)S(1)}, u32[]{:S(2)}, u32[]{:S(2)}) collective-permute-start(f32[3,64,128]{2,0,1:T(4,128)S(1)} %add.422), channel_id=1, source_target_pairs={{0,4},{1,5},{2,6},{3,7},{4,0},{5,1},{6,2},{7,3},{8,12},{9,13},{10,... | collective-permute-start | bytes 294920 | tf_op jit(solution)/shard_map/ppermute | solution.py:126
  298.4 21.0 %collective-permute-start.8 = (bf16[384,1024]{1,0:T(8,128)(2,1)S(1)}, bf16[384,1024]{1,0:T(8,128)(2,1)S(1)}, u32[]{:S(2)}, u32[]{:S(2)}) collective-permute-start(bf16[384,1024]{1,0:T(8,128)(2,1)S(1)} %get-tuple-element.28), channel_id=1, source_target_pairs={{2,0},{4,2},{6,4},{7,6},{5,7},{3,5},{1,3},{0,1},{10,8},{12,10},{14... | collective-permute-start | bytes 2359304 | tf_op jit(solution)/shard_map/ppermute | solution.py:150
  301.3 85.1 %collective-permute-start.38 = (bf16[384,3328]{1,0:T(8,128)(2,1)S(1)}, bf16[384,3328]{1,0:T(8,128)(2,1)S(1)}, u32[]{:S(2)}, u32[]{:S(2)}) collective-permute-start(bf16[384,3328]{1,0:T(8,128)(2,1)S(1)} %add_convert_fusion.1), channel_id=1, source_target_pairs={{0,16},{8,24},{16,0},{24,8},{1,17},{9,25},{17,1},{25,9},{2,18},{10... | collective-permute-start | bytes 7667720 | tf_op jit(solution)/shard_map/ppermute | solution.py:126
  321.1 19.0 %collective-permute-start.9 = (bf16[384,1024]{1,0:T(8,128)(2,1)S(1)}, bf16[384,1024]{1,0:T(8,128)(2,1)S(1)}, u32[]{:S(2)}, u32[]{:S(2)}) collective-permute-start(bf16[384,1024]{1,0:T(8,128)(2,1)S(1)} %fusion.4), channel_id=1, source_target_pairs={{2,0},{4,2},{6,4},{7,6},{5,7},{3,5},{1,3},{0,1},{10,8},{12,10},{14... | collective-permute-start | bytes 2359304 | tf_op jit(solution)/shard_map/ppermute | solution.py:150
  337.2 25.1 %collective-permute-start.41 = (bf16[64,1024]{1,0:T(8,128)(2,1)S(1)}, bf16[64,1024]{1,0:T(8,128)(2,1)S(1)}, u32[]{:S(2)}, u32[]{:S(2)}) collective-permute-start(bf16[64,1024]{1,0:T(8,128)(2,1)S(1)} %get-tuple-element.13), channel_id=1, source_target_pairs={{0,24},{8,16},{16,8},{24,0},{1,25},{9,17},{17,9},{25,1},{2,26},{10... | collective-permute-start | bytes 393224 | tf_op jit(solution)/shard_map/ppermute | solution.py:126
  339.4 26.9 %collective-permute-start.40 = (bf16[64,1024]{1,0:T(8,128)(2,1)S(1)}, bf16[64,1024]{1,0:T(8,128)(2,1)S(1)}, u32[]{:S(2)}, u32[]{:S(2)}) collective-permute-start(bf16[64,1024]{1,0:T(8,128)(2,1)S(1)} %get-tuple-element.14), channel_id=1, source_target_pairs={{0,16},{8,24},{16,0},{24,8},{1,17},{9,25},{17,1},{25,9},{2,18},{10... | collective-permute-start | bytes 393224 | tf_op jit(solution)/shard_map/ppermute | solution.py:126
  340.1 28.9 %collective-permute-start.6 = (bf16[384,1024]{1,0:T(8,128)(2,1)S(1)}, bf16[384,1024]{1,0:T(8,128)(2,1)S(1)}, u32[]{:S(2)}, u32[]{:S(2)}) collective-permute-start(bf16[384,1024]{1,0:T(8,128)(2,1)S(1)} %get-tuple-element.27), channel_id=1, source_target_pairs={{0,2},{2,4},{4,6},{6,7},{7,5},{5,3},{3,1},{1,0},{8,10},{10,12},{12... | collective-permute-start | bytes 2359304 | tf_op jit(solution)/shard_map/ppermute | solution.py:147
  362.3 19.7 %collective-permute-start.10 = (bf16[384,1024]{1,0:T(8,128)(2,1)S(1)}, bf16[384,1024]{1,0:T(8,128)(2,1)S(1)}, u32[]{:S(2)}, u32[]{:S(2)}) collective-permute-start(bf16[384,1024]{1,0:T(8,128)(2,1)S(1)} %fusion.5), channel_id=1, source_target_pairs={{2,0},{4,2},{6,4},{7,6},{5,7},{3,5},{1,3},{0,1},{10,8},{12,10},{14... | collective-permute-start | bytes 2359304 | tf_op jit(solution)/shard_map/ppermute | solution.py:150
  383.8 40.2 %collective-permute-start.11 = (bf16[384,1024]{1,0:T(8,128)(2,1)S(1)}, bf16[384,1024]{1,0:T(8,128)(2,1)S(1)}, u32[]{:S(2)}, u32[]{:S(2)}) collective-permute-start(bf16[384,1024]{1,0:T(8,128)(2,1)S(1)} %fusion.10), channel_id=1, source_target_pairs={{0,0},{1,1},{2,8},{3,9},{4,16},{5,17},{6,24},{7,25},{8,2},{9,3},{1... | collective-permute-start | bytes 2359304 | tf_op jit(solution)/shard_map/ppermute | solution.py:134
  (31 other events, 343.1 us)

commit v2 on v0

v2 whole, which is shorter than its diff:
```python
import functools

import jax
import jax.numpy as jnp
from jax import lax
from jax.experimental import pallas as pl
from jax.experimental.pallas import tpu as pltpu
from jax.sharding import PartitionSpec as P

BLK = 128
F32 = jnp.float32
BF16 = jnp.bfloat16
VMEM_LIMIT = 44 * 1024 * 1024


TURNED = (((1,), (1,)), ((), ()))
FIRSTS = (((0,), (0,)), ((), ()))


def params():
    return pltpu.CompilerParams(vmem_limit_bytes=VMEM_LIMIT)


def whole(shape):
    return pl.BlockSpec(shape, lambda *_: (0,) * len(shape))


def call(kernel, name, scalars, operands, out_shapes, scratch_shapes=()):
    return pl.pallas_call(
        kernel,
        grid_spec=pltpu.PrefetchScalarGridSpec(
            num_scalar_prefetch=len(scalars),
            grid=(1,),
            in_specs=[whole(x.shape) for x in operands],
            out_specs=[whole(x.shape) for x in out_shapes],
            scratch_shapes=list(scratch_shapes),
        ),
        out_shape=list(out_shapes),
        compiler_params=params(),
        name=name,
    )(*scalars, *operands)


def mask_kernel(at_ref, live_ref, grad_ref, out_ref):
    row = lax.broadcasted_iota(jnp.int32, grad_ref.shape, 0)
    grad = grad_ref[...]
    out_ref[...] = jnp.where(row < live_ref[at_ref[0]], grad, jnp.zeros_like(grad))


def select_kernel(n_dp, owned, rank, at_ref, id_ref, up_ref, *out_refs):
    mask_ref = out_refs[-1]
    dp = at_ref[0]
    blocks = mask_ref.shape[1]
    column = lax.broadcasted_iota(jnp.int32, (BLK, owned * rank), 1)
    for r in range(n_dp):
        chosen = jnp.int32(0)
        for b in range(blocks):
            local = id_ref[(dp ^ r) * blocks + b] - dp * owned
            chosen = jnp.where((local >= 0) & (local < owned), local, chosen)
            hit = (column >= local * rank) & (column < (local + 1) * rank)
            mask_ref[r, b] = jnp.where(hit, 1.0, 0.0).astype(BF16)
        out_refs[r][...] = up_ref[chosen]


def up_kernel(n_dp, owned, at_ref, id_ref, grad_ref, *refs):
    part_ref, block_ref = refs[n_dp:]
    dp = at_ref[0]
    blocks, rank, _ = block_ref.shape
    for b in range(blocks):
        source = (id_ref[dp * blocks + b] // owned) ^ dp
        for r in range(n_dp):

            @pl.when(source == r)
            def _():
                block_ref[b] = refs[r][...]

    for b in range(blocks):
        part_ref[b * rank : (b + 1) * rank, :] = lax.dot_general(
            block_ref[b],
            grad_ref[b * BLK : (b + 1) * BLK, :],
            TURNED,
            preferred_element_type=F32,
        )


def term_kernel(
    n_dp, owned, at_ref, id_ref, live_ref, down_ref, grad_ref, block_ref, branch_ref, *out_refs
):
    dp = at_ref[0]
    blocks, rank, width = block_ref.shape
    down_act = down_ref[...].astype(BF16)
    row = lax.broadcasted_iota(jnp.int32, (BLK, width), 0)
    for r in range(n_dp):
        out_refs[r][...] = jnp.zeros(out_refs[r].shape, BF16)
    for b in range(blocks):
        rows = slice(b * BLK, (b + 1) * BLK)
        act = down_act[b * rank : (b + 1) * rank]
        branch = lax.dot_general(act, block_ref[b], FIRSTS, preferred_element_type=F32)
        branch_ref[rows, :] = jnp.where(row + b * BLK < live_ref[dp], branch, 0.0)
        term = jnp.dot(act, grad_ref[rows, :], preferred_element_type=F32).astype(BF16)
        owner = (id_ref[dp * blocks + b] // owned) ^ dp
        for r in range(n_dp):

            @pl.when(owner == r)
            def _():
                out_refs[r][...] = term


def up_grad_kernel(n_dp, blocks, at_ref, id_ref, *refs):
    out_ref = refs[n_dp]
    dp = at_ref[0]
    owned = out_ref.shape[0]
    for a in range(owned):
        total = jnp.zeros(out_ref.shape[1:], F32)
        for r in range(n_dp):
            uses = jnp.int32(0)
            for b in range(blocks):
                uses += (id_ref[(dp ^ r) * blocks + b] == dp * owned + a).astype(jnp.int32)
            total += jnp.where(uses > 0, refs[r][...].astype(F32), 0.0)
        out_ref[a] = total.astype(BF16)


def ring_slot(offset, at, n_dp, n_mp):
    dp, mp = at[0], at[1]
    place = jnp.where(mp % 2 == 0, mp // 2, n_mp - 1 - mp // 2)
    there = (place + offset + n_mp) % n_mp
    index = jnp.where(there < n_mp // 2, 2 * there, 2 * (n_mp - 1 - there) + 1)
    q = n_mp // n_dp
    return (index // q) ^ dp, index % q


def add_kernel(at_ref, a_ref, b_ref, ahead_ref, behind_ref, a_out, b_out):
    a_out[...] = (a_ref[0, 0].astype(F32) + ahead_ref[...].astype(F32)).astype(BF16)
    b_out[...] = (b_ref[0, 0].astype(F32) + behind_ref[...].astype(F32)).astype(BF16)


def half_add_kernel(at_ref, a_ref, b_ref, ahead_ref, behind_ref, a_out, b_out):
    first = pl.program_id(0) == 0

    @pl.when(first)
    def _():
        a_out[...] = (a_ref[0, 0].astype(F32) + ahead_ref[...].astype(F32)).astype(BF16)
        b_out[...] = b_ref[0, 0]

    @pl.when(jnp.logical_not(first))
    def _():
        a_out[...] = a_ref[0, 0]
        b_out[...] = (b_ref[0, 0].astype(F32) + behind_ref[...].astype(F32)).astype(BF16)


def ring_add(step, at, total, ahead, behind, n_mp, halves):
    n_dp, _, rows, width = total.shape
    top = rows // 2

    def slot(offset):
        def index(i, at_ref):
            group, part = ring_slot(offset, at_ref, n_dp, n_mp)
            return group, part, i, 0

        return pl.BlockSpec((1, 1, top, width), index)

    arrived = pl.BlockSpec((top, width), lambda i, at_ref: (0 if halves else i, 0))
    sent = pl.BlockSpec((top, width), lambda i, at_ref: (i, 0))
    return pl.pallas_call(
        half_add_kernel if halves else add_kernel,
        grid_spec=pltpu.PrefetchScalarGridSpec(
            num_scalar_prefetch=1,
            grid=(2,),
            in_specs=[slot(step), slot(-step), arrived, arrived],
            out_specs=[sent, sent],
        ),
        out_shape=[jax.ShapeDtypeStruct((rows, width), BF16)] * 2,
        compiler_params=params(),
        name="ring_add",
    )(at, total, total, ahead, behind)


def opposite_kernel(at_ref, total_ref, first_ref, second_ref):
    top = first_ref.shape[0]
    first_ref[...] = total_ref[0, 0, :top]
    second_ref[...] = total_ref[0, 0, top:]


def opposite(at, total, n_mp):
    n_dp, _, rows, width = total.shape

    def index(i, at_ref):
        group, part = ring_slot(n_mp // 2, at_ref, n_dp, n_mp)
        return group, part, 0, 0

    out = pl.BlockSpec((rows // 2, width), lambda i, at_ref: (0, 0))
    return pl.pallas_call(
        opposite_kernel,
        grid_spec=pltpu.PrefetchScalarGridSpec(
            num_scalar_prefetch=1,
            grid=(1,),
            in_specs=[pl.BlockSpec((1, 1, rows, width), index)],
            out_specs=[out, out],
        ),
        out_shape=[jax.ShapeDtypeStruct((rows // 2, width), BF16)] * 2,
        compiler_params=params(),
        name="opposite",
    )(at, total)


def last_add_kernel(n_dp, n_mp, at_ref, live_ref, own_ref, ahead_ref, behind_ref, out_ref):
    total = own_ref[0, 0].astype(F32) + ahead_ref[...].astype(F32) + behind_ref[...].astype(F32)
    row = lax.broadcasted_iota(jnp.int32, total.shape, 0) + pl.program_id(0) * total.shape[0]
    live = live_ref[at_ref[1] // (n_mp // n_dp)]
    out_ref[...] = jnp.where(row < live, total, 0.0).astype(BF16)


def last_add(at, live_rows, total, ahead, behind, n_mp):
    n_dp, _, rows, width = total.shape

    def index(i, at_ref, live_ref):
        group, part = ring_slot(0, at_ref, n_dp, n_mp)
        return group, part, i, 0

    half = pl.BlockSpec((rows // 2, width), lambda i, at_ref, live_ref: (i, 0))
    return pl.pallas_call(
        functools.partial(last_add_kernel, n_dp, n_mp),
        grid_spec=pltpu.PrefetchScalarGridSpec(
            num_scalar_prefetch=2,
            grid=(2,),
            in_specs=[pl.BlockSpec((1, 1, rows // 2, width), index), half, half],
            out_specs=half,
        ),
        out_shape=jax.ShapeDtypeStruct((rows, width), BF16),
        compiler_params=params(),
        name="last_add",
    )(at, live_rows, total, ahead, behind)


def combine_kernel(own_ref, *refs):
    total = own_ref[...]
    for ref in refs[:-2]:
        total += ref[...].astype(F32)
    refs[-1][...] = total.astype(BF16)


def combine(start, own, near, arrived, out):
    rows, units = own.shape
    tile = 32
    first = start // tile
    placed = pl.BlockSpec((tile, units), lambda i: (i + first, 0))
    piece = pl.BlockSpec((tile, units), lambda i: (i, 0))
    return pl.pallas_call(
        combine_kernel,
        grid=(arrived[0].shape[0] // tile,),
        in_specs=[placed, placed]
        + [piece] * len(arrived)
        + [pl.BlockSpec(memory_space=pl.ANY)],
        out_specs=placed,
        out_shape=jax.ShapeDtypeStruct((rows, units), BF16),
        input_output_aliases={2 + len(arrived): 0},
        compiler_params=params(),
        name="combine",
    )(own, near, *arrived, out)


def blank_kernel(out_ref):
    pass


def blank(shape, dtype):
    return pl.pallas_call(
        blank_kernel,
        out_specs=pl.BlockSpec(memory_space=pl.ANY),
        out_shape=jax.ShapeDtypeStruct(shape, dtype),
        name="blank",
    )()


def forward_kernel(count, *refs):
    w_ref, a_ref, m_ref = refs[count : count + 3]
    y_ref, p_ref = refs[-2:]
    hid = jnp.concatenate([ref[...] for ref in refs[:count]], axis=0)
    out = jnp.dot(hid, w_ref[...], preferred_element_type=F32).astype(BF16)
    groups, _, blocks, _, tile = y_ref.shape
    y_ref[:, 0] = out.reshape(groups, blocks, BLK, tile)

    @pl.when(pl.program_id(0) == 0)
    def _():
        ranks = a_ref.shape[1]
        rank = p_ref.shape[1] // blocks
        part = jnp.dot(hid, a_ref[...], preferred_element_type=F32)
        part = jnp.where(m_ref[...].reshape(part.shape) > 0, part, 0.0)
        picked = part[:, :rank]
        for a in range(1, ranks // rank):
            picked = picked + part[:, a * rank : (a + 1) * rank]
        picked = picked.astype(BF16)
        row = lax.broadcasted_iota(jnp.int32, (BLK, BLK), 0)
        column = lax.broadcasted_iota(jnp.int32, (BLK, BLK), 1)
        unit = jnp.where(row == column, 1.0, 0.0).astype(BF16)
        for g in range(groups):
            for b in range(blocks):
                start = (g * blocks + b) * BLK
                p_ref[g, b * rank : (b + 1) * rank, :] = lax.dot_general(
                    picked[start : start + BLK], unit, FIRSTS, preferred_element_type=F32
                ).astype(BF16)


def forward_part(groups, blocks, hids, weight, factor, masks, total, q, rank):
    units, cols = weight.shape
    n_dp, all_blocks, _, ranks = masks.shape
    width = cols // q
    tile = min(512, width)
    per = width // tile
    group, block = groups[0] // groups[1], blocks[0] // blocks[1]
    in_specs = [whole(hid.shape) for hid in hids] + [
        pl.BlockSpec((units, tile), lambda i: (0, i)),
        whole((units, ranks)),
        pl.BlockSpec((groups[1], blocks[1], BLK, ranks), lambda i: (group, block, 0, 0)),
    ]
    operands = [*hids, weight, factor, masks]
    aliases = {}
    if total is not None:
        aliases = {len(operands): 0}
        in_specs.append(pl.BlockSpec(memory_space=pl.ANY))
        operands.append(total)
    turned = (groups[1], blocks[1] * rank, BLK)
    return pl.pallas_call(
        functools.partial(forward_kernel, len(hids)),
        grid=(cols // tile,),
        in_specs=in_specs,
        out_specs=[
            pl.BlockSpec(
                (groups[1], 1, blocks[1], BLK, tile),
                lambda i: (group, i // per, block, 0, i % per),
            ),
            whole(turned),
        ],
        out_shape=[
            jax.ShapeDtypeStruct((n_dp, q, all_blocks, BLK, width), BF16),
            jax.ShapeDtypeStruct(turned, BF16),
        ],
        input_output_aliases=aliases,
        compiler_params=params(),
        name="forward_part",
    )(*operands)


def spread(act, mask):
    blocks, _, ranks = mask.shape
    rank = act.shape[0] // blocks
    row = lax.broadcasted_iota(jnp.int32, (rank, ranks), 0)
    column = lax.broadcasted_iota(jnp.int32, (rank, ranks), 1)
    repeat = jnp.where(column % rank == row, 1.0, 0.0).astype(BF16)
    wide = [
        lax.dot_general(
            act[b * rank : (b + 1) * rank], repeat, FIRSTS, preferred_element_type=F32
        )
        for b in range(blocks)
    ]
    wide = jnp.concatenate(wide, axis=0)
    return jnp.where(mask.reshape(wide.shape) > 0, wide, 0.0).astype(BF16)


def backward_kernel(groups, n_mp, offsets, at_ref, *refs):
    first, count = groups
    slots = len(offsets)
    block_refs = refs[: slots + 1]
    act_refs = refs[slots + 1 : slots + 1 + count]
    m_ref, w_ref, a_ref = refs[slots + 1 + count : slots + 4 + count]
    z_refs = refs[slots + 4 + count : -3]
    g_ref, u_ref, sems = refs[-3:]
    _, q, rows, _ = g_ref.shape
    n_dp = n_mp // q
    top = rows // 2

    def transfers(act):
        for index in range(slots + 1):
            there, part = ring_slot(offsets[min(index, slots - 1)], at_ref, n_dp, n_mp)
            target = g_ref.at[there % count, part]
            if index >= slots - 1:
                target = target.at[pl.ds(top * (index - slots + 1), top)]
            copy = pltpu.make_async_copy(block_refs[index], target, sems.at[index])
            pl.when(there // count == first // count)(copy.start if act else copy.wait)

    @pl.when(pl.program_id(0) == 0)
    def _():
        transfers(True)
        for g in range(count):
            u_ref[g * rows : (g + 1) * rows, :] = spread(act_refs[g][...], m_ref[g])
        transfers(False)

    grads = [
        jnp.concatenate([g_ref[g, h] for h in range(q)], axis=1) for g in range(count)
    ]
    out = lax.dot_general(
        jnp.concatenate(grads, axis=0), w_ref[...], TURNED, preferred_element_type=F32
    )
    out += jnp.dot(u_ref[...], a_ref[...], preferred_element_type=F32)
    for g in range(count):
        z_refs[g][...] = out[g * rows : (g + 1) * rows].astype(z_refs[g].dtype)


def backward_part(groups, at, blocks, offsets, acts, masks, weight, turned_factor, n_mp):
    units, cols = weight.shape
    n_dp, parts, _, ranks = masks.shape
    rows = parts * BLK
    q = n_mp // n_dp
    first, count = groups
    tile = min(896, units)
    return pl.pallas_call(
        functools.partial(backward_kernel, groups, n_mp, offsets),
        grid_spec=pltpu.PrefetchScalarGridSpec(
            num_scalar_prefetch=1,
            grid=(pl.cdiv(units, tile),),
            in_specs=[pl.BlockSpec(memory_space=pl.ANY)] * len(blocks)
            + [whole(act.shape) for act in acts]
            + [
                pl.BlockSpec(
                    (count, parts, BLK, ranks), lambda i, at_ref: (first // count, 0, 0, 0)
                ),
                pl.BlockSpec((tile, cols), lambda i, at_ref: (i, 0)),
                pl.BlockSpec((ranks, tile), lambda i, at_ref: (0, i)),
            ],
            out_specs=[pl.BlockSpec((rows, tile), lambda i, at_ref: (0, i))] * count,
            scratch_shapes=[
                pltpu.VMEM((count, q, rows, cols // q), BF16),
                pltpu.VMEM((count * rows, ranks), BF16),
                pltpu.SemaphoreType.DMA((len(blocks),)),
            ],
        ),
        out_shape=[
            jax.ShapeDtypeStruct((rows, units), BF16 if (first + g) % 2 else F32)
            for g in range(count)
        ],
        compiler_params=params(),
        name="backward_part",
    )(at, *blocks, *acts, masks, weight, turned_factor)


def factor_grad_kernel(n_dp, m_ref, *refs):
    acts = [spread(refs[r][...], m_ref[r]) for r in range(n_dp)]
    hid = jnp.concatenate([ref[...] for ref in refs[n_dp:-1]], axis=0)
    out = lax.dot_general(
        jnp.concatenate(acts, axis=0), hid, FIRSTS, preferred_element_type=F32
    )
    refs[-1][...] = out.astype(BF16)


def factor_grad(masks, acts, hids):
    ranks = masks.shape[3]
    units = hids[0].shape[1]
    tile = units // 2 if units % 256 == 0 else units
    return pl.pallas_call(
        functools.partial(factor_grad_kernel, len(acts)),
        grid=(units // tile,),
        in_specs=[whole(masks.shape)]
        + [whole(act.shape) for act in acts]
        + [pl.BlockSpec((hid.shape[0], tile), lambda i: (0, i)) for hid in hids],
        out_specs=pl.BlockSpec((ranks, tile), lambda i: (0, i)),
        out_shape=jax.ShapeDtypeStruct((ranks, units), BF16),
        compiler_params=params(),
        name="factor_grad",
    )(masks, *acts, *hids)


def shards(
    hidden, down_weight, adapter_down, adapter_up, output_grad, adapter_per_block, live_rows
):
    n_dp = lax.axis_size("dp")
    n_mp = lax.axis_size("mp")
    at = jnp.stack([lax.axis_index("dp"), lax.axis_index("mp")])
    q = n_mp // n_dp
    rows, units = hidden.shape
    width = output_grad.shape[1]
    owned, _, rank = adapter_down.shape
    blocks = rows // BLK
    half = n_mp // 2
    top = rows // 2
    fence = lambda *values: lax.optimization_barrier(values)
    like = jax.ShapeDtypeStruct

    def exchange(value, bit, axis="dp"):
        count = n_dp if axis == "dp" else n_mp
        return lax.ppermute(value, axis, [(i, i ^ bit) for i in range(count)])

    def swap_places(value):
        pairs = [
            (j * n_mp + m, (m // q) * n_mp + j * q + m % q)
            for j in range(n_dp)
            for m in range(n_mp)
        ]
        return lax.ppermute(value, ("dp", "mp"), pairs)

    ring = list(range(0, n_mp, 2)) + list(range(n_mp - 1, 0, -2))
    up_ring = [(ring[i], ring[(i + 1) % n_mp]) for i in range(n_mp)]
    down_ring = [(b, a) for a, b in up_ring]

    def onward(value):
        return lax.ppermute(value, "mp", up_ring)

    def backward_on(value):
        return lax.ppermute(value, "mp", down_ring)

    evens = range(2, n_dp, 2)

    def fetch(hidden, piece):
        held = {0: hidden[piece * BLK : (piece + 1) * BLK]}
        bit = 2
        while bit < n_dp:
            for r in list(held):
                held[r ^ bit] = exchange(held[r], bit)
            bit *= 2
        return {r: held[r] for r in evens}

    def pass_on(fetched):
        return {r + 1: exchange(fetched[r], 1) for r in evens}

    far_steps = [1 << k for k in range(n_mp.bit_length() - 2, -1, -1)]
    sum_steps = [far_steps[:-2], far_steps[-2:-1], far_steps[-1:]]

    def sum_step(value, index):
        for bit in sum_steps[index]:
            value = value + exchange(value.astype(BF16), bit, "mp").astype(F32)
        return value

    (masked_grad,) = call(
        mask_kernel, "mask", [at, live_rows], [output_grad], [like(output_grad.shape, BF16)]
    )
    swapped = swap_places(masked_grad)
    near = exchange(hidden, 1)
    adapter_up, masked_grad, at = fence(adapter_up, masked_grad, at)
    *chosen, masks = call(
        functools.partial(select_kernel, n_dp, owned, rank),
        "select",
        [at, adapter_per_block],
        [adapter_up],
        [like((rank, width), BF16)] * n_dp + [like((n_dp, blocks, BLK, owned * rank), BF16)],
    )
    arrived_up = [exchange(chosen[r], r) if r else chosen[0] for r in range(n_dp)]
    arrived_up[1], hidden_0 = fence(arrived_up[1], hidden)
    fetched = [fetch(hidden_0, 0)]
    turned_factor = jnp.transpose(adapter_down, (0, 2, 1)).reshape(owned * rank, units)
    factor = turned_factor.T

    def forward(groups, span, hids, total):
        return forward_part(groups, span, hids, down_weight, factor, masks, total, q, rank)

    picked = {}
    total, own = forward((0, 1), (0, blocks), [hidden], None)
    picked[0] = [own[0]]
    arrived_up, total, hidden = fence(arrived_up, total, hidden)
    up_sum, block_up = call(
        functools.partial(up_kernel, n_dp, owned),
        "up_part",
        [at, adapter_per_block],
        [masked_grad, *arrived_up],
        [like((blocks * rank, BLK), F32), like((blocks, rank, width), BF16)],
    )
    up_sum = sum_step(up_sum, 0)
    swapped, near, fetched[0], total, up_sum, hidden = fence(
        swapped, near, fetched[0], total, up_sum, hidden
    )

    ahead = behind = swapped
    ring_blocks = [swapped]
    offsets = [0] + [sign * step for step in range(1, half) for sign in (-1, 1)] + [half]
    ahead, behind = onward(ahead), backward_on(behind)
    fetched.append(fetch(hidden, 1))
    passed = [pass_on(fetched[0])]
    up_sum = sum_step(up_sum, 1)
    total, own = forward((1, 1), (0, blocks), [near], total)
    picked[1] = [own[0]]
    ahead, behind, fetched[1], passed, total, up_sum, hidden = fence(
        ahead, behind, fetched[1], passed, total, up_sum, hidden
    )
    ring_blocks += [ahead, behind]
    ahead, behind = onward(ahead), backward_on(behind)
    fetched.append(fetch(hidden, 2))
    passed.append(pass_on(fetched[1]))
    up_sum = sum_step(up_sum, 2)

    def forward_pairs(span, total):
        pieces = range(span[0], span[0] + span[1])
        for r in evens:
            hids = [fetched[p][r] for p in pieces] + [passed[p][r + 1] for p in pieces]
            total, pair = forward((r, 2), span, hids, total)
            for g in range(2):
                picked.setdefault(r + g, []).append(pair[g])
        return total

    total = forward_pairs((0, 2), total)
    ahead, behind, fetched[2], passed, total, up_sum = fence(
        ahead, behind, fetched[2], passed, total, up_sum
    )
    ring_blocks += [ahead, behind]
    for _ in range(3, half):
        ahead, behind = onward(ahead), backward_on(behind)
        ring_blocks += [ahead, behind]
    passed.append(pass_on(fetched[2]))
    passed, up_act = fence(passed, up_sum.astype(BF16))
    acts = [exchange(up_act, r) if r else up_act for r in range(n_dp)]
    total = forward_pairs((2, 1), total)
    ahead, behind, acts, total, picked = fence(ahead, behind, acts, total, picked)
    ring_blocks[-2:] = [ahead, behind]
    total = total.reshape(n_dp, q, rows, width)

    last = [onward(ahead[:top]), backward_on(behind[top:])]
    ahead, behind = opposite(at, total, n_mp)
    ahead, behind = onward(ahead), backward_on(behind)
    held = {r: jnp.concatenate(picked[r], axis=0) for r in range(n_dp)}
    bit = 1
    while bit < n_dp:
        sent = [r for r in held if r & bit]
        arrived = exchange(jnp.concatenate([held.pop(r).astype(BF16) for r in sent]), bit)
        for index, r in enumerate(sent):
            size = blocks * rank
            piece = arrived[index * size : (index + 1) * size]
            held[r ^ bit] = held[r ^ bit].astype(F32) + piece.astype(F32)
        bit *= 2
    down_sum = held[0]
    last, ahead, behind, down_sum, acts = fence(last, ahead, behind, down_sum, acts)
    ring_blocks += last

    def backward(first, count, acts):
        return backward_part(
            (first, count),
            at,
            ring_blocks,
            offsets,
            acts[first : first + count],
            masks,
            down_weight,
            turned_factor,
            n_mp,
        )

    def add_and_send(step, ahead, behind, acts, halves=False):
        ahead, behind = ring_add(step, at, total, ahead, behind, n_mp, halves)
        ahead, behind, acts = fence(ahead, behind, acts)
        return onward(ahead), backward_on(behind), acts

    ends = [0, rows // 3, 3 * rows // 4, rows]

    def partial_gradient(piece):
        cut = slice(ends[piece], ends[piece + 1])
        held = {r: (parts[r][cut] + parts[r + 1][cut].astype(F32)).astype(BF16) for r in evens}
        sent = []
        bit = n_dp // 2
        while bit > 1:
            for r in [r for r in held if r & bit]:
                value = exchange(held.pop(r), bit)
                if r == bit:
                    sent.append(value)
                else:
                    held[r ^ bit] = held[r ^ bit] + value
            bit //= 2
        return sent

    ahead, behind, acts = add_and_send(half - 1, ahead, behind, acts, halves=True)
    down_sum = sum_step(down_sum, 0)
    parts = {}
    for r in evens:
        parts[r], parts[r + 1] = backward(r, 2, acts)
    ahead, behind, parts, down_sum, acts = fence(ahead, behind, parts, down_sum, acts)
    for r in evens:
        parts[r + 1] = exchange(parts[r + 1], 1)
    ahead, behind, acts = add_and_send(half - 2, ahead, behind, acts)
    down_sum = sum_step(down_sum, 1)
    parts, acts = fence(parts, acts)
    arriving = [partial_gradient(0)]
    (parts[1],) = backward(1, 1, acts)
    ahead, behind, parts, arriving, down_sum, acts = fence(
        ahead, behind, parts, arriving, down_sum, acts
    )
    for step in range(half - 3, 0, -1):
        ahead, behind, acts = add_and_send(step, ahead, behind, acts)
    arriving.append(partial_gradient(1))
    down_sum = sum_step(down_sum, 2)
    parts[1] = exchange(parts[1], 1)
    (parts[0],) = backward(0, 1, acts)
    ahead, behind, parts, arriving, down_sum, acts = fence(
        ahead, behind, parts, arriving, down_sum, acts
    )

    base_out = last_add(at, live_rows, total, ahead, behind, n_mp)
    base_out, parts, down_sum, acts = fence(base_out, parts, down_sum, acts)
    base_out = swap_places(base_out)
    branch, *terms = call(
        functools.partial(term_kernel, n_dp, owned),
        "term_up",
        [at, adapter_per_block, live_rows],
        [down_sum, masked_grad, block_up],
        [like((rows, width), F32)] + [like((rank, width), BF16)] * n_dp,
    )
    terms = [exchange(terms[r], r) if r else terms[0] for r in range(n_dp)]
    arriving.append(partial_gradient(2))
    hidden_gradient = blank((rows, units), BF16)
    for piece in range(2):
        hidden_gradient = combine(
            ends[piece], parts[0], parts[1], arriving[piece], hidden_gradient
        )
    groups = [hidden_0, near]
    for r in evens:
        groups += [piece[r] for piece in fetched] + [piece[r + 1] for piece in passed]
    down_grad = factor_grad(masks, acts, groups)
    down_grad = jnp.transpose(down_grad.reshape(owned, rank, units), (0, 2, 1))
    base_out, terms, arriving[2], hidden_gradient, down_grad, branch = fence(
        base_out, terms, arriving[2], hidden_gradient, down_grad, branch
    )
    (up_grad,) = call(
        functools.partial(up_grad_kernel, n_dp, blocks),
        "up_grad",
        [at, adapter_per_block],
        terms,
        [like((owned, rank, width), BF16)],
    )
    hidden_gradient = combine(ends[2], parts[0], parts[1], arriving[2], hidden_gradient)
    layer_out = (base_out.astype(F32) + branch).astype(BF16)
    return layer_out, hidden_gradient, down_grad, up_grad


def solution(mesh):
    return jax.shard_map(
        shards,
        mesh=mesh,
        in_specs=(
            P("dp", "mp"),
            P("mp", "dp"),
            P("dp", "mp", None),
            P("dp", None, "mp"),
            P("dp", "mp"),
            P(),
            P(),
        ),
        out_specs=(P("dp", "mp"), P("dp", "mp"), P("dp", "mp", None), P("dp", None, "mp")),
        check_vma=False,
    )
```

time: 735 us -> 320 us (0.44)
  waiting for transfers between devices: 569 us -> 107 us
  Pallas kernels: 0 us -> 123 us
  matrix products: 88.4 us -> 0 us
  starting transfers between devices: 8.28 us -> 51.4 us
  blocking collectives: 42.8 us -> 0 us
  local copies, waits for them, and re-layouts: 8.02 us -> 24.6 us
  between operations: 13.9 us -> 1.42 us
    all_gather x4 -> x0, waiting for transfers between devices: 368 us -> none  [the longest x1 323 us: shards(): panel = lax.all_gather(down_weight, 'dp', axis=1, tiled=True)]
    reduce_scatter x1 -> x0, waiting for transfers between devices: 178 us -> none  [shards(): lax.psum_scatter(partial_value, 'mp', scatter_dimension=1, tiled=True)]
    pallas_call x0 -> x22, Pallas kernels: none -> 123 us  [the longest x3 46.4 us: backward_part(): pl.pallas_call(functools.partial(backward_kernel, groups, n_mp, offsets),...]
    ppermute x0 -> x47, waiting for transfers between devices: none -> 107 us  [the longest x29 90.3 us: exchange(): return lax.ppermute(value, axis, [(i, i ^ bit) for i in range(count)])]
    dot_general x14 -> x0, matrix products: 88.4 us -> none  [the longest x1 32.2 us: shards(): lax.dot_general(grad_full, panel, (((1,), (1,)), ((), ())), preferred_ele...]
    ppermute x0 -> x47, starting transfers between devices: none -> 51.4 us  [the longest x29 24.1 us: exchange(): return lax.ppermute(value, axis, [(i, i ^ bit) for i in range(count)])]
    psum x1 -> x0, blocking collectives: 42.8 us -> none  [shards(): down_sum, up_sum = lax.psum((down_part, up_part), 'mp')]
    all_to_all x2 -> x0, waiting for transfers between devices: 20.5 us -> none  [the longest x1 15.1 us: shards(): lax.all_to_all(back_down, 'dp', split_axis=0, concat_axis=0, tiled=True)]
  transfers between devices with their start and end apart: 7 -> 47, of which waited for: 6 -> 17; matrix products, arithmetic and copies ran while one was open for 13% -> 3% of each run, Pallas kernels for 0% -> 36%
where the time goes in v2:
time: 320 us; the launch traced here: 318 us
  Pallas kernels  123 us (38%)
  waiting for transfers between devices  107 us (33%)
  starting transfers between devices  51.4 us (16%)
  local copies, waits for them, and re-layouts  24.6 us (8%)
  other arithmetic  10.7 us (3%)
    ppermute x29, waiting for transfers between devices, exchange(): return lax.ppermute(value, axis, [(i, i ^ bit) for i in range(count)])  90.3 us
    pallas_call x3, Pallas kernels, backward_part(): pl.pallas_call(functools.partial(backward_kernel, groups, n_mp, offsets),...  46.4 us
    pallas_call x4, Pallas kernels, forward_part(): pl.pallas_call(functools.partial(forward_kernel, len(hids)), grid=(cols /...  43.8 us
    ppermute x29, starting transfers between devices, exchange(): return lax.ppermute(value, axis, [(i, i ^ bit) for i in range(count)])  24.1 us
    unnamed x106, local copies, waits for them, and re-layouts  19.6 us
    ppermute x8, waiting for transfers between devices, onward(): return lax.ppermute(value, 'mp', up_ring)  12.1 us
    pallas_call x5, Pallas kernels, call(): pl.pallas_call(kernel, grid_spec=pltpu.PrefetchScalarGridSpec(num_scalar_...  11.3 us
    ppermute x8, starting transfers between devices, onward(): return lax.ppermute(value, 'mp', up_ring)  10.4 us
  transfers between devices with their start and end apart: 47, of which 17 were waited for; matrix products, arithmetic and copies ran while one was open for 3% of the time, Pallas kernels for 36%

profile of v2, /device:TPU:0, one launch (start us, length us, event | category | flops | bytes accessed | tf_op | source)
XLA Modules:
  0.0 318.1 jit_solution(1362054822241606604)
XLA Ops:
  11.0 2.6 collective-permute-start.3
  15.4 4.2 %collective-permute-start.4 = (bf16[64,1024]{1,0:T(8,128)(2,1)}, bf16[64,1024]{1,0:T(8,128)(2,1)}, u32[]{:S(2)}, u32[]{:S(2)}) collective-permute-start(bf16[64,1024]{1,0:T(8,128)(2,1)} %get-tuple-element.173), channel_id=1, source_target_pairs={{0,16},{8,24},{16,0},{24,8},{1,17},{9,25},{17,1},{25,9},{2,18},{10... | collective-permute-start | bytes 393224 | tf_op jit(solution)/shard_map/ppermute | solution.py:480
  20.5 2.8 copy.17.refs_2_.refs_5_.refs_3_
  25.0 10.7 %forward_part.4 = (bf16[4,2,3,128,1024]{4,3,2,1,0:T(8,128)(2,1)}, bf16[1,192,128]{2,1,0:T(8,128)(2,1)S(1)}) custom-call(bf16[384,3328]{1,0:T(8,128)(2,1)S(1)} %copy-done.3, bf16[3328,2048]{1,0:T(8,128)(2,1)} %refs_11_.3, bf16[3328,256]{1,0:T(8,128)(2,1)S(1)} %copy.17.refs_2_.refs_5_.refs_3_, ...), custom_call_target="tpu_custom_call" | custom-call | tf_op jit(solution)/shard_map/forward_part/pallas_call | solution.py:323
  35.7 17.1 %collective-permute-done.4.refs_2_ = bf16[64,1024]{1,0:T(8,128)(2,1)} collective-permute-done((bf16[64,1024]{1,0:T(8,128)(2,1)}, bf16[64,1024]{1,0:T(8,128)(2,1)}, u32[]{:S(2)}, u32[]{:S(2)}) %collective-permute-start.4) | collective-permute-done | bytes 131104 | tf_op jit(solution)/shard_map/ppermute | solution.py:480
  57.4 3.1 collective-permute-start.6
  68.2 11.4 %forward_part.5 = (bf16[4,2,3,128,1024]{4,3,2,1,0:T(8,128)(2,1)}, bf16[1,192,128]{2,1,0:T(8,128)(2,1)S(1)}) custom-call(bf16[384,3328]{1,0:T(8,128)(2,1)} %collective-permute-done.1.refs_0_.refs_5_, bf16[3328,2048]{1,0:T(8,128)(2,1)} %refs_11_.3, bf16[3328,256]{1,0:T(8,128)(2,1)S(1)} %copy.17.refs_2_.refs_5_.refs_3_, ...), custom_call_target="tpu_custom_call", output_to_operand_aliasing={{0}: (4, {})} | custom-call | tf_op jit(solution)/shard_map/forward_part/pallas_call | solution.py:323
  79.6 7.3 %collective-permute-done.11 = bf16[192,128]{1,0:T(8,128)(2,1)S(1)} collective-permute-done((bf16[192,128]{1,0:T(8,128)(2,1)S(1)}, bf16[192,128]{1,0:T(8,128)(2,1)S(1)}, u32[]{:S(2)}, u32[]{:S(2)}) %collective-permute-start.11) | collective-permute-done | bytes 49184 | tf_op jit(solution)/shard_map/ppermute | solution.py:480
  89.9 18.6 %collective-permute-done.16 = bf16[192,128]{1,0:T(8,128)(2,1)S(1)} collective-permute-done((bf16[192,128]{1,0:T(8,128)(2,1)S(1)}, bf16[192,128]{1,0:T(8,128)(2,1)S(1)}, u32[]{:S(2)}, u32[]{:S(2)}) %collective-permute-start.16) | collective-permute-done | bytes 49184 | tf_op jit(solution)/shard_map/ppermute | solution.py:480
  108.5 12.7 %forward_part.6 = (bf16[4,2,3,128,1024]{4,3,2,1,0:T(8,128)(2,1)}, bf16[2,128,128]{2,1,0:T(8,128)(2,1)S(1)}) custom-call(bf16[128,3328]{1,0:T(8,128)(2,1)} %collective-permute-done.3.refs_0_.refs_6_, bf16[128,3328]{1,0:T(8,128)(2,1)S(1)} %collective-permute-done.9.refs_1_.refs_7_, ...), custom_call_target="tpu_custom_call", output_to_operand_aliasing={{0}: (7, {})} | custom-call | tf_op jit(solution)/shard_map/forward_part/pallas_call | solution.py:323
  125.6 9.1 %forward_part.7 = (bf16[4,2,3,128,1024]{4,3,2,1,0:T(8,128)(2,1)}, bf16[2,64,128]{2,1,0:T(8,128)(2,1)S(1)}) custom-call(bf16[128,3328]{1,0:T(8,128)(2,1)S(1)} %collective-permute-done.14.refs_0_.refs_8_, bf16[128,3328]{1,0:T(8,128)(2,1)S(1)} %collective-permute-done.19.refs_1_.refs_11_, bf16[3328,2048]{1,0:T(8,128)(2,1)} %refs_11_.3, ...), custom_call_target="tpu_custom_call", output_to_operand_aliasing={{0}: (5, {})} | custom-call | tf_op jit(solution)/shard_map/forward_part/pallas_call | solution.py:323
  134.7 6.7 %collective-permute-done.17.refs_5_ = bf16[384,1024]{1,0:T(8,128)(2,1)S(1)} collective-permute-done((bf16[384,1024]{1,0:T(8,128)(2,1)S(1)}, bf16[384,1024]{1,0:T(8,128)(2,1)S(1)}, u32[]{:S(2)}, u32[]{:S(2)}) %collective-permute-start.17) | collective-permute-done | bytes 786464 | tf_op jit(solution)/shard_map/ppermute | solution.py:495
  141.5 3.5 %collective-permute-start.23 = (bf16[192,1024]{1,0:T(8,128)(2,1)S(1)}, bf16[192,1024]{1,0:T(8,128)(2,1)S(1)}, u32[]{:S(2)}, u32[]{:S(2)}) collective-permute-start(bf16[192,1024]{1,0:T(8,128)(2,1)S(1)} %slice.58), channel_id=1, source_target_pairs={{0,2},{2,4},{4,6},{6,7},{7,5},{5,3},{3,1},{1,0},{8,10},{10,12},{12... | collective-permute-start | bytes 1179656 | tf_op jit(solution)/shard_map/ppermute | solution.py:495
  145.1 2.8 copy-done
  151.0 3.7 %collective-permute-done.28 = bf16[192,128]{1,0:T(8,128)(2,1)S(1)} collective-permute-done((bf16[192,128]{1,0:T(8,128)(2,1)S(1)}, bf16[192,128]{1,0:T(8,128)(2,1)S(1)}, u32[]{:S(2)}, u32[]{:S(2)}) %collective-permute-start.28) | collective-permute-done | bytes 49184 | tf_op jit(solution)/shard_map/ppermute | solution.py:480
  157.0 5.4 %collective-permute-done.25.ahead_ref = bf16[192,1024]{1,0:T(8,128)(2,1)S(1)} collective-permute-done((bf16[192,1024]{1,0:T(8,128)(2,1)S(1)}, bf16[192,1024]{1,0:T(8,128)(2,1)S(1)}, u32[]{:S(2)}, u32[]{:S(2)}) %collective-permute-start.25) | collective-permute-done | bytes 393248 | tf_op jit(solution)/shard_map/ppermute | solution.py:495
  169.1 20.9 %backward_part.3 = (f32[384,3328]{1,0:T(8,128)}, bf16[384,3328]{1,0:T(8,128)(2,1)}) custom-call(s32[2]{0:T(128)S(1)} %pad_add_fusion.at_ref, bf16[384,1024]{1,0:T(8,128)(2,1)S(1)} %collective-permute-done.refs_0_, bf16[384,1024]{1,0:T(8,128)(2,1)S(1)} %collective-permute-done.7.refs_1_, bf16[384,1024]{1,0:T(8,128)(2,1)S(1)} %collective-permute-done.8.refs_2_, ...), custom_call_target="tpu_custom_call" | custom-call | tf_op jit(solution)/shard_map/backward_part/pallas_call | solution.py:406
  191.2 4.1 %collective-permute-done.34 = bf16[384,3328]{1,0:T(8,128)(2,1)} collective-permute-done((bf16[384,3328]{1,0:T(8,128)(2,1)}, bf16[384,3328]{1,0:T(8,128)(2,1)}, u32[]{:S(2)}, u32[]{:S(2)}) %collective-permute-start.34) | collective-permute-done | bytes 2555936 | tf_op jit(solution)/shard_map/ppermute | solution.py:480
  195.3 2.7 add_convert_fusion.1
  200.6 18.3 %collective-permute-done.36 = bf16[192,128]{1,0:T(8,128)(2,1)S(1)} collective-permute-done((bf16[192,128]{1,0:T(8,128)(2,1)S(1)}, bf16[192,128]{1,0:T(8,128)(2,1)S(1)}, u32[]{:S(2)}, u32[]{:S(2)}) %collective-permute-start.36) | collective-permute-done | bytes 49184 | tf_op jit(solution)/shard_map/ppermute | solution.py:480
  218.9 12.5 %backward_part.4 = bf16[384,3328]{1,0:T(8,128)(2,1)} custom-call(s32[2]{0:T(128)S(1)} %pad_add_fusion.at_ref, bf16[384,1024]{1,0:T(8,128)(2,1)S(1)} %collective-permute-done.refs_0_, bf16[384,1024]{1,0:T(8,128)(2,1)S(1)} %collective-permute-done.7.refs_1_, bf16[384,1024]{1,0:T(8,128)(2,1)S(1)} %copy-done.11, ...), custom_call_target="tpu_custom_call" | custom-call | tf_op jit(solution)/shard_map/backward_part/pallas_call | solution.py:406
  232.4 3.0 add_convert_fusion
  242.5 13.0 %backward_part.5.own_ref = f32[384,3328]{1,0:T(8,128)} custom-call(s32[2]{0:T(128)S(1)} %pad_add_fusion.at_ref, bf16[384,1024]{1,0:T(8,128)(2,1)S(1)} %copy-done.7, bf16[384,1024]{1,0:T(8,128)(2,1)S(1)} %copy-done.9, bf16[384,1024]{1,0:T(8,128)(2,1)S(1)} %copy-done.12, bf16[384,1024]{1,0:T(8,128)(2,1)S(1)} %copy-done.14, bf16[384,1024]{1,0:T(8,128)(2,1)S(1)} %copy-done.16, ...), custom_call_target="tpu_custom_call" | custom-call | tf_op jit(solution)/shard_map/backward_part/pallas_call | solution.py:406
  255.5 4.7 %collective-permute-done.41 = bf16[192,128]{1,0:T(8,128)(2,1)S(1)} collective-permute-done((bf16[192,128]{1,0:T(8,128)(2,1)S(1)}, bf16[192,128]{1,0:T(8,128)(2,1)S(1)}, u32[]{:S(2)}, u32[]{:S(2)}) %collective-permute-start.41) | collective-permute-done | bytes 49184 | tf_op jit(solution)/shard_map/ppermute | solution.py:480
  266.0 7.6 %collective-permute-start.42 = (bf16[384,1024]{1,0:T(8,128)(2,1)}, bf16[384,1024]{1,0:T(8,128)(2,1)}, u32[]{:S(2)}, u32[]{:S(2)}) collective-permute-start(bf16[384,1024]{1,0:T(8,128)(2,1)} %last_add.1), channel_id=1, source_target_pairs={{0,0},{1,1},{2,8},{3,9},{4,16},{5,17},{6,24},{7,25},{8,2},{9,3},{1... | collective-permute-start | bytes 2359304 | tf_op jit(solution)/shard_map/ppermute | solution.py:488
  276.0 3.5 %term_up.1 = (f32[384,1024]{1,0:T(8,128)S(1)}, bf16[64,1024]{1,0:T(8,128)(2,1)S(1)}, bf16[64,1024]{1,0:T(8,128)(2,1)}, bf16[64,1024]{1,0:T(8,128)(2,1)}, bf16[64,1024]{1,0:T(8,128)(2,1)}) custom-call(s32[2]{0:T(128)S(1)} %pad_add_fusion.at_ref, s32[12]{0:T(128)S(1)} %copy-done.46, s32[4]{0:T(128)S(1)} %copy-done.48, ...), custom_call_target="tpu_custom_call" | custom-call | tf_op jit(solution)/shard_map/term_up/pallas_call | solution.py:29
  283.5 2.4 copy-done.1
  288.7 4.8 %combine.4.refs_2_ = bf16[384,3328]{1,0:T(8,128)(2,1)} custom-call(f32[384,3328]{1,0:T(8,128)S(1)} %copy-done.1, bf16[384,3328]{1,0:T(8,128)(2,1)S(1)} %collective-permute-done.39.refs_0_, bf16[160,3328]{1,0:T(8,128)(2,1)} %collective-permute-done.40.refs_1_, bf16[384,3328]{1,0:T(8,128)(2,1)} %combine.3.refs_2_), custom_call_target="tpu_custom_call", output_to_operand_aliasing={{}: (3, {})} | custom-call | tf_op jit(solution)/shard_map/combine/pallas_call | solution.py:248
  293.6 6.3 %factor_grad.1 = bf16[256,3328]{1,0:T(8,128)(2,1)} custom-call(bf16[4,3,128,256]{3,2,1,0:T(8,128)(2,1)S(1)} %get-tuple-element.175.refs_3_.refs_6_.refs_4_.refs_11_.refs_10_.m_ref, bf16[192,128]{1,0:T(8,128)(2,1)S(1)} %convert_add_fusion.4.refs_9_.refs_0_, bf16[192,128]{1,0:T(8,128)(2,1)S(1)} %collective-permute-done.20.refs_9_.refs_1_, ...), custom_call_target="tpu_custom_call" | custom-call | tf_op jit(solution)/shard_map/factor_grad/pallas_call | solution.py:449
  299.8 8.9 %collective-permute-done.44.refs_2_ = bf16[64,1024]{1,0:T(8,128)(2,1)} collective-permute-done((bf16[64,1024]{1,0:T(8,128)(2,1)}, bf16[64,1024]{1,0:T(8,128)(2,1)}, u32[]{:S(2)}, u32[]{:S(2)}) %collective-permute-start.44) | collective-permute-done | bytes 131104 | tf_op jit(solution)/shard_map/ppermute | solution.py:480
  312.4 2.9 combine.5
  315.3 2.8 up_grad.1
  (220 shorter events, 76.8 us)
Async XLA Ops:
  0.6 62.2 %collective-permute-start.1 = (bf16[384,3328]{1,0:T(8,128)(2,1)}, bf16[384,3328]{1,0:T(8,128)(2,1)}, u32[]{:S(2)}, u32[]{:S(2)}) collective-permute-start(bf16[384,3328]{1,0:T(8,128)(2,1)} %refs_4_.2), channel_id=1, source_target_pairs={{0,8},{8,0},{16,24},{24,16},{1,9},{9,1},{17,25},{25,17},{2,10},{10... | collective-permute-start | bytes 7667720 | tf_op jit(solution)/shard_map/ppermute | solution.py:480
  11.0 51.8 %collective-permute-start.3 = (bf16[128,3328]{1,0:T(8,128)(2,1)}, bf16[128,3328]{1,0:T(8,128)(2,1)}, u32[]{:S(2)}, u32[]{:S(2)}) collective-permute-start(bf16[128,3328]{1,0:T(8,128)(2,1)} %slice.51), channel_id=1, source_target_pairs={{0,16},{8,24},{16,0},{24,8},{1,17},{9,25},{17,1},{25,9},{2,18},{10... | collective-permute-start | bytes 2555912 | tf_op jit(solution)/shard_map/ppermute | solution.py:480
  13.6 49.1 %collective-permute-start = (bf16[384,1024]{1,0:T(8,128)(2,1)}, bf16[384,1024]{1,0:T(8,128)(2,1)S(1)}, u32[]{:S(2)}, u32[]{:S(2)}) collective-permute-start(bf16[384,1024]{1,0:T(8,128)(2,1)} %mask.1.grad_ref), channel_id=1, source_target_pairs={{0,0},{1,1},{2,8},{3,9},{4,16},{5,17},{6,24},{7,25},{8,2},{9,3},{1... | collective-permute-start | bytes 2359304 | tf_op jit(solution)/shard_map/ppermute | solution.py:488
  15.4 37.3 %collective-permute-start.4 = (bf16[64,1024]{1,0:T(8,128)(2,1)}, bf16[64,1024]{1,0:T(8,128)(2,1)}, u32[]{:S(2)}, u32[]{:S(2)}) collective-permute-start(bf16[64,1024]{1,0:T(8,128)(2,1)} %get-tuple-element.173), channel_id=1, source_target_pairs={{0,16},{8,24},{16,0},{24,8},{1,17},{9,25},{17,1},{25,9},{2,18},{10... | collective-permute-start | bytes 393224 | tf_op jit(solution)/shard_map/ppermute | solution.py:480
  19.7 35.5 %collective-permute-start.5 = (bf16[64,1024]{1,0:T(8,128)(2,1)}, bf16[64,1024]{1,0:T(8,128)(2,1)}, u32[]{:S(2)}, u32[]{:S(2)}) collective-permute-start(bf16[64,1024]{1,0:T(8,128)(2,1)} %get-tuple-element.174), channel_id=1, source_target_pairs={{0,24},{8,16},{16,8},{24,0},{1,25},{9,17},{17,9},{25,1},{2,26},{10... | collective-permute-start | bytes 393224 | tf_op jit(solution)/shard_map/ppermute | solution.py:480
  62.9 24.1 %collective-permute-start.9 = (bf16[128,3328]{1,0:T(8,128)(2,1)S(1)}, bf16[128,3328]{1,0:T(8,128)(2,1)S(1)}, u32[]{:S(2)}, u32[]{:S(2)}) collective-permute-start(bf16[128,3328]{1,0:T(8,128)(2,1)S(1)} %slice.52), channel_id=1, source_target_pairs={{0,16},{8,24},{16,0},{24,8},{1,17},{9,25},{17,1},{25,9},{2,18},{10... | collective-permute-start | bytes 2555912 | tf_op jit(solution)/shard_map/ppermute | solution.py:480
  64.6 22.4 %collective-permute-start.10 = (bf16[128,3328]{1,0:T(8,128)(2,1)}, bf16[128,3328]{1,0:T(8,128)(2,1)S(1)}, u32[]{:S(2)}, u32[]{:S(2)}) collective-permute-start(bf16[128,3328]{1,0:T(8,128)(2,1)} %collective-permute-done.3.refs_0_.refs_6_), channel_id=1, source_target_pairs={{0,8},{8,0},{16,24},{24,16},{1,9},{9,1},{17,25},{25,17},{2,10},{10... | collective-permute-start | bytes 2555912 | tf_op jit(solution)/shard_map/ppermute | solution.py:480
  64.6 22.4 %collective-permute-start.7 = (bf16[384,1024]{1,0:T(8,128)(2,1)S(1)}, bf16[384,1024]{1,0:T(8,128)(2,1)S(1)}, u32[]{:S(2)}, u32[]{:S(2)}) collective-permute-start(bf16[384,1024]{1,0:T(8,128)(2,1)S(1)} %collective-permute-done.refs_0_), channel_id=1, source_target_pairs={{0,2},{2,4},{4,6},{6,7},{7,5},{5,3},{3,1},{1,0},{8,10},{10,12},{12... | collective-permute-start | bytes 2359304 | tf_op jit(solution)/shard_map/ppermute | solution.py:495
  66.2 20.8 %collective-permute-start.8 = (bf16[384,1024]{1,0:T(8,128)(2,1)S(1)}, bf16[384,1024]{1,0:T(8,128)(2,1)S(1)}, u32[]{:S(2)}, u32[]{:S(2)}) collective-permute-start(bf16[384,1024]{1,0:T(8,128)(2,1)S(1)} %collective-permute-done.refs_0_), channel_id=1, source_target_pairs={{2,0},{4,2},{6,4},{7,6},{5,7},{3,5},{1,3},{0,1},{10,8},{12,10},{14... | collective-permute-start | bytes 2359304 | tf_op jit(solution)/shard_map/ppermute | solution.py:498
  66.6 20.3 %collective-permute-start.11 = (bf16[192,128]{1,0:T(8,128)(2,1)S(1)}, bf16[192,128]{1,0:T(8,128)(2,1)S(1)}, u32[]{:S(2)}, u32[]{:S(2)}) collective-permute-start(bf16[192,128]{1,0:T(8,128)(2,1)S(1)} %convert_element_type.83), channel_id=1, source_target_pairs={{0,2},{1,3},{2,0},{3,1},{4,6},{5,7},{6,4},{7,5},{8,10},{9,11},{10,... | collective-permute-start | bytes 147464 | tf_op jit(solution)/shard_map/ppermute | solution.py:480
  87.0 21.5 %collective-permute-start.15 = (bf16[128,3328]{1,0:T(8,128)(2,1)S(1)}, bf16[128,3328]{1,0:T(8,128)(2,1)S(1)}, u32[]{:S(2)}, u32[]{:S(2)}) collective-permute-start(bf16[128,3328]{1,0:T(8,128)(2,1)S(1)} %collective-permute-done.9.refs_1_.refs_7_), channel_id=1, source_target_pairs={{0,8},{8,0},{16,24},{24,16},{1,9},{9,1},{17,25},{25,17},{2,10},{10... | collective-permute-start | bytes 2555912 | tf_op jit(solution)/shard_map/ppermute | solution.py:480
  87.1 34.1 %collective-permute-start.14 = (bf16[128,3328]{1,0:T(8,128)(2,1)S(1)}, bf16[128,3328]{1,0:T(8,128)(2,1)S(1)}, u32[]{:S(2)}, u32[]{:S(2)}) collective-permute-start(bf16[128,3328]{1,0:T(8,128)(2,1)S(1)} %slice.53), channel_id=1, source_target_pairs={{0,16},{8,24},{16,0},{24,8},{1,17},{9,25},{17,1},{25,9},{2,18},{10... | collective-permute-start | bytes 2555912 | tf_op jit(solution)/shard_map/ppermute | solution.py:480
  87.8 33.4 %collective-permute-start.12 = (bf16[384,1024]{1,0:T(8,128)(2,1)S(1)}, bf16[384,1024]{1,0:T(8,128)(2,1)S(1)}, u32[]{:S(2)}, u32[]{:S(2)}) collective-permute-start(bf16[384,1024]{1,0:T(8,128)(2,1)S(1)} %collective-permute-done.7.refs_1_), channel_id=1, source_target_pairs={{0,2},{2,4},{4,6},{6,7},{7,5},{5,3},{3,1},{1,0},{8,10},{10,12},{12... | collective-permute-start | bytes 2359304 | tf_op jit(solution)/shard_map/ppermute | solution.py:495
  88.9 32.4 %collective-permute-start.13 = (bf16[384,1024]{1,0:T(8,128)(2,1)S(1)}, bf16[384,1024]{1,0:T(8,128)(2,1)S(1)}, u32[]{:S(2)}, u32[]{:S(2)}) collective-permute-start(bf16[384,1024]{1,0:T(8,128)(2,1)S(1)} %collective-permute-done.8.refs_2_), channel_id=1, source_target_pairs={{2,0},{4,2},{6,4},{7,6},{5,7},{3,5},{1,3},{0,1},{10,8},{12,10},{14... | collective-permute-start | bytes 2359304 | tf_op jit(solution)/shard_map/ppermute | solution.py:498
  89.8 18.7 %collective-permute-start.16 = (bf16[192,128]{1,0:T(8,128)(2,1)S(1)}, bf16[192,128]{1,0:T(8,128)(2,1)S(1)}, u32[]{:S(2)}, u32[]{:S(2)}) collective-permute-start(bf16[192,128]{1,0:T(8,128)(2,1)S(1)} %convert_element_type.85), channel_id=1, source_target_pairs={{0,1},{1,0},{2,3},{3,2},{4,5},{5,4},{6,7},{7,6},{8,9},{9,8},{10,11... | collective-permute-start | bytes 147464 | tf_op jit(solution)/shard_map/ppermute | solution.py:480
  121.4 19.9 %collective-permute-start.17 = (bf16[384,1024]{1,0:T(8,128)(2,1)S(1)}, bf16[384,1024]{1,0:T(8,128)(2,1)S(1)}, u32[]{:S(2)}, u32[]{:S(2)}) collective-permute-start(bf16[384,1024]{1,0:T(8,128)(2,1)S(1)} %collective-permute-done.12.refs_3_), channel_id=1, source_target_pairs={{0,2},{2,4},{4,6},{6,7},{7,5},{5,3},{3,1},{1,0},{8,10},{10,12},{12... | collective-permute-start | bytes 2359304 | tf_op jit(solution)/shard_map/ppermute | solution.py:495
  121.4 19.9 %collective-permute-start.18 = (bf16[384,1024]{1,0:T(8,128)(2,1)S(1)}, bf16[384,1024]{1,0:T(8,128)(2,1)S(1)}, u32[]{:S(2)}, u32[]{:S(2)}) collective-permute-start(bf16[384,1024]{1,0:T(8,128)(2,1)S(1)} %collective-permute-done.13.refs_4_), channel_id=1, source_target_pairs={{2,0},{4,2},{6,4},{7,6},{5,7},{3,5},{1,3},{0,1},{10,8},{12,10},{14... | collective-permute-start | bytes 2359304 | tf_op jit(solution)/shard_map/ppermute | solution.py:498
  165.6 24.5 %collective-permute-start.29 = (bf16[384,1024]{1,0:T(8,128)(2,1)S(1)}, bf16[384,1024]{1,0:T(8,128)(2,1)S(1)}, u32[]{:S(2)}, u32[]{:S(2)}) collective-permute-start(bf16[384,1024]{1,0:T(8,128)(2,1)S(1)} %get-tuple-element.237), channel_id=1, source_target_pairs={{0,2},{2,4},{4,6},{6,7},{7,5},{5,3},{3,1},{1,0},{8,10},{10,12},{12... | collective-permute-start | bytes 2359304 | tf_op jit(solution)/shard_map/ppermute | solution.py:495
  167.4 22.7 %collective-permute-start.30 = (bf16[384,1024]{1,0:T(8,128)(2,1)S(1)}, bf16[384,1024]{1,0:T(8,128)(2,1)S(1)}, u32[]{:S(2)}, u32[]{:S(2)}) collective-permute-start(bf16[384,1024]{1,0:T(8,128)(2,1)S(1)} %get-tuple-element.238), channel_id=1, source_target_pairs={{2,0},{4,2},{6,4},{7,6},{5,7},{3,5},{1,3},{0,1},{10,8},{12,10},{14... | collective-permute-start | bytes 2359304 | tf_op jit(solution)/shard_map/ppermute | solution.py:498
  167.7 22.4 %collective-permute-start.31 = (bf16[192,128]{1,0:T(8,128)(2,1)S(1)}, bf16[192,128]{1,0:T(8,128)(2,1)S(1)}, u32[]{:S(2)}, u32[]{:S(2)}) collective-permute-start(bf16[192,128]{1,0:T(8,128)(2,1)S(1)} %convert_element_type.94), channel_id=1, source_target_pairs={{0,4},{1,5},{2,6},{3,7},{4,0},{5,1},{6,2},{7,3},{8,12},{9,13},{10,... | collective-permute-start | bytes 147464 | tf_op jit(solution)/shard_map/ppermute | solution.py:480
  198.0 33.4 %collective-permute-start.35 = (bf16[128,3328]{1,0:T(8,128)(2,1)}, bf16[128,3328]{1,0:T(8,128)(2,1)S(1)}, u32[]{:S(2)}, u32[]{:S(2)}) collective-permute-start(bf16[128,3328]{1,0:T(8,128)(2,1)} %add_convert_fusion.1), channel_id=1, source_target_pairs={{0,16},{8,24},{16,0},{24,8},{1,17},{9,25},{17,1},{25,9},{2,18},{10... | collective-permute-start | bytes 2555912 | tf_op jit(solution)/shard_map/ppermute | solution.py:480
  198.2 33.3 %collective-permute-start.32 = (bf16[384,1024]{1,0:T(8,128)(2,1)S(1)}, bf16[384,1024]{1,0:T(8,128)(2,1)S(1)}, u32[]{:S(2)}, u32[]{:S(2)}) collective-permute-start(bf16[384,1024]{1,0:T(8,128)(2,1)S(1)} %get-tuple-element.256), channel_id=1, source_target_pairs={{0,2},{2,4},{4,6},{6,7},{7,5},{5,3},{3,1},{1,0},{8,10},{10,12},{12... | collective-permute-start | bytes 2359304 | tf_op jit(solution)/shard_map/ppermute | solution.py:495
  198.5 33.0 %collective-permute-start.33 = (bf16[384,1024]{1,0:T(8,128)(2,1)S(1)}, bf16[384,1024]{1,0:T(8,128)(2,1)S(1)}, u32[]{:S(2)}, u32[]{:S(2)}) collective-permute-start(bf16[384,1024]{1,0:T(8,128)(2,1)S(1)} %get-tuple-element.257), channel_id=1, source_target_pairs={{2,0},{4,2},{6,4},{7,6},{5,7},{3,5},{1,3},{0,1},{10,8},{12,10},{14... | collective-permute-start | bytes 2359304 | tf_op jit(solution)/shard_map/ppermute | solution.py:498
  232.4 29.6 %collective-permute-start.39 = (bf16[384,3328]{1,0:T(8,128)(2,1)}, bf16[384,3328]{1,0:T(8,128)(2,1)S(1)}, u32[]{:S(2)}, u32[]{:S(2)}) collective-permute-start(bf16[384,3328]{1,0:T(8,128)(2,1)} %backward_part.4), channel_id=1, source_target_pairs={{0,8},{8,0},{16,24},{24,16},{1,9},{9,1},{17,25},{25,17},{2,10},{10... | collective-permute-start | bytes 7667720 | tf_op jit(solution)/shard_map/ppermute | solution.py:480
  235.4 26.6 %collective-permute-start.40 = (bf16[160,3328]{1,0:T(8,128)(2,1)}, bf16[160,3328]{1,0:T(8,128)(2,1)}, u32[]{:S(2)}, u32[]{:S(2)}) collective-permute-start(bf16[160,3328]{1,0:T(8,128)(2,1)} %add_convert_fusion), channel_id=1, source_target_pairs={{0,16},{8,24},{16,0},{24,8},{1,17},{9,25},{17,1},{25,9},{2,18},{10... | collective-permute-start | bytes 3194888 | tf_op jit(solution)/shard_map/ppermute | solution.py:480
  239.3 21.0 %collective-permute-start.37 = (bf16[384,1024]{1,0:T(8,128)(2,1)}, bf16[384,1024]{1,0:T(8,128)(2,1)S(1)}, u32[]{:S(2)}, u32[]{:S(2)}) collective-permute-start(bf16[384,1024]{1,0:T(8,128)(2,1)} %get-tuple-element.279), channel_id=1, source_target_pairs={{0,2},{2,4},{4,6},{6,7},{7,5},{5,3},{3,1},{1,0},{8,10},{10,12},{12... | collective-permute-start | bytes 2359304 | tf_op jit(solution)/shard_map/ppermute | solution.py:495
  239.3 21.9 %collective-permute-start.38 = (bf16[384,1024]{1,0:T(8,128)(2,1)}, bf16[384,1024]{1,0:T(8,128)(2,1)S(1)}, u32[]{:S(2)}, u32[]{:S(2)}) collective-permute-start(bf16[384,1024]{1,0:T(8,128)(2,1)} %get-tuple-element.280), channel_id=1, source_target_pairs={{2,0},{4,2},{6,4},{7,6},{5,7},{3,5},{1,3},{0,1},{10,8},{12,10},{14... | collective-permute-start | bytes 2359304 | tf_op jit(solution)/shard_map/ppermute | solution.py:498
  241.3 18.9 %collective-permute-start.41 = (bf16[192,128]{1,0:T(8,128)(2,1)S(1)}, bf16[192,128]{1,0:T(8,128)(2,1)S(1)}, u32[]{:S(2)}, u32[]{:S(2)}) collective-permute-start(bf16[192,128]{1,0:T(8,128)(2,1)S(1)} %convert_element_type.102), channel_id=1, source_target_pairs={{0,1},{1,0},{2,3},{3,2},{4,5},{5,4},{6,7},{7,6},{8,9},{9,8},{10,11... | collective-permute-start | bytes 147464 | tf_op jit(solution)/shard_map/ppermute | solution.py:480
  266.0 44.1 %collective-permute-start.42 = (bf16[384,1024]{1,0:T(8,128)(2,1)}, bf16[384,1024]{1,0:T(8,128)(2,1)}, u32[]{:S(2)}, u32[]{:S(2)}) collective-permute-start(bf16[384,1024]{1,0:T(8,128)(2,1)} %last_add.1), channel_id=1, source_target_pairs={{0,0},{1,1},{2,8},{3,9},{4,16},{5,17},{6,24},{7,25},{8,2},{9,3},{1... | collective-permute-start | bytes 2359304 | tf_op jit(solution)/shard_map/ppermute | solution.py:488
  276.0 34.2 %collective-permute-start.46 = (bf16[96,3328]{1,0:T(8,128)(2,1)}, bf16[96,3328]{1,0:T(8,128)(2,1)}, u32[]{:S(2)}, u32[]{:S(2)}) collective-permute-start(bf16[96,3328]{1,0:T(8,128)(2,1)} %add_convert_fusion.3), channel_id=1, source_target_pairs={{0,16},{8,24},{16,0},{24,8},{1,17},{9,25},{17,1},{25,9},{2,18},{10... | collective-permute-start | bytes 1916936 | tf_op jit(solution)/shard_map/ppermute | solution.py:480
  281.3 27.4 %collective-permute-start.44 = (bf16[64,1024]{1,0:T(8,128)(2,1)}, bf16[64,1024]{1,0:T(8,128)(2,1)}, u32[]{:S(2)}, u32[]{:S(2)}) collective-permute-start(bf16[64,1024]{1,0:T(8,128)(2,1)} %get-tuple-element.306), channel_id=1, source_target_pairs={{0,16},{8,24},{16,0},{24,8},{1,17},{9,25},{17,1},{25,9},{2,18},{10... | collective-permute-start | bytes 393224 | tf_op jit(solution)/shard_map/ppermute | solution.py:480
  283.3 26.8 %collective-permute-start.45 = (bf16[64,1024]{1,0:T(8,128)(2,1)}, bf16[64,1024]{1,0:T(8,128)(2,1)}, u32[]{:S(2)}, u32[]{:S(2)}) collective-permute-start(bf16[64,1024]{1,0:T(8,128)(2,1)} %get-tuple-element.307), channel_id=1, source_target_pairs={{0,24},{8,16},{16,8},{24,0},{1,25},{9,17},{17,9},{25,1},{2,26},{10... | collective-permute-start | bytes 393224 | tf_op jit(solution)/shard_map/ppermute | solution.py:480
  (68 other events, 1301.6 us)

commit v3 on v2

--- a/solution.py
+++ b/solution.py
@@ -8,6 +8,7 @@
 from jax.sharding import PartitionSpec as P
 
 BLK = 128
+SCALE = 8
 F32 = jnp.float32
 BF16 = jnp.bfloat16
 VMEM_LIMIT = 44 * 1024 * 1024
@@ -19,6 +20,10 @@
 
 def params():
     return pltpu.CompilerParams(vmem_limit_bytes=VMEM_LIMIT)
+
+
+def cost(flops):
+    return pl.CostEstimate(flops=int(flops), bytes_accessed=0, transcendentals=0)
 
 
 def whole(shape):
@@ -233,7 +238,7 @@
 
 
 def combine_kernel(own_ref, *refs):
-    total = own_ref[...]
+    total = own_ref[...].astype(F32)
     for ref in refs[:-2]:
         total += ref[...].astype(F32)
     refs[-1][...] = total.astype(BF16)
@@ -336,6 +341,7 @@
             jax.ShapeDtypeStruct(turned, BF16),
         ],
         input_output_aliases=aliases,
+        cost_estimate=cost(SCALE * groups[1] * blocks[1] * BLK * units * cols),
         compiler_params=params(),
         name="forward_part",
     )(*operands)
@@ -425,9 +431,10 @@
             ],
         ),
         out_shape=[
-            jax.ShapeDtypeStruct((rows, units), BF16 if (first + g) % 2 else F32)
-            for g in range(count)
-        ],
+            jax.ShapeDtypeStruct((rows, units), BF16)
+        ]
+        * count,
+        cost_estimate=cost(SCALE * count * rows * units * cols),
         compiler_params=params(),
         name="backward_part",
     )(at, *blocks, *acts, masks, weight, turned_factor)
@@ -498,9 +505,10 @@
         return lax.ppermute(value, "mp", down_ring)
 
     evens = range(2, n_dp, 2)
+    cuts = [0, rows // 4, 2 * rows // 3, rows]
 
     def fetch(hidden, piece):
-        held = {0: hidden[piece * BLK : (piece + 1) * BLK]}
+        held = {0: hidden[cuts[piece] : cuts[piece + 1]]}
         bit = 2
         while bit < n_dp:
             for r in list(held):
@@ -573,10 +581,8 @@
     ahead, behind = onward(ahead), backward_on(behind)
     fetched.append(fetch(hidden, 2))
     passed.append(pass_on(fetched[1]))
-    up_sum = sum_step(up_sum, 2)
-
-    def forward_pairs(span, total):
-        pieces = range(span[0], span[0] + span[1])
+
+    def forward_pairs(span, pieces, total):
         for r in evens:
             hids = [fetched[p][r] for p in pieces] + [passed[p][r + 1] for p in pieces]
             total, pair = forward((r, 2), span, hids, total)
@@ -584,7 +590,9 @@
                 picked.setdefault(r + g, []).append(pair[g])
         return total
 
-    total = forward_pairs((0, 2), total)
+    total = forward_pairs((0, 2), (0, 1), total)
+    total, up_sum = fence(total, up_sum)
+    up_sum = sum_step(up_sum, 2)
     ahead, behind, fetched[2], passed, total, up_sum = fence(
         ahead, behind, fetched[2], passed, total, up_sum
     )
@@ -595,7 +603,7 @@
     passed.append(pass_on(fetched[2]))
     passed, up_act = fence(passed, up_sum.astype(BF16))
     acts = [exchange(up_act, r) if r else up_act for r in range(n_dp)]
-    total = forward_pairs((2, 1), total)
+    total = forward_pairs((2, 1), (2,), total)
     ahead, behind, acts, total, picked = fence(ahead, behind, acts, total, picked)
     ring_blocks[-2:] = [ahead, behind]
     total = total.reshape(n_dp, q, rows, width)
@@ -630,16 +638,19 @@
             n_mp,
         )
 
-    def add_and_send(step, ahead, behind, acts, halves=False):
+    def add_and_send(step, ahead, behind, *others, halves=False):
         ahead, behind = ring_add(step, at, total, ahead, behind, n_mp, halves)
-        ahead, behind, acts = fence(ahead, behind, acts)
-        return onward(ahead), backward_on(behind), acts
+        ahead, behind, *others = fence(ahead, behind, *others)
+        return onward(ahead), backward_on(behind), *others
 
     ends = [0, rows // 3, 3 * rows // 4, rows]
 
     def partial_gradient(piece):
         cut = slice(ends[piece], ends[piece + 1])
-        held = {r: (parts[r][cut] + parts[r + 1][cut].astype(F32)).astype(BF16) for r in evens}
+        held = {
+            r: (parts[r][cut].astype(F32) + parts[r + 1][cut].astype(F32)).astype(BF16)
+            for r in evens
+        }
         sent = []
         bit = n_dp // 2
         while bit > 1:
@@ -658,18 +669,19 @@
     for r in evens:
         parts[r], parts[r + 1] = backward(r, 2, acts)
     ahead, behind, parts, down_sum, acts = fence(ahead, behind, parts, down_sum, acts)
+    ahead, behind, acts, parts = add_and_send(half - 2, ahead, behind, acts, parts)
     for r in evens:
         parts[r + 1] = exchange(parts[r + 1], 1)
-    ahead, behind, acts = add_and_send(half - 2, ahead, behind, acts)
-    down_sum = sum_step(down_sum, 1)
     parts, acts = fence(parts, acts)
     arriving = [partial_gradient(0)]
     (parts[1],) = backward(1, 1, acts)
+    parts[1], down_sum = fence(parts[1], down_sum)
+    down_sum = sum_step(down_sum, 1)
     ahead, behind, parts, arriving, down_sum, acts = fence(
         ahead, behind, parts, arriving, down_sum, acts
     )
     for step in range(half - 3, 0, -1):
-        ahead, behind, acts = add_and_send(step, ahead, behind, acts)
+        ahead, behind, acts, parts = add_and_send(step, ahead, behind, acts, parts)
     arriving.append(partial_gradient(1))
     down_sum = sum_step(down_sum, 2)
     parts[1] = exchange(parts[1], 1)
@@ -679,8 +691,6 @@
     )
 
     base_out = last_add(at, live_rows, total, ahead, behind, n_mp)
-    base_out, parts, down_sum, acts = fence(base_out, parts, down_sum, acts)
-    base_out = swap_places(base_out)
     branch, *terms = call(
         functools.partial(term_kernel, n_dp, owned),
         "term_up",
@@ -688,6 +698,8 @@
         [down_sum, masked_grad, block_up],
         [like((rows, width), F32)] + [like((rank, width), BF16)] * n_dp,
     )
+    base_out, terms, parts, acts = fence(base_out, terms, parts, acts)
+    base_out = swap_places(base_out)
     terms = [exchange(terms[r], r) if r else terms[0] for r in range(n_dp)]
     arriving.append(partial_gradient(2))
     hidden_gradient = blank((rows, units), BF16)
@@ -700,8 +712,8 @@
         groups += [piece[r] for piece in fetched] + [piece[r + 1] for piece in passed]
     down_grad = factor_grad(masks, acts, groups)
     down_grad = jnp.transpose(down_grad.reshape(owned, rank, units), (0, 2, 1))
-    base_out, terms, arriving[2], hidden_gradient, down_grad, branch = fence(
-        base_out, terms, arriving[2], hidden_gradient, down_grad, branch
+    base_out, terms, hidden_gradient, down_grad, branch = fence(
+        base_out, terms, hidden_gradient, down_grad, branch
     )
     (up_grad,) = call(
         functools.partial(up_grad_kernel, n_dp, blocks),
@@ -710,8 +722,9 @@
         terms,
         [like((owned, rank, width), BF16)],
     )
+    layer_out = (base_out.astype(F32) + branch).astype(BF16)
+    layer_out, up_grad, arriving[2] = fence(layer_out, up_grad, arriving[2])
     hidden_gradient = combine(ends[2], parts[0], parts[1], arriving[2], hidden_gradient)
-    layer_out = (base_out.astype(F32) + branch).astype(BF16)
     return layer_out, hidden_gradient, down_grad, up_grad
 
 

time: 320 us -> 295 us (0.922)
  waiting for transfers between devices: 107 us -> 83.1 us
  starting transfers between devices: 51.4 us -> 57.6 us
    ppermute x29, waiting for transfers between devices: 90.3 us -> 67.8 us  [exchange(): return lax.ppermute(value, axis, [(i, i ^ bit) for i in range(count)])]
    ppermute x29, starting transfers between devices: 24.1 us -> 31.4 us  [exchange(): return lax.ppermute(value, axis, [(i, i ^ bit) for i in range(count)])]
    ppermute x8, starting transfers between devices: 10.4 us -> 5.99 us  [onward(): return lax.ppermute(value, 'mp', up_ring)]
    ppermute x8, starting transfers between devices: 7.48 us -> 11.3 us  [backward_on(): return lax.ppermute(value, 'mp', down_ring)]
    unnamed x106 -> x130, local copies, waits for them, and re-layouts: 19.6 us -> 18.7 us
  transfers between devices with their start and end apart: 47 -> 47, of which waited for: 17 -> 19; matrix products, arithmetic and copies ran while one was open for 3% -> 4% of each run, Pallas kernels for 36% -> 37%
where the time goes in v3:
time: 295 us; the launch traced here: 294 us
  Pallas kernels  120 us (41%)
  waiting for transfers between devices  83.1 us (28%)
  starting transfers between devices  57.6 us (20%)
  local copies, waits for them, and re-layouts  22.7 us (8%)
  other arithmetic  8.89 us (3%)
    ppermute x29, waiting for transfers between devices, exchange(): return lax.ppermute(value, axis, [(i, i ^ bit) for i in range(count)])  67.8 us
    pallas_call x3, Pallas kernels, backward_part(): pl.pallas_call(functools.partial(backward_kernel, groups, n_mp, offsets),...  46.5 us
    pallas_call x4, Pallas kernels, forward_part(): pl.pallas_call(functools.partial(forward_kernel, len(hids)), grid=(cols /...  43.7 us
    ppermute x29, starting transfers between devices, exchange(): return lax.ppermute(value, axis, [(i, i ^ bit) for i in range(count)])  31.4 us
    unnamed x130, local copies, waits for them, and re-layouts  18.7 us
    ppermute x8, waiting for transfers between devices, onward(): return lax.ppermute(value, 'mp', up_ring)  13.6 us
    ppermute x8, starting transfers between devices, backward_on(): return lax.ppermute(value, 'mp', down_ring)  11.3 us
    pallas_call x5, Pallas kernels, call(): pl.pallas_call(kernel, grid_spec=pltpu.PrefetchScalarGridSpec(num_scalar_...  9.1 us
  transfers between devices with their start and end apart: 47, of which 19 were waited for; matrix products, arithmetic and copies ran while one was open for 4% of the time, Pallas kernels for 37%

profile of v3, /device:TPU:0, one launch (start us, length us, event | category | flops | bytes accessed | tf_op | source)
XLA Modules:
  0.0 293.8 jit_solution(8650254977595111153)
XLA Ops:
  9.1 5.9 %collective-permute-start.4 = (bf16[64,1024]{1,0:T(8,128)(2,1)}, bf16[64,1024]{1,0:T(8,128)(2,1)}, u32[]{:S(2)}, u32[]{:S(2)}) collective-permute-start(bf16[64,1024]{1,0:T(8,128)(2,1)} %get-tuple-element.187), channel_id=1, source_target_pairs={{0,16},{8,24},{16,0},{24,8},{1,17},{9,25},{17,1},{25,9},{2,18},{10... | collective-permute-start | bytes 393224 | tf_op jit(solution)/shard_map/ppermute | solution.py:487
  15.9 3.8 %copy.17.refs_2_.refs_5_.refs_3_ = bf16[3328,256]{1,0:T(8,128)(2,1)} copy(bf16[3328,256]{0,1:T(8,128)(2,1)} %bitcast.31) | data formatting | bytes 3407872 | tf_op jit(solution)/shard_map/transpose | solution.py:547
  24.0 10.5 %forward_part.4 = (bf16[4,2,3,128,1024]{4,3,2,1,0:T(8,128)(2,1)}, bf16[1,192,128]{2,1,0:T(8,128)(2,1)S(1)}) custom-call(bf16[384,3328]{1,0:T(8,128)(2,1)S(1)} %copy-done.3, bf16[3328,2048]{1,0:T(8,128)(2,1)} %refs_11_.3, bf16[3328,256]{1,0:T(8,128)(2,1)S(1)} %copy-done.6, bf16[4,3,128,256]{3,2,1,0:T(8,128)(2,1)S(1)} %copy-done.23), custom_call_target="tpu_custom_call" | custom-call | flops 20937965568 | tf_op jit(solution)/shard_map/forward_part/pallas_call | solution.py:328
  37.5 14.2 %collective-permute-done.6 = bf16[192,128]{1,0:T(8,128)(2,1)S(1)} collective-permute-done((bf16[192,128]{1,0:T(8,128)(2,1)S(1)}, bf16[192,128]{1,0:T(8,128)(2,1)S(1)}, u32[]{:S(2)}, u32[]{:S(2)}) %collective-permute-start.6) | collective-permute-done | bytes 49184 | tf_op jit(solution)/shard_map/ppermute | solution.py:487
  54.2 2.6 collective-permute-start.9
  56.9 11.4 %forward_part.5 = (bf16[4,2,3,128,1024]{4,3,2,1,0:T(8,128)(2,1)}, bf16[1,192,128]{2,1,0:T(8,128)(2,1)S(1)}) custom-call(bf16[384,3328]{1,0:T(8,128)(2,1)} %collective-permute-done.1.refs_0_.refs_5_, bf16[3328,2048]{1,0:T(8,128)(2,1)} %refs_11_.3, bf16[3328,256]{1,0:T(8,128)(2,1)S(1)} %copy-done.7, ...), custom_call_target="tpu_custom_call", output_to_operand_aliasing={{0}: (4, {})} | custom-call | flops 20937965568 | tf_op jit(solution)/shard_map/forward_part/pallas_call | solution.py:328
  68.4 4.8 %collective-permute-done.11 = bf16[192,128]{1,0:T(8,128)(2,1)S(1)} collective-permute-done((bf16[192,128]{1,0:T(8,128)(2,1)S(1)}, bf16[192,128]{1,0:T(8,128)(2,1)S(1)}, u32[]{:S(2)}, u32[]{:S(2)}) %collective-permute-start.11) | collective-permute-done | bytes 49184 | tf_op jit(solution)/shard_map/ppermute | solution.py:487
  73.2 6.8 %collective-permute-done.9.refs_1_.refs_7_ = bf16[160,3328]{1,0:T(8,128)(2,1)S(1)} collective-permute-done((bf16[160,3328]{1,0:T(8,128)(2,1)S(1)}, bf16[160,3328]{1,0:T(8,128)(2,1)S(1)}, u32[]{:S(2)}, u32[]{:S(2)}) %collective-permute-start.9) | collective-permute-done | bytes 1064992 | tf_op jit(solution)/shard_map/ppermute | solution.py:487
  83.9 12.6 %forward_part.6 = (bf16[4,2,3,128,1024]{4,3,2,1,0:T(8,128)(2,1)}, bf16[2,128,128]{2,1,0:T(8,128)(2,1)S(1)}) custom-call(bf16[96,3328]{1,0:T(8,128)(2,1)S(1)} %collective-permute-done.3.refs_0_.refs_6_, bf16[160,3328]{1,0:T(8,128)(2,1)S(1)} %collective-permute-done.9.refs_1_.refs_7_, ...), custom_call_target="tpu_custom_call", output_to_operand_aliasing={{0}: (7, {})} | custom-call | flops 27917287424 | tf_op jit(solution)/shard_map/forward_part/pallas_call | solution.py:328
  98.1 2.9 collective-permute-done.16
  107.3 9.1 %forward_part.7 = (bf16[4,2,3,128,1024]{4,3,2,1,0:T(8,128)(2,1)}, bf16[2,64,128]{2,1,0:T(8,128)(2,1)S(1)}) custom-call(bf16[128,3328]{1,0:T(8,128)(2,1)S(1)} %collective-permute-done.14.refs_0_.refs_8_, bf16[128,3328]{1,0:T(8,128)(2,1)S(1)} %collective-permute-done.19.refs_1_.refs_11_, bf16[3328,2048]{1,0:T(8,128)(2,1)} %refs_11_.3, ...), custom_call_target="tpu_custom_call", output_to_operand_aliasing={{0}: (5, {})} | custom-call | flops 13958643712 | tf_op jit(solution)/shard_map/forward_part/pallas_call | solution.py:328
  116.4 6.5 %collective-permute-done.17.refs_5_ = bf16[384,1024]{1,0:T(8,128)(2,1)S(1)} collective-permute-done((bf16[384,1024]{1,0:T(8,128)(2,1)S(1)}, bf16[384,1024]{1,0:T(8,128)(2,1)S(1)}, u32[]{:S(2)}, u32[]{:S(2)}) %collective-permute-start.17) | collective-permute-done | bytes 786464 | tf_op jit(solution)/shard_map/ppermute | solution.py:502
  125.3 2.8 copy-done
  132.7 2.3 collective-permute-done.28
  136.1 7.1 %collective-permute-done.25.ahead_ref = bf16[192,1024]{1,0:T(8,128)(2,1)S(1)} collective-permute-done((bf16[192,1024]{1,0:T(8,128)(2,1)S(1)}, bf16[192,1024]{1,0:T(8,128)(2,1)S(1)}, u32[]{:S(2)}, u32[]{:S(2)}) %collective-permute-start.25) | collective-permute-done | bytes 393248 | tf_op jit(solution)/shard_map/ppermute | solution.py:502
  148.9 20.8 %backward_part.3 = (bf16[384,3328]{1,0:T(8,128)(2,1)}, bf16[384,3328]{1,0:T(8,128)(2,1)}) custom-call(s32[2]{0:T(128)S(1)} %pad_add_fusion.at_ref, bf16[384,1024]{1,0:T(8,128)(2,1)} %collective-permute-done.refs_0_, bf16[384,1024]{1,0:T(8,128)(2,1)S(1)} %copy-done.51, bf16[384,1024]{1,0:T(8,128)(2,1)S(1)} %copy-done.53, bf16[384,1024]{1,0:T(8,128)(2,1)S(1)} %copy-done.55, ...), custom_call_target="tpu_custom_call" | custom-call | flops 41875931136 | tf_op jit(solution)/shard_map/backward_part/pallas_call | solution.py:412
  173.5 2.9 %collective-permute-done.34 = bf16[384,3328]{1,0:T(8,128)(2,1)S(1)} collective-permute-done((bf16[384,3328]{1,0:T(8,128)(2,1)}, bf16[384,3328]{1,0:T(8,128)(2,1)S(1)}, u32[]{:S(2)}, u32[]{:S(2)}) %collective-permute-start.34) | collective-permute-done | bytes 2555936 | tf_op jit(solution)/shard_map/ppermute | solution.py:487
  181.0 12.5 %backward_part.4 = bf16[384,3328]{1,0:T(8,128)(2,1)} custom-call(s32[2]{0:T(128)S(1)} %pad_add_fusion.at_ref, bf16[384,1024]{1,0:T(8,128)(2,1)} %collective-permute-done.refs_0_, bf16[384,1024]{1,0:T(8,128)(2,1)S(1)} %copy-done.51, bf16[384,1024]{1,0:T(8,128)(2,1)S(1)} %copy-done.53, bf16[384,1024]{1,0:T(8,128)(2,1)S(1)} %copy-done.55, ...), custom_call_target="tpu_custom_call" | custom-call | flops 20937965568 | tf_op jit(solution)/shard_map/backward_part/pallas_call | solution.py:412
  197.8 2.6 collective-permute-done.35.refs_1_
  205.9 2.8 add_convert_fusion
  212.5 13.3 %backward_part.5.own_ref = bf16[384,3328]{1,0:T(8,128)(2,1)} custom-call(s32[2]{0:T(128)S(1)} %pad_add_fusion.at_ref, bf16[384,1024]{1,0:T(8,128)(2,1)} %collective-permute-done.refs_0_, bf16[384,1024]{1,0:T(8,128)(2,1)S(1)} %copy-done.51, bf16[384,1024]{1,0:T(8,128)(2,1)S(1)} %copy-done.53, bf16[384,1024]{1,0:T(8,128)(2,1)S(1)} %copy-done.55, ...), custom_call_target="tpu_custom_call" | custom-call | flops 20937965568 | tf_op jit(solution)/shard_map/backward_part/pallas_call | solution.py:412
  225.8 9.0 %collective-permute-done.40.refs_1_ = bf16[160,3328]{1,0:T(8,128)(2,1)S(1)} collective-permute-done((bf16[160,3328]{1,0:T(8,128)(2,1)}, bf16[160,3328]{1,0:T(8,128)(2,1)S(1)}, u32[]{:S(2)}, u32[]{:S(2)}) %collective-permute-start.40) | collective-permute-done | bytes 1064992 | tf_op jit(solution)/shard_map/ppermute | solution.py:487
  235.8 2.9 last_add.1
  238.7 2.2 term_up.1
  242.1 7.4 %collective-permute-start.42 = (bf16[384,1024]{1,0:T(8,128)(2,1)}, bf16[384,1024]{1,0:T(8,128)(2,1)}, u32[]{:S(2)}, u32[]{:S(2)}) collective-permute-start(bf16[384,1024]{1,0:T(8,128)(2,1)} %last_add.1), channel_id=1, source_target_pairs={{0,0},{1,1},{2,8},{3,9},{4,16},{5,17},{6,24},{7,25},{8,2},{9,3},{1... | collective-permute-start | bytes 2359304 | tf_op jit(solution)/shard_map/ppermute | solution.py:495
  249.5 2.2 add_convert_fusion.3
  258.5 2.3 combine.4.refs_2_
  262.2 6.2 %factor_grad.1 = bf16[256,3328]{1,0:T(8,128)(2,1)} custom-call(bf16[4,3,128,256]{3,2,1,0:T(8,128)(2,1)S(1)} %copy-done.27, bf16[192,128]{1,0:T(8,128)(2,1)S(1)} %convert_add_fusion.4.refs_9_.refs_0_, bf16[192,128]{1,0:T(8,128)(2,1)S(1)} %copy-done.41, bf16[192,128]{1,0:T(8,128)(2,1)S(1)} %copy-done.43, bf16[192,128]{1,0:T(8,128)(2,1)S(1)} %copy-done.45, ...), custom_call_target="tpu_custom_call" | custom-call | tf_op jit(solution)/shard_map/factor_grad/pallas_call | solution.py:456
  268.4 16.1 %collective-permute-done.44.refs_2_ = bf16[64,1024]{1,0:T(8,128)(2,1)} collective-permute-done((bf16[64,1024]{1,0:T(8,128)(2,1)}, bf16[64,1024]{1,0:T(8,128)(2,1)}, u32[]{:S(2)}, u32[]{:S(2)}) %collective-permute-start.44) | collective-permute-done | bytes 131104 | tf_op jit(solution)/shard_map/ppermute | solution.py:487
  285.8 2.8 up_grad.1
  288.6 2.3 add_convert_fusion.2
  290.9 2.9 combine.5
  (243 shorter events, 78.0 us)
Async XLA Ops:
  0.6 51.4 %collective-permute-start.1 = (bf16[384,3328]{1,0:T(8,128)(2,1)}, bf16[384,3328]{1,0:T(8,128)(2,1)}, u32[]{:S(2)}, u32[]{:S(2)}) collective-permute-start(bf16[384,3328]{1,0:T(8,128)(2,1)} %refs_4_.2), channel_id=1, source_target_pairs={{0,8},{8,0},{16,24},{24,16},{1,9},{9,1},{17,25},{25,17},{2,10},{10... | collective-permute-start | bytes 7667720 | tf_op jit(solution)/shard_map/ppermute | solution.py:487
  7.6 44.5 %collective-permute-start = (bf16[384,1024]{1,0:T(8,128)(2,1)S(1)}, bf16[384,1024]{1,0:T(8,128)(2,1)}, u32[]{:S(2)}, u32[]{:S(2)}) collective-permute-start(bf16[384,1024]{1,0:T(8,128)(2,1)S(1)} %mask.1.grad_ref), channel_id=1, source_target_pairs={{0,0},{1,1},{2,8},{3,9},{4,16},{5,17},{6,24},{7,25},{8,2},{9,3},{1... | collective-permute-start | bytes 2359304 | tf_op jit(solution)/shard_map/ppermute | solution.py:495
  9.1 25.5 %collective-permute-start.4 = (bf16[64,1024]{1,0:T(8,128)(2,1)}, bf16[64,1024]{1,0:T(8,128)(2,1)}, u32[]{:S(2)}, u32[]{:S(2)}) collective-permute-start(bf16[64,1024]{1,0:T(8,128)(2,1)} %get-tuple-element.187), channel_id=1, source_target_pairs={{0,16},{8,24},{16,0},{24,8},{1,17},{9,25},{17,1},{25,9},{2,18},{10... | collective-permute-start | bytes 393224 | tf_op jit(solution)/shard_map/ppermute | solution.py:487
  15.1 19.5 %collective-permute-start.5 = (bf16[64,1024]{1,0:T(8,128)(2,1)}, bf16[64,1024]{1,0:T(8,128)(2,1)}, u32[]{:S(2)}, u32[]{:S(2)}) collective-permute-start(bf16[64,1024]{1,0:T(8,128)(2,1)} %get-tuple-element.188), channel_id=1, source_target_pairs={{0,24},{8,16},{16,8},{24,0},{1,25},{9,17},{17,9},{25,1},{2,26},{10... | collective-permute-start | bytes 393224 | tf_op jit(solution)/shard_map/ppermute | solution.py:487
  19.7 32.4 %collective-permute-start.3 = (bf16[96,3328]{1,0:T(8,128)(2,1)S(1)}, bf16[96,3328]{1,0:T(8,128)(2,1)S(1)}, u32[]{:S(2)}, u32[]{:S(2)}) collective-permute-start(bf16[96,3328]{1,0:T(8,128)(2,1)S(1)} %slice.51), channel_id=1, source_target_pairs={{0,16},{8,24},{16,0},{24,8},{1,17},{9,25},{17,1},{25,9},{2,18},{10... | collective-permute-start | bytes 1916936 | tf_op jit(solution)/shard_map/ppermute | solution.py:487
  52.1 21.1 %collective-permute-start.7 = (bf16[384,1024]{1,0:T(8,128)(2,1)}, bf16[384,1024]{1,0:T(8,128)(2,1)S(1)}, u32[]{:S(2)}, u32[]{:S(2)}) collective-permute-start(bf16[384,1024]{1,0:T(8,128)(2,1)} %collective-permute-done.refs_0_), channel_id=1, source_target_pairs={{0,2},{2,4},{4,6},{6,7},{7,5},{5,3},{3,1},{1,0},{8,10},{10,12},{12... | collective-permute-start | bytes 2359304 | tf_op jit(solution)/shard_map/ppermute | solution.py:502
  52.1 21.1 %collective-permute-start.8 = (bf16[384,1024]{1,0:T(8,128)(2,1)}, bf16[384,1024]{1,0:T(8,128)(2,1)S(1)}, u32[]{:S(2)}, u32[]{:S(2)}) collective-permute-start(bf16[384,1024]{1,0:T(8,128)(2,1)} %collective-permute-done.refs_0_), channel_id=1, source_target_pairs={{2,0},{4,2},{6,4},{7,6},{5,7},{3,5},{1,3},{0,1},{10,8},{12,10},{14... | collective-permute-start | bytes 2359304 | tf_op jit(solution)/shard_map/ppermute | solution.py:505
  54.2 25.8 %collective-permute-start.9 = (bf16[160,3328]{1,0:T(8,128)(2,1)S(1)}, bf16[160,3328]{1,0:T(8,128)(2,1)S(1)}, u32[]{:S(2)}, u32[]{:S(2)}) collective-permute-start(bf16[160,3328]{1,0:T(8,128)(2,1)S(1)} %slice.52), channel_id=1, source_target_pairs={{0,16},{8,24},{16,0},{24,8},{1,17},{9,25},{17,1},{25,9},{2,18},{10... | collective-permute-start | bytes 3194888 | tf_op jit(solution)/shard_map/ppermute | solution.py:487
  56.8 16.4 %collective-permute-start.10 = (bf16[96,3328]{1,0:T(8,128)(2,1)S(1)}, bf16[96,3328]{1,0:T(8,128)(2,1)S(1)}, u32[]{:S(2)}, u32[]{:S(2)}) collective-permute-start(bf16[96,3328]{1,0:T(8,128)(2,1)S(1)} %collective-permute-done.3.refs_0_.refs_6_), channel_id=1, source_target_pairs={{0,8},{8,0},{16,24},{24,16},{1,9},{9,1},{17,25},{25,17},{2,10},{10... | collective-permute-start | bytes 1916936 | tf_op jit(solution)/shard_map/ppermute | solution.py:487
  56.8 16.4 %collective-permute-start.11 = (bf16[192,128]{1,0:T(8,128)(2,1)S(1)}, bf16[192,128]{1,0:T(8,128)(2,1)S(1)}, u32[]{:S(2)}, u32[]{:S(2)}) collective-permute-start(bf16[192,128]{1,0:T(8,128)(2,1)S(1)} %convert_element_type.92), channel_id=1, source_target_pairs={{0,2},{1,3},{2,0},{3,1},{4,6},{5,7},{6,4},{7,5},{8,10},{9,11},{10,... | collective-permute-start | bytes 147464 | tf_op jit(solution)/shard_map/ppermute | solution.py:487
  80.0 21.0 %collective-permute-start.12 = (bf16[384,1024]{1,0:T(8,128)(2,1)S(1)}, bf16[384,1024]{1,0:T(8,128)(2,1)S(1)}, u32[]{:S(2)}, u32[]{:S(2)}) collective-permute-start(bf16[384,1024]{1,0:T(8,128)(2,1)S(1)} %collective-permute-done.7.refs_1_), channel_id=1, source_target_pairs={{0,2},{2,4},{4,6},{6,7},{7,5},{5,3},{3,1},{1,0},{8,10},{10,12},{12... | collective-permute-start | bytes 2359304 | tf_op jit(solution)/shard_map/ppermute | solution.py:502
  80.4 20.7 %collective-permute-start.13 = (bf16[384,1024]{1,0:T(8,128)(2,1)S(1)}, bf16[384,1024]{1,0:T(8,128)(2,1)S(1)}, u32[]{:S(2)}, u32[]{:S(2)}) collective-permute-start(bf16[384,1024]{1,0:T(8,128)(2,1)S(1)} %collective-permute-done.8.refs_2_), channel_id=1, source_target_pairs={{2,0},{4,2},{6,4},{7,6},{5,7},{3,5},{1,3},{0,1},{10,8},{12,10},{14... | collective-permute-start | bytes 2359304 | tf_op jit(solution)/shard_map/ppermute | solution.py:505
  82.1 20.9 %collective-permute-start.14 = (bf16[128,3328]{1,0:T(8,128)(2,1)S(1)}, bf16[128,3328]{1,0:T(8,128)(2,1)S(1)}, u32[]{:S(2)}, u32[]{:S(2)}) collective-permute-start(bf16[128,3328]{1,0:T(8,128)(2,1)S(1)} %slice.53), channel_id=1, source_target_pairs={{0,16},{8,24},{16,0},{24,8},{1,17},{9,25},{17,1},{25,9},{2,18},{10... | collective-permute-start | bytes 2555912 | tf_op jit(solution)/shard_map/ppermute | solution.py:487
  103.0 20.0 %collective-permute-start.17 = (bf16[384,1024]{1,0:T(8,128)(2,1)S(1)}, bf16[384,1024]{1,0:T(8,128)(2,1)S(1)}, u32[]{:S(2)}, u32[]{:S(2)}) collective-permute-start(bf16[384,1024]{1,0:T(8,128)(2,1)S(1)} %collective-permute-done.12.refs_3_), channel_id=1, source_target_pairs={{0,2},{2,4},{4,6},{6,7},{7,5},{5,3},{3,1},{1,0},{8,10},{10,12},{12... | collective-permute-start | bytes 2359304 | tf_op jit(solution)/shard_map/ppermute | solution.py:502
  103.4 19.6 %collective-permute-start.18 = (bf16[384,1024]{1,0:T(8,128)(2,1)S(1)}, bf16[384,1024]{1,0:T(8,128)(2,1)S(1)}, u32[]{:S(2)}, u32[]{:S(2)}) collective-permute-start(bf16[384,1024]{1,0:T(8,128)(2,1)S(1)} %collective-permute-done.13.refs_4_), channel_id=1, source_target_pairs={{2,0},{4,2},{6,4},{7,6},{5,7},{3,5},{1,3},{0,1},{10,8},{12,10},{14... | collective-permute-start | bytes 2359304 | tf_op jit(solution)/shard_map/ppermute | solution.py:505
  105.3 17.7 %collective-permute-start.20 = (bf16[192,128]{1,0:T(8,128)(2,1)S(1)}, bf16[192,128]{1,0:T(8,128)(2,1)S(1)}, u32[]{:S(2)}, u32[]{:S(2)}) collective-permute-start(bf16[192,128]{1,0:T(8,128)(2,1)S(1)} %convert_add_fusion.4.refs_9_.refs_0_), channel_id=1, source_target_pairs={{0,8},{8,0},{16,24},{24,16},{1,9},{9,1},{17,25},{25,17},{2,10},{10... | collective-permute-start | bytes 147464 | tf_op jit(solution)/shard_map/ppermute | solution.py:487
  105.5 17.5 %collective-permute-start.21 = (bf16[192,128]{1,0:T(8,128)(2,1)S(1)}, bf16[192,128]{1,0:T(8,128)(2,1)S(1)}, u32[]{:S(2)}, u32[]{:S(2)}) collective-permute-start(bf16[192,128]{1,0:T(8,128)(2,1)S(1)} %convert_add_fusion.4.refs_9_.refs_0_), channel_id=1, source_target_pairs={{0,16},{8,24},{16,0},{24,8},{1,17},{9,25},{17,1},{25,9},{2,18},{10... | collective-permute-start | bytes 147464 | tf_op jit(solution)/shard_map/ppermute | solution.py:487
  144.7 25.1 %collective-permute-start.29 = (bf16[384,1024]{1,0:T(8,128)(2,1)S(1)}, bf16[384,1024]{1,0:T(8,128)(2,1)S(1)}, u32[]{:S(2)}, u32[]{:S(2)}) collective-permute-start(bf16[384,1024]{1,0:T(8,128)(2,1)S(1)} %get-tuple-element.253), channel_id=1, source_target_pairs={{0,2},{2,4},{4,6},{6,7},{7,5},{5,3},{3,1},{1,0},{8,10},{10,12},{12... | collective-permute-start | bytes 2359304 | tf_op jit(solution)/shard_map/ppermute | solution.py:502
  145.9 23.9 %collective-permute-start.30 = (bf16[384,1024]{1,0:T(8,128)(2,1)S(1)}, bf16[384,1024]{1,0:T(8,128)(2,1)S(1)}, u32[]{:S(2)}, u32[]{:S(2)}) collective-permute-start(bf16[384,1024]{1,0:T(8,128)(2,1)S(1)} %get-tuple-element.254), channel_id=1, source_target_pairs={{2,0},{4,2},{6,4},{7,6},{5,7},{3,5},{1,3},{0,1},{10,8},{12,10},{14... | collective-permute-start | bytes 2359304 | tf_op jit(solution)/shard_map/ppermute | solution.py:505
  146.8 23.0 %collective-permute-start.31 = (bf16[192,128]{1,0:T(8,128)(2,1)S(1)}, bf16[192,128]{1,0:T(8,128)(2,1)S(1)}, u32[]{:S(2)}, u32[]{:S(2)}) collective-permute-start(bf16[192,128]{1,0:T(8,128)(2,1)S(1)} %convert_element_type.103), channel_id=1, source_target_pairs={{0,4},{1,5},{2,6},{3,7},{4,0},{5,1},{6,2},{7,3},{8,12},{9,13},{10,... | collective-permute-start | bytes 147464 | tf_op jit(solution)/shard_map/ppermute | solution.py:487
  171.5 26.3 %collective-permute-start.32 = (bf16[384,1024]{1,0:T(8,128)(2,1)S(1)}, bf16[384,1024]{1,0:T(8,128)(2,1)S(1)}, u32[]{:S(2)}, u32[]{:S(2)}) collective-permute-start(bf16[384,1024]{1,0:T(8,128)(2,1)S(1)} %get-tuple-element.274), channel_id=1, source_target_pairs={{0,2},{2,4},{4,6},{6,7},{7,5},{5,3},{3,1},{1,0},{8,10},{10,12},{12... | collective-permute-start | bytes 2359304 | tf_op jit(solution)/shard_map/ppermute | solution.py:502
  172.5 25.3 %collective-permute-start.33 = (bf16[384,1024]{1,0:T(8,128)(2,1)}, bf16[384,1024]{1,0:T(8,128)(2,1)S(1)}, u32[]{:S(2)}, u32[]{:S(2)}) collective-permute-start(bf16[384,1024]{1,0:T(8,128)(2,1)} %get-tuple-element.275), channel_id=1, source_target_pairs={{2,0},{4,2},{6,4},{7,6},{5,7},{3,5},{1,3},{0,1},{10,8},{12,10},{14... | collective-permute-start | bytes 2359304 | tf_op jit(solution)/shard_map/ppermute | solution.py:505
  179.3 21.1 %collective-permute-start.35 = (bf16[128,3328]{1,0:T(8,128)(2,1)S(1)}, bf16[128,3328]{1,0:T(8,128)(2,1)S(1)}, u32[]{:S(2)}, u32[]{:S(2)}) collective-permute-start(bf16[128,3328]{1,0:T(8,128)(2,1)S(1)} %add_convert_fusion.1), channel_id=1, source_target_pairs={{0,16},{8,24},{16,0},{24,8},{1,17},{9,25},{17,1},{25,9},{2,18},{10... | collective-permute-start | bytes 2555912 | tf_op jit(solution)/shard_map/ppermute | solution.py:487
  203.2 22.6 %collective-permute-start.37 = (bf16[384,1024]{1,0:T(8,128)(2,1)}, bf16[384,1024]{1,0:T(8,128)(2,1)}, u32[]{:S(2)}, u32[]{:S(2)}) collective-permute-start(bf16[384,1024]{1,0:T(8,128)(2,1)} %get-tuple-element.302), channel_id=1, source_target_pairs={{0,2},{2,4},{4,6},{6,7},{7,5},{5,3},{3,1},{1,0},{8,10},{10,12},{12... | collective-permute-start | bytes 2359304 | tf_op jit(solution)/shard_map/ppermute | solution.py:502
  204.4 21.4 %collective-permute-start.38 = (bf16[384,1024]{1,0:T(8,128)(2,1)}, bf16[384,1024]{1,0:T(8,128)(2,1)}, u32[]{:S(2)}, u32[]{:S(2)}) collective-permute-start(bf16[384,1024]{1,0:T(8,128)(2,1)} %get-tuple-element.303), channel_id=1, source_target_pairs={{2,0},{4,2},{6,4},{7,6},{5,7},{3,5},{1,3},{0,1},{10,8},{12,10},{14... | collective-permute-start | bytes 2359304 | tf_op jit(solution)/shard_map/ppermute | solution.py:505
  205.9 29.9 %collective-permute-start.39 = (bf16[384,3328]{1,0:T(8,128)(2,1)}, bf16[384,3328]{1,0:T(8,128)(2,1)S(1)}, u32[]{:S(2)}, u32[]{:S(2)}) collective-permute-start(bf16[384,3328]{1,0:T(8,128)(2,1)} %backward_part.4), channel_id=1, source_target_pairs={{0,8},{8,0},{16,24},{24,16},{1,9},{9,1},{17,25},{25,17},{2,10},{10... | collective-permute-start | bytes 7667720 | tf_op jit(solution)/shard_map/ppermute | solution.py:487
  208.7 26.1 %collective-permute-start.40 = (bf16[160,3328]{1,0:T(8,128)(2,1)}, bf16[160,3328]{1,0:T(8,128)(2,1)S(1)}, u32[]{:S(2)}, u32[]{:S(2)}) collective-permute-start(bf16[160,3328]{1,0:T(8,128)(2,1)} %add_convert_fusion), channel_id=1, source_target_pairs={{0,16},{8,24},{16,0},{24,8},{1,17},{9,25},{17,1},{25,9},{2,18},{10... | collective-permute-start | bytes 3194888 | tf_op jit(solution)/shard_map/ppermute | solution.py:487
  242.1 43.8 %collective-permute-start.42 = (bf16[384,1024]{1,0:T(8,128)(2,1)}, bf16[384,1024]{1,0:T(8,128)(2,1)}, u32[]{:S(2)}, u32[]{:S(2)}) collective-permute-start(bf16[384,1024]{1,0:T(8,128)(2,1)} %last_add.1), channel_id=1, source_target_pairs={{0,0},{1,1},{2,8},{3,9},{4,16},{5,17},{6,24},{7,25},{8,2},{9,3},{1... | collective-permute-start | bytes 2359304 | tf_op jit(solution)/shard_map/ppermute | solution.py:495
  251.7 39.2 %collective-permute-start.46 = (bf16[96,3328]{1,0:T(8,128)(2,1)}, bf16[96,3328]{1,0:T(8,128)(2,1)}, u32[]{:S(2)}, u32[]{:S(2)}) collective-permute-start(bf16[96,3328]{1,0:T(8,128)(2,1)} %add_convert_fusion.3), channel_id=1, source_target_pairs={{0,16},{8,24},{16,0},{24,8},{1,17},{9,25},{17,1},{25,9},{2,18},{10... | collective-permute-start | bytes 1916936 | tf_op jit(solution)/shard_map/ppermute | solution.py:487
  251.7 16.7 %collective-permute-start.43 = (bf16[64,1024]{1,0:T(8,128)(2,1)}, bf16[64,1024]{1,0:T(8,128)(2,1)}, u32[]{:S(2)}, u32[]{:S(2)}) collective-permute-start(bf16[64,1024]{1,0:T(8,128)(2,1)} %get-tuple-element.331), channel_id=1, source_target_pairs={{0,8},{8,0},{16,24},{24,16},{1,9},{9,1},{17,25},{25,17},{2,10},{10... | collective-permute-start | bytes 393224 | tf_op jit(solution)/shard_map/ppermute | solution.py:487
  251.7 32.7 %collective-permute-start.44 = (bf16[64,1024]{1,0:T(8,128)(2,1)}, bf16[64,1024]{1,0:T(8,128)(2,1)}, u32[]{:S(2)}, u32[]{:S(2)}) collective-permute-start(bf16[64,1024]{1,0:T(8,128)(2,1)} %get-tuple-element.332), channel_id=1, source_target_pairs={{0,16},{8,24},{16,0},{24,8},{1,17},{9,25},{17,1},{25,9},{2,18},{10... | collective-permute-start | bytes 393224 | tf_op jit(solution)/shard_map/ppermute | solution.py:487
  253.7 32.1 %collective-permute-start.45 = (bf16[64,1024]{1,0:T(8,128)(2,1)}, bf16[64,1024]{1,0:T(8,128)(2,1)}, u32[]{:S(2)}, u32[]{:S(2)}) collective-permute-start(bf16[64,1024]{1,0:T(8,128)(2,1)} %get-tuple-element.333), channel_id=1, source_target_pairs={{0,24},{8,16},{16,8},{24,0},{1,25},{9,17},{17,9},{25,1},{2,26},{10... | collective-permute-start | bytes 393224 | tf_op jit(solution)/shard_map/ppermute | solution.py:487
  (80 other events, 983.0 us)

commit v4 on v3

--- a/solution.py
+++ b/solution.py
@@ -8,7 +8,7 @@
 from jax.sharding import PartitionSpec as P
 
 BLK = 128
-SCALE = 8
+LOW, HIGH = 2, 8
 F32 = jnp.float32
 BF16 = jnp.bfloat16
 VMEM_LIMIT = 44 * 1024 * 1024
@@ -246,7 +246,7 @@
 
 def combine(start, own, near, arrived, out):
     rows, units = own.shape
-    tile = 32
+    tile = 48
     first = start // tile
     placed = pl.BlockSpec((tile, units), lambda i: (i + first, 0))
     piece = pl.BlockSpec((tile, units), lambda i: (i, 0))
@@ -341,7 +341,7 @@
             jax.ShapeDtypeStruct(turned, BF16),
         ],
         input_output_aliases=aliases,
-        cost_estimate=cost(SCALE * groups[1] * blocks[1] * BLK * units * cols),
+        cost_estimate=cost(LOW * groups[1] * blocks[1] * BLK * units * cols),
         compiler_params=params(),
         name="forward_part",
     )(*operands)
@@ -363,81 +363,81 @@
     return jnp.where(mask.reshape(wide.shape) > 0, wide, 0.0).astype(BF16)
 
 
-def backward_kernel(groups, n_mp, offsets, at_ref, *refs):
-    first, count = groups
+def backward_kernel(group, n_mp, offsets, more, at_ref, *refs):
     slots = len(offsets)
     block_refs = refs[: slots + 1]
-    act_refs = refs[slots + 1 : slots + 1 + count]
-    m_ref, w_ref, a_ref = refs[slots + 1 + count : slots + 4 + count]
-    z_refs = refs[slots + 4 + count : -3]
+    act_ref, m_ref, w_ref, a_ref = refs[slots + 1 : slots + 5]
+    z_refs = refs[slots + 5 + more : -3]
     g_ref, u_ref, sems = refs[-3:]
-    _, q, rows, _ = g_ref.shape
+    q, rows, _ = g_ref.shape
     n_dp = n_mp // q
     top = rows // 2
 
     def transfers(act):
         for index in range(slots + 1):
             there, part = ring_slot(offsets[min(index, slots - 1)], at_ref, n_dp, n_mp)
-            target = g_ref.at[there % count, part]
+            target = g_ref.at[part]
             if index >= slots - 1:
                 target = target.at[pl.ds(top * (index - slots + 1), top)]
             copy = pltpu.make_async_copy(block_refs[index], target, sems.at[index])
-            pl.when(there // count == first // count)(copy.start if act else copy.wait)
+            pl.when(there == group)(copy.start if act else copy.wait)
 
     @pl.when(pl.program_id(0) == 0)
     def _():
         transfers(True)
-        for g in range(count):
-            u_ref[g * rows : (g + 1) * rows, :] = spread(act_refs[g][...], m_ref[g])
+        u_ref[...] = spread(act_ref[...], m_ref[0])
         transfers(False)
 
-    grads = [
-        jnp.concatenate([g_ref[g, h] for h in range(q)], axis=1) for g in range(count)
-    ]
     out = lax.dot_general(
-        jnp.concatenate(grads, axis=0), w_ref[...], TURNED, preferred_element_type=F32
+        jnp.concatenate([g_ref[h] for h in range(q)], axis=1),
+        w_ref[...],
+        TURNED,
+        preferred_element_type=F32,
     )
     out += jnp.dot(u_ref[...], a_ref[...], preferred_element_type=F32)
-    for g in range(count):
-        z_refs[g][...] = out[g * rows : (g + 1) * rows].astype(z_refs[g].dtype)
-
-
-def backward_part(groups, at, blocks, offsets, acts, masks, weight, turned_factor, n_mp):
+    for ref in refs[slots + 5 : slots + 5 + more]:
+        out += ref[...].astype(F32)
+    start = 0
+    for z_ref in z_refs:
+        size = z_ref.shape[0]
+        z_ref[...] = out[start : start + size].astype(BF16)
+        start += size
+
+
+def backward_part(
+    group, at, blocks, offsets, act, masks, weight, turned_factor, n_mp, others, pieces
+):
     units, cols = weight.shape
     n_dp, parts, _, ranks = masks.shape
     rows = parts * BLK
     q = n_mp // n_dp
-    first, count = groups
     tile = min(896, units)
-    return pl.pallas_call(
-        functools.partial(backward_kernel, groups, n_mp, offsets),
+    columns = lambda i, at_ref: (0, i)
+    return pl.pallas_call(
+        functools.partial(backward_kernel, group, n_mp, offsets, len(others)),
         grid_spec=pltpu.PrefetchScalarGridSpec(
             num_scalar_prefetch=1,
             grid=(pl.cdiv(units, tile),),
             in_specs=[pl.BlockSpec(memory_space=pl.ANY)] * len(blocks)
-            + [whole(act.shape) for act in acts]
             + [
-                pl.BlockSpec(
-                    (count, parts, BLK, ranks), lambda i, at_ref: (first // count, 0, 0, 0)
-                ),
+                whole(act.shape),
+                pl.BlockSpec((1, parts, BLK, ranks), lambda i, at_ref: (group, 0, 0, 0)),
                 pl.BlockSpec((tile, cols), lambda i, at_ref: (i, 0)),
-                pl.BlockSpec((ranks, tile), lambda i, at_ref: (0, i)),
-            ],
-            out_specs=[pl.BlockSpec((rows, tile), lambda i, at_ref: (0, i))] * count,
+                pl.BlockSpec((ranks, tile), columns),
+            ]
+            + [pl.BlockSpec((rows, tile), columns)] * len(others),
+            out_specs=[pl.BlockSpec((size, tile), columns) for size in pieces],
             scratch_shapes=[
-                pltpu.VMEM((count, q, rows, cols // q), BF16),
-                pltpu.VMEM((count * rows, ranks), BF16),
+                pltpu.VMEM((q, rows, cols // q), BF16),
+                pltpu.VMEM((rows, ranks), BF16),
                 pltpu.SemaphoreType.DMA((len(blocks),)),
             ],
         ),
-        out_shape=[
-            jax.ShapeDtypeStruct((rows, units), BF16)
-        ]
-        * count,
-        cost_estimate=cost(SCALE * count * rows * units * cols),
+        out_shape=[jax.ShapeDtypeStruct((size, units), BF16) for size in pieces],
+        cost_estimate=cost((HIGH if others else LOW) * rows * units * cols),
         compiler_params=params(),
         name="backward_part",
-    )(at, *blocks, *acts, masks, weight, turned_factor)
+    )(at, *blocks, act, masks, weight, turned_factor, *others)
 
 
 def factor_grad_kernel(n_dp, m_ref, *refs):
@@ -487,12 +487,32 @@
         return lax.ppermute(value, axis, [(i, i ^ bit) for i in range(count)])
 
     def swap_places(value):
-        pairs = [
-            (j * n_mp + m, (m // q) * n_mp + j * q + m % q)
-            for j in range(n_dp)
-            for m in range(n_mp)
-        ]
-        return lax.ppermute(value, ("dp", "mp"), pairs)
+        index = lambda j, m: j * n_mp + m
+        near_pairs, far = [], []
+        for j in range(n_dp):
+            for m in range(n_mp):
+                c, h = m // q, m % q
+                if c // 2 == j // 2 or n_dp != 4:
+                    near_pairs.append((index(j, m), index(c, j * q + h)))
+                else:
+                    far.append((j, c, h))
+        swapped = lax.ppermute(value, ("dp", "mp"), near_pairs)
+        if far:
+            routes = (
+                lambda j, c, h: index(j ^ 2, c * q + h),
+                lambda j, c, h: index(c ^ 2, j * q + h),
+            )
+            halves = []
+            for route, half_rows in zip(routes, (value[:top], value[top:])):
+                first = [(index(j, c * q + h), route(j, c, h)) for j, c, h in far]
+                second = [(route(j, c, h), index(c, j * q + h)) for j, c, h in far]
+                halves.append(
+                    lax.ppermute(
+                        lax.ppermute(half_rows, ("dp", "mp"), first), ("dp", "mp"), second
+                    )
+                )
+            swapped = swapped + jnp.concatenate(halves, axis=0)
+        return swapped
 
     ring = list(range(0, n_mp, 2)) + list(range(n_mp - 1, 0, -2))
     up_ring = [(ring[i], ring[(i + 1) % n_mp]) for i in range(n_mp)]
@@ -505,7 +525,7 @@
         return lax.ppermute(value, "mp", down_ring)
 
     evens = range(2, n_dp, 2)
-    cuts = [0, rows // 4, 2 * rows // 3, rows]
+    cuts = list(range(0, rows + 1, BLK))
 
     def fetch(hidden, piece):
         held = {0: hidden[cuts[piece] : cuts[piece + 1]]}
@@ -541,18 +561,29 @@
         [like((rank, width), BF16)] * n_dp + [like((n_dp, blocks, BLK, owned * rank), BF16)],
     )
     arrived_up = [exchange(chosen[r], r) if r else chosen[0] for r in range(n_dp)]
-    arrived_up[1], hidden_0 = fence(arrived_up[1], hidden)
-    fetched = [fetch(hidden_0, 0)]
     turned_factor = jnp.transpose(adapter_down, (0, 2, 1)).reshape(owned * rank, units)
     factor = turned_factor.T
+    swapped, near, arrived_up, factor, masks, hidden = fence(
+        swapped, near, arrived_up, factor, masks, hidden
+    )
 
     def forward(groups, span, hids, total):
         return forward_part(groups, span, hids, down_weight, factor, masks, total, q, rank)
 
+    def forward_pairs(span, piece, total):
+        for r in evens:
+            hids = [fetched[p][r] for p in piece] + [passed[p][r + 1] for p in piece]
+            total, pair = forward((r, 2), span, hids, total)
+            for g in range(2):
+                picked.setdefault(r + g, []).append(pair[g])
+        return total
+
+    offsets = [0] + [sign * step for step in range(1, half) for sign in (-1, 1)] + [half]
+    ahead = behind = swapped
+    ring_blocks = [swapped]
     picked = {}
-    total, own = forward((0, 1), (0, blocks), [hidden], None)
-    picked[0] = [own[0]]
-    arrived_up, total, hidden = fence(arrived_up, total, hidden)
+    ahead, behind = onward(ahead), backward_on(behind)
+    fetched = [fetch(hidden, 0)]
     up_sum, block_up = call(
         functools.partial(up_kernel, n_dp, owned),
         "up_part",
@@ -560,14 +591,14 @@
         [masked_grad, *arrived_up],
         [like((blocks * rank, BLK), F32), like((blocks, rank, width), BF16)],
     )
+    up_sum, hidden = fence(up_sum, hidden)
     up_sum = sum_step(up_sum, 0)
-    swapped, near, fetched[0], total, up_sum, hidden = fence(
-        swapped, near, fetched[0], total, up_sum, hidden
-    )
-
-    ahead = behind = swapped
-    ring_blocks = [swapped]
-    offsets = [0] + [sign * step for step in range(1, half) for sign in (-1, 1)] + [half]
+    total, own = forward((0, 1), (0, blocks), [hidden], None)
+    picked[0] = [own[0]]
+    ahead, behind, fetched[0], total, up_sum, hidden = fence(
+        ahead, behind, fetched[0], total, up_sum, hidden
+    )
+    ring_blocks += [ahead, behind]
     ahead, behind = onward(ahead), backward_on(behind)
     fetched.append(fetch(hidden, 1))
     passed = [pass_on(fetched[0])]
@@ -578,38 +609,66 @@
         ahead, behind, fetched[1], passed, total, up_sum, hidden
     )
     ring_blocks += [ahead, behind]
-    ahead, behind = onward(ahead), backward_on(behind)
+    for _ in range(3, half):
+        ahead, behind = onward(ahead), backward_on(behind)
+        ring_blocks += [ahead, behind]
     fetched.append(fetch(hidden, 2))
     passed.append(pass_on(fetched[1]))
-
-    def forward_pairs(span, pieces, total):
-        for r in evens:
-            hids = [fetched[p][r] for p in pieces] + [passed[p][r + 1] for p in pieces]
-            total, pair = forward((r, 2), span, hids, total)
-            for g in range(2):
-                picked.setdefault(r + g, []).append(pair[g])
-        return total
-
     total = forward_pairs((0, 2), (0, 1), total)
     total, up_sum = fence(total, up_sum)
     up_sum = sum_step(up_sum, 2)
-    ahead, behind, fetched[2], passed, total, up_sum = fence(
-        ahead, behind, fetched[2], passed, total, up_sum
-    )
-    ring_blocks += [ahead, behind]
-    for _ in range(3, half):
-        ahead, behind = onward(ahead), backward_on(behind)
-        ring_blocks += [ahead, behind]
+    ahead, behind, fetched[2], passed, total, up_act = fence(
+        ahead, behind, fetched[2], passed, total, up_sum.astype(BF16)
+    )
+    ring_blocks[-2:] = [ahead, behind]
+    last = [onward(ahead[:top]), backward_on(behind[top:])]
     passed.append(pass_on(fetched[2]))
-    passed, up_act = fence(passed, up_sum.astype(BF16))
+    passed, up_act = fence(passed, up_act)
     acts = [exchange(up_act, r) if r else up_act for r in range(n_dp)]
     total = forward_pairs((2, 1), (2,), total)
-    ahead, behind, acts, total, picked = fence(ahead, behind, acts, total, picked)
-    ring_blocks[-2:] = [ahead, behind]
+    last, acts, total, picked = fence(last, acts, total, picked)
+    ring_blocks += last
     total = total.reshape(n_dp, q, rows, width)
 
-    last = [onward(ahead[:top]), backward_on(behind[top:])]
+    def backward(group, acts, others=(), pieces=(rows,)):
+        return backward_part(
+            group,
+            at,
+            ring_blocks,
+            offsets,
+            acts[group],
+            masks,
+            down_weight,
+            turned_factor,
+            n_mp,
+            others,
+            pieces,
+        )
+
+    def add_and_send(step, ahead, behind, *others, halves=False):
+        ahead, behind = ring_add(step, at, total, ahead, behind, n_mp, halves)
+        ahead, behind, *others = fence(ahead, behind, *others)
+        return onward(ahead), backward_on(behind), *others
+
+    ends = [0, 3 * rows // 8, 3 * rows // 4, rows]
+    pieces = [b - a for a, b in zip(ends, ends[1:])]
+
+    def partial_gradient(piece):
+        held = {r: parts[r][piece] for r in evens}
+        sent = []
+        bit = n_dp // 2
+        while bit > 1:
+            for r in [r for r in held if r & bit]:
+                value = exchange(held.pop(r), bit)
+                if r == bit:
+                    sent.append(value)
+                else:
+                    held[r ^ bit] = held[r ^ bit] + value
+            bit //= 2
+        return sent
+
     ahead, behind = opposite(at, total, n_mp)
+    ahead, behind, acts = fence(ahead, behind, acts)
     ahead, behind = onward(ahead), backward_on(behind)
     held = {r: jnp.concatenate(picked[r], axis=0) for r in range(n_dp)}
     bit = 1
@@ -622,70 +681,31 @@
             held[r ^ bit] = held[r ^ bit].astype(F32) + piece.astype(F32)
         bit *= 2
     down_sum = held[0]
-    last, ahead, behind, down_sum, acts = fence(last, ahead, behind, down_sum, acts)
-    ring_blocks += last
-
-    def backward(first, count, acts):
-        return backward_part(
-            (first, count),
-            at,
-            ring_blocks,
-            offsets,
-            acts[first : first + count],
-            masks,
-            down_weight,
-            turned_factor,
-            n_mp,
-        )
-
-    def add_and_send(step, ahead, behind, *others, halves=False):
-        ahead, behind = ring_add(step, at, total, ahead, behind, n_mp, halves)
-        ahead, behind, *others = fence(ahead, behind, *others)
-        return onward(ahead), backward_on(behind), *others
-
-    ends = [0, rows // 3, 3 * rows // 4, rows]
-
-    def partial_gradient(piece):
-        cut = slice(ends[piece], ends[piece + 1])
-        held = {
-            r: (parts[r][cut].astype(F32) + parts[r + 1][cut].astype(F32)).astype(BF16)
-            for r in evens
-        }
-        sent = []
-        bit = n_dp // 2
-        while bit > 1:
-            for r in [r for r in held if r & bit]:
-                value = exchange(held.pop(r), bit)
-                if r == bit:
-                    sent.append(value)
-                else:
-                    held[r ^ bit] = held[r ^ bit] + value
-            bit //= 2
-        return sent
-
-    ahead, behind, acts = add_and_send(half - 1, ahead, behind, acts, halves=True)
-    down_sum = sum_step(down_sum, 0)
     parts = {}
     for r in evens:
-        parts[r], parts[r + 1] = backward(r, 2, acts)
+        (parts[r + 1],) = backward(r + 1, acts)
     ahead, behind, parts, down_sum, acts = fence(ahead, behind, parts, down_sum, acts)
-    ahead, behind, acts, parts = add_and_send(half - 2, ahead, behind, acts, parts)
+    ahead, behind, acts, parts = add_and_send(
+        half - 1, ahead, behind, acts, parts, halves=True
+    )
     for r in evens:
-        parts[r + 1] = exchange(parts[r + 1], 1)
-    parts, acts = fence(parts, acts)
+        parts[r] = backward(r, acts, [exchange(parts.pop(r + 1), 1)], pieces)
+    parts, down_sum = fence(parts, down_sum)
+    down_sum = sum_step(down_sum, 0)
+    ahead, behind, parts, down_sum, acts = fence(ahead, behind, parts, down_sum, acts)
     arriving = [partial_gradient(0)]
-    (parts[1],) = backward(1, 1, acts)
-    parts[1], down_sum = fence(parts[1], down_sum)
+    ahead, behind, acts = add_and_send(half - 2, ahead, behind, acts)
     down_sum = sum_step(down_sum, 1)
+    (parts[1],) = backward(1, acts)
     ahead, behind, parts, arriving, down_sum, acts = fence(
         ahead, behind, parts, arriving, down_sum, acts
     )
+    arriving.append(partial_gradient(1))
     for step in range(half - 3, 0, -1):
-        ahead, behind, acts, parts = add_and_send(step, ahead, behind, acts, parts)
-    arriving.append(partial_gradient(1))
+        ahead, behind, acts = add_and_send(step, ahead, behind, acts)
     down_sum = sum_step(down_sum, 2)
     parts[1] = exchange(parts[1], 1)
-    (parts[0],) = backward(0, 1, acts)
+    (parts[0],) = backward(0, acts)
     ahead, behind, parts, arriving, down_sum, acts = fence(
         ahead, behind, parts, arriving, down_sum, acts
     )
@@ -707,13 +727,13 @@
         hidden_gradient = combine(
             ends[piece], parts[0], parts[1], arriving[piece], hidden_gradient
         )
-    groups = [hidden_0, near]
+    groups = [hidden, near]
     for r in evens:
         groups += [piece[r] for piece in fetched] + [piece[r + 1] for piece in passed]
     down_grad = factor_grad(masks, acts, groups)
     down_grad = jnp.transpose(down_grad.reshape(owned, rank, units), (0, 2, 1))
-    base_out, terms, hidden_gradient, down_grad, branch = fence(
-        base_out, terms, hidden_gradient, down_grad, branch
+    base_out, terms, arriving[2], hidden_gradient, down_grad, branch = fence(
+        base_out, terms, arriving[2], hidden_gradient, down_grad, branch
     )
     (up_grad,) = call(
         functools.partial(up_grad_kernel, n_dp, blocks),
@@ -723,7 +743,6 @@
         [like((owned, rank, width), BF16)],
     )
     layer_out = (base_out.astype(F32) + branch).astype(BF16)
-    layer_out, up_grad, arriving[2] = fence(layer_out, up_grad, arriving[2])
     hidden_gradient = combine(ends[2], parts[0], parts[1], arriving[2], hidden_gradient)
     return layer_out, hidden_gradient, down_grad, up_grad
 

time: 295 us -> 293 us (level); the launches traced: 294 us -> 288 us
  waiting for transfers between devices: 83.1 us -> 65 us
  starting transfers between devices: 57.6 us -> 75 us
  other arithmetic: 8.89 us -> 3.33 us
  Pallas kernels: 120 us -> 125 us
  local copies, waits for them, and re-layouts: 22.7 us -> 18.5 us
    ppermute x29, waiting for transfers between devices: 67.8 us -> 35.3 us  [exchange(): return lax.ppermute(value, axis, [(i, i ^ bit) for i in range(count)])]
    ppermute x2 -> x10, waiting for transfers between devices: 0.01 us -> 29.7 us  [the longest x4 29.6 us: swap_places(): lax.ppermute(half_rows, ('dp', 'mp'), first)]
    ppermute x2 -> x10, starting transfers between devices: 8.93 us -> 25.2 us  [the longest x4 11.9 us: swap_places(): lax.ppermute(lax.ppermute(half_rows, ('dp', 'mp'), first), ('dp', 'mp'),...]
    ppermute x8, waiting for transfers between devices: 13.6 us -> 0.02 us  [onward(): return lax.ppermute(value, 'mp', up_ring)]
    unnamed x130 -> x104, local copies, waits for them, and re-layouts: 18.7 us -> 10.8 us
    convert_element_type x3 -> x1, other arithmetic: 6.36 us -> 0.01 us  [shards(): up_sum.astype(BF16)]
    pallas_call x3 -> x4, Pallas kernels: 46.5 us -> 52.6 us  [backward_part(): pl.pallas_call(functools.partial(backward_kernel, group, n_mp, offsets, l...]
    slice x3, local copies, waits for them, and re-layouts: 0.17 us -> 4.02 us  [fetch(): held = {0: hidden[cuts[piece]:cuts[piece + 1]]}]
  transfers between devices with their start and end apart: 47 -> 55, of which waited for: 19 -> 17; matrix products, arithmetic and copies ran while one was open for 4% -> 2% of each run, Pallas kernels for 37% -> 40%
where the time goes in v4:
time: 293 us; the launch traced here: 288 us
  Pallas kernels  125 us (43%)
  starting transfers between devices  75 us (26%)
  waiting for transfers between devices  65 us (22%)
  local copies, waits for them, and re-layouts  18.5 us (6%)
  other arithmetic  3.33 us (1%)
    pallas_call x4, Pallas kernels, backward_part(): pl.pallas_call(functools.partial(backward_kernel, group, n_mp, offsets, l...  52.6 us
    pallas_call x4, Pallas kernels, forward_part(): pl.pallas_call(functools.partial(forward_kernel, len(hids)), grid=(cols /...  43.8 us
    ppermute x29, waiting for transfers between devices, exchange(): return lax.ppermute(value, axis, [(i, i ^ bit) for i in range(count)])  35.3 us
    ppermute x29, starting transfers between devices, exchange(): return lax.ppermute(value, axis, [(i, i ^ bit) for i in range(count)])  31.4 us
    ppermute x4, waiting for transfers between devices, swap_places(): lax.ppermute(half_rows, ('dp', 'mp'), first)  29.6 us
    ppermute x4, starting transfers between devices, swap_places(): lax.ppermute(lax.ppermute(half_rows, ('dp', 'mp'), first), ('dp', 'mp'),...  11.9 us
    ppermute x8, starting transfers between devices, backward_on(): return lax.ppermute(value, 'mp', down_ring)  11.7 us
    unnamed x104, local copies, waits for them, and re-layouts  10.8 us
  transfers between devices with their start and end apart: 55, of which 17 were waited for; matrix products, arithmetic and copies ran while one was open for 2% of the time, Pallas kernels for 40%

profile of v4, /device:TPU:0, one launch (start us, length us, event | category | flops | bytes accessed | tf_op | source)
XLA Modules:
  0.0 288.3 jit_solution(17037210849635688535)
XLA Ops:
  7.0 10.2 %collective-permute-done.1 = bf16[192,1024]{1,0:T(8,128)(2,1)S(1)} collective-permute-done((bf16[192,1024]{1,0:T(8,128)(2,1)S(1)}, bf16[192,1024]{1,0:T(8,128)(2,1)S(1)}, u32[]{:S(2)}, u32[]{:S(2)}) %collective-permute-start.1) | collective-permute-done | bytes 393248 | tf_op jit(solution)/shard_map/ppermute | solution.py:511
  17.3 4.4 %collective-permute-start.2 = (bf16[192,1024]{1,0:T(8,128)(2,1)S(1)}, bf16[192,1024]{1,0:T(8,128)(2,1)S(1)}, u32[]{:S(2)}, u32[]{:S(2)}) collective-permute-start(bf16[192,1024]{1,0:T(8,128)(2,1)S(1)} %collective-permute-done.1), channel_id=1, source_target_pairs={{20,16},{21,17},{22,24},{23,25},{28,18},{29,19},{30,26},{31,27},{0... | collective-permute-start | bytes 1179656 | tf_op jit(solution)/shard_map/ppermute | solution.py:510
  21.7 8.3 %collective-permute-done.3 = bf16[192,1024]{1,0:T(8,128)(2,1)S(1)} collective-permute-done((bf16[192,1024]{1,0:T(8,128)(2,1)S(1)}, bf16[192,1024]{1,0:T(8,128)(2,1)S(1)}, u32[]{:S(2)}, u32[]{:S(2)}) %collective-permute-start.3) | collective-permute-done | bytes 393248 | tf_op jit(solution)/shard_map/ppermute | solution.py:511
  32.0 8.9 %collective-permute-start.7 = (bf16[64,1024]{1,0:T(8,128)(2,1)S(1)}, bf16[64,1024]{1,0:T(8,128)(2,1)S(1)}, u32[]{:S(2)}, u32[]{:S(2)}) collective-permute-start(bf16[64,1024]{1,0:T(8,128)(2,1)S(1)} %get-tuple-element.183), channel_id=1, source_target_pairs={{0,16},{8,24},{16,0},{24,8},{1,17},{9,25},{17,1},{25,9},{2,18},{10... | collective-permute-start | bytes 393224 | tf_op jit(solution)/shard_map/ppermute | solution.py:487
  41.2 3.0 %collective-permute-done.7.refs_2_ = bf16[64,1024]{1,0:T(8,128)(2,1)S(1)} collective-permute-done((bf16[64,1024]{1,0:T(8,128)(2,1)S(1)}, bf16[64,1024]{1,0:T(8,128)(2,1)S(1)}, u32[]{:S(2)}, u32[]{:S(2)}) %collective-permute-start.7) | collective-permute-done | bytes 131104 | tf_op jit(solution)/shard_map/ppermute | solution.py:487
  44.2 2.4 collective-permute-done.8.refs_3_
  60.9 10.6 %forward_part.4 = (bf16[4,2,3,128,1024]{4,3,2,1,0:T(8,128)(2,1)}, bf16[1,192,128]{2,1,0:T(8,128)(2,1)S(1)}) custom-call(bf16[384,3328]{1,0:T(8,128)(2,1)S(1)} %copy-done.8, bf16[3328,2048]{1,0:T(8,128)(2,1)} %refs_11_.7, bf16[3328,256]{1,0:T(8,128)(2,1)S(1)} %copy-done.4, bf16[4,3,128,256]{3,2,1,0:T(8,128)(2,1)S(1)} %get-tuple-element.196.refs_3_.refs_6_.refs_4_.refs_10_.m_ref), custom_call_target="tpu_custom_call" | custom-call | flops 5234491392 | tf_op jit(solution)/shard_map/forward_part/pallas_call | solution.py:328
  75.6 11.4 %forward_part.5 = (bf16[4,2,3,128,1024]{4,3,2,1,0:T(8,128)(2,1)}, bf16[1,192,128]{2,1,0:T(8,128)(2,1)S(1)}) custom-call(bf16[384,3328]{1,0:T(8,128)(2,1)} %collective-permute-done.5.refs_0_.refs_5_, bf16[3328,2048]{1,0:T(8,128)(2,1)} %refs_11_.7, bf16[3328,256]{1,0:T(8,128)(2,1)S(1)} %copy-done.5, ...), custom_call_target="tpu_custom_call", output_to_operand_aliasing={{0}: (4, {})} | custom-call | flops 5234491392 | tf_op jit(solution)/shard_map/forward_part/pallas_call | solution.py:328
  87.1 7.5 %collective-permute-done.17 = bf16[192,128]{1,0:T(8,128)(2,1)S(1)} collective-permute-done((bf16[192,128]{1,0:T(8,128)(2,1)S(1)}, bf16[192,128]{1,0:T(8,128)(2,1)S(1)}, u32[]{:S(2)}, u32[]{:S(2)}) %collective-permute-start.17) | collective-permute-done | bytes 49184 | tf_op jit(solution)/shard_map/ppermute | solution.py:487
  99.9 12.7 %forward_part.6 = (bf16[4,2,3,128,1024]{4,3,2,1,0:T(8,128)(2,1)}, bf16[2,128,128]{2,1,0:T(8,128)(2,1)S(1)}) custom-call(bf16[128,3328]{1,0:T(8,128)(2,1)} %collective-permute-done.11.refs_0_.refs_6_, bf16[128,3328]{1,0:T(8,128)(2,1)S(1)} %collective-permute-done.15.refs_1_.refs_7_, ...), custom_call_target="tpu_custom_call", output_to_operand_aliasing={{0}: (7, {})} | custom-call | flops 6979321856 | tf_op jit(solution)/shard_map/forward_part/pallas_call | solution.py:328
  114.7 3.7 %collective-permute-done.22 = bf16[192,128]{1,0:T(8,128)(2,1)S(1)} collective-permute-done((bf16[192,128]{1,0:T(8,128)(2,1)S(1)}, bf16[192,128]{1,0:T(8,128)(2,1)S(1)}, u32[]{:S(2)}, u32[]{:S(2)}) %collective-permute-start.22) | collective-permute-done | bytes 49184 | tf_op jit(solution)/shard_map/ppermute | solution.py:487
  122.8 9.1 %forward_part.7 = (bf16[4,2,3,128,1024]{4,3,2,1,0:T(8,128)(2,1)}, bf16[2,64,128]{2,1,0:T(8,128)(2,1)S(1)}) custom-call(bf16[128,3328]{1,0:T(8,128)(2,1)S(1)} %collective-permute-done.20.refs_0_.refs_8_, bf16[128,3328]{1,0:T(8,128)(2,1)S(1)} %collective-permute-done.25.refs_1_.refs_11_, bf16[3328,2048]{1,0:T(8,128)(2,1)} %refs_11_.7, ...), custom_call_target="tpu_custom_call", output_to_operand_aliasing={{0}: (5, {})} | custom-call | flops 3489660928 | tf_op jit(solution)/shard_map/forward_part/pallas_call | solution.py:328
  133.2 2.8 copy-done
  141.1 13.0 %backward_part.4 = bf16[384,3328]{1,0:T(8,128)(2,1)} custom-call(s32[2]{0:T(128)S(1)} %pad_add_fusion.at_ref, bf16[384,1024]{1,0:T(8,128)(2,1)S(1)} %maximum_add_fusion.refs_0_, bf16[384,1024]{1,0:T(8,128)(2,1)} %collective-permute-done.9.refs_1_, bf16[384,1024]{1,0:T(8,128)(2,1)} %collective-permute-done.10.refs_2_, ...), custom_call_target="tpu_custom_call" | custom-call | flops 5234491392 | tf_op jit(solution)/shard_map/backward_part/pallas_call | solution.py:416
  158.1 3.1 %collective-permute-done.35.refs_13_ = bf16[384,3328]{1,0:T(8,128)(2,1)} collective-permute-done((bf16[384,3328]{1,0:T(8,128)(2,1)}, bf16[384,3328]{1,0:T(8,128)(2,1)}, u32[]{:S(2)}, u32[]{:S(2)}) %collective-permute-start.35) | collective-permute-done | bytes 2555936 | tf_op jit(solution)/shard_map/ppermute | solution.py:487
  161.3 13.2 %backward_part.5 = (bf16[144,3328]{1,0:T(8,128)(2,1)}, bf16[144,3328]{1,0:T(8,128)(2,1)}, bf16[96,3328]{1,0:T(8,128)(2,1)}) custom-call(s32[2]{0:T(128)S(1)} %pad_add_fusion.at_ref, bf16[384,1024]{1,0:T(8,128)(2,1)S(1)} %maximum_add_fusion.refs_0_, bf16[384,1024]{1,0:T(8,128)(2,1)} %collective-permute-done.9.refs_1_, ...), custom_call_target="tpu_custom_call" | custom-call | flops 20937965568 | tf_op jit(solution)/shard_map/backward_part/pallas_call | solution.py:416
  174.5 2.7 collective-permute-start.36
  177.1 2.7 collective-permute-done.36
  179.9 3.3 %collective-permute-start.39 = (bf16[144,3328]{1,0:T(8,128)(2,1)}, bf16[144,3328]{1,0:T(8,128)(2,1)}, u32[]{:S(2)}, u32[]{:S(2)}) collective-permute-start(bf16[144,3328]{1,0:T(8,128)(2,1)} %get-tuple-element.287), channel_id=1, source_target_pairs={{0,16},{8,24},{16,0},{24,8},{1,17},{9,25},{17,1},{25,9},{2,18},{10... | collective-permute-start | bytes 2875400 | tf_op jit(solution)/shard_map/ppermute | solution.py:487
  186.4 13.2 %backward_part.6 = bf16[384,3328]{1,0:T(8,128)(2,1)} custom-call(s32[2]{0:T(128)S(1)} %pad_add_fusion.at_ref, bf16[384,1024]{1,0:T(8,128)(2,1)S(1)} %maximum_add_fusion.refs_0_, bf16[384,1024]{1,0:T(8,128)(2,1)} %collective-permute-done.9.refs_1_, bf16[384,1024]{1,0:T(8,128)(2,1)} %collective-permute-done.10.refs_2_, bf16[384,1024]{1,0:T(8,128)(2,1)S(1)} %copy-done.15, ...), custom_call_target="tpu_custom_call" | custom-call | flops 5234491392 | tf_op jit(solution)/shard_map/backward_part/pallas_call | solution.py:416
  199.6 3.6 %collective-permute-done.40 = bf16[192,128]{1,0:T(8,128)(2,1)S(1)} collective-permute-done((bf16[192,128]{1,0:T(8,128)(2,1)S(1)}, bf16[192,128]{1,0:T(8,128)(2,1)S(1)}, u32[]{:S(2)}, u32[]{:S(2)}) %collective-permute-start.40) | collective-permute-done | bytes 49184 | tf_op jit(solution)/shard_map/ppermute | solution.py:487
  211.4 13.3 %backward_part.7.own_ref = bf16[384,3328]{1,0:T(8,128)(2,1)} custom-call(s32[2]{0:T(128)S(1)} %pad_add_fusion.at_ref, bf16[384,1024]{1,0:T(8,128)(2,1)S(1)} %maximum_add_fusion.refs_0_, bf16[384,1024]{1,0:T(8,128)(2,1)} %collective-permute-done.9.refs_1_, bf16[384,1024]{1,0:T(8,128)(2,1)} %collective-permute-done.10.refs_2_, ...), custom_call_target="tpu_custom_call" | custom-call | flops 5234491392 | tf_op jit(solution)/shard_map/backward_part/pallas_call | solution.py:416
  224.6 3.6 %collective-permute-done.45 = bf16[192,128]{1,0:T(8,128)(2,1)S(1)} collective-permute-done((bf16[192,128]{1,0:T(8,128)(2,1)S(1)}, bf16[192,128]{1,0:T(8,128)(2,1)S(1)}, u32[]{:S(2)}, u32[]{:S(2)}) %collective-permute-start.45) | collective-permute-done | bytes 49184 | tf_op jit(solution)/shard_map/ppermute | solution.py:487
  235.7 7.4 %collective-permute-start.46 = (bf16[384,1024]{1,0:T(8,128)(2,1)}, bf16[384,1024]{1,0:T(8,128)(2,1)}, u32[]{:S(2)}, u32[]{:S(2)}) collective-permute-start(bf16[384,1024]{1,0:T(8,128)(2,1)} %last_add.1), channel_id=1, source_target_pairs={{0,0},{1,1},{2,8},{3,9},{8,2},{9,3},{10,10},{11,11},{20,20},{21,21... | collective-permute-start | bytes 2359304 | tf_op jit(solution)/shard_map/ppermute | solution.py:499
  243.2 2.7 collective-permute-done.47
  245.9 4.2 %collective-permute-start.48 = (bf16[192,1024]{1,0:T(8,128)(2,1)}, bf16[192,1024]{1,0:T(8,128)(2,1)}, u32[]{:S(2)}, u32[]{:S(2)}) collective-permute-start(bf16[192,1024]{1,0:T(8,128)(2,1)} %collective-permute-done.47), channel_id=1, source_target_pairs={{20,16},{21,17},{22,24},{23,25},{28,18},{29,19},{30,26},{31,27},{0... | collective-permute-start | bytes 1179656 | tf_op jit(solution)/shard_map/ppermute | solution.py:510
  250.1 8.4 %collective-permute-done.49 = bf16[192,1024]{1,0:T(8,128)(2,1)} collective-permute-done((bf16[192,1024]{1,0:T(8,128)(2,1)S(1)}, bf16[192,1024]{1,0:T(8,128)(2,1)}, u32[]{:S(2)}, u32[]{:S(2)}) %collective-permute-start.49) | collective-permute-done | bytes 393248 | tf_op jit(solution)/shard_map/ppermute | solution.py:511
  260.6 3.4 %combine.3.refs_2_ = bf16[384,3328]{1,0:T(8,128)(2,1)} custom-call(bf16[384,3328]{1,0:T(8,128)(2,1)S(1)} %copy-done.1, bf16[384,3328]{1,0:T(8,128)(2,1)} %collective-permute-done.43.refs_0_, bf16[144,3328]{1,0:T(8,128)(2,1)} %collective-permute-done.39.refs_1_, bf16[384,3328]{1,0:T(8,128)(2,1)} %blank.1.refs_2_), custom_call_target="tpu_custom_call", output_to_operand_aliasing={{}: (3, {})} | custom-call | tf_op jit(solution)/shard_map/combine/pallas_call | solution.py:253
  263.9 4.2 %combine.4.refs_2_ = bf16[384,3328]{1,0:T(8,128)(2,1)} custom-call(bf16[384,3328]{1,0:T(8,128)(2,1)S(1)} %copy-done.1, bf16[384,3328]{1,0:T(8,128)(2,1)} %collective-permute-done.43.refs_0_, bf16[144,3328]{1,0:T(8,128)(2,1)} %collective-permute-done.44.refs_1_, bf16[384,3328]{1,0:T(8,128)(2,1)} %combine.3.refs_2_), custom_call_target="tpu_custom_call", output_to_operand_aliasing={{}: (3, {})} | custom-call | tf_op jit(solution)/shard_map/combine/pallas_call | solution.py:253
  268.2 6.1 %factor_grad.1 = bf16[256,3328]{1,0:T(8,128)(2,1)} custom-call(bf16[4,3,128,256]{3,2,1,0:T(8,128)(2,1)S(1)} %get-tuple-element.196.refs_3_.refs_6_.refs_4_.refs_10_.m_ref, bf16[192,128]{1,0:T(8,128)(2,1)S(1)} %add_convert_fusion.2.refs_9_.refs_0_, bf16[192,128]{1,0:T(8,128)(2,1)S(1)} %collective-permute-done.26.refs_9_.refs_1_, ...), custom_call_target="tpu_custom_call" | custom-call | tf_op jit(solution)/shard_map/factor_grad/pallas_call | solution.py:456
  278.3 2.5 collective-permute-done.52.refs_2_
  280.8 2.4 collective-permute-done.53.refs_3_
  (235 shorter events, 78.8 us)
Async XLA Ops:
  0.6 46.0 %collective-permute-start.5 = (bf16[384,3328]{1,0:T(8,128)(2,1)}, bf16[384,3328]{1,0:T(8,128)(2,1)}, u32[]{:S(2)}, u32[]{:S(2)}) collective-permute-start(bf16[384,3328]{1,0:T(8,128)(2,1)} %refs_4_.2), channel_id=1, source_target_pairs={{0,8},{8,0},{16,24},{24,16},{1,9},{9,1},{17,25},{25,17},{2,10},{10... | collective-permute-start | bytes 7667720 | tf_op jit(solution)/shard_map/ppermute | solution.py:487
  5.0 24.9 %collective-permute-start.3 = (bf16[192,1024]{1,0:T(8,128)(2,1)S(1)}, bf16[192,1024]{1,0:T(8,128)(2,1)S(1)}, u32[]{:S(2)}, u32[]{:S(2)}) collective-permute-start(bf16[192,1024]{1,0:T(8,128)(2,1)S(1)} %get-tuple-element.357), channel_id=1, source_target_pairs={{4,0},{5,1},{6,8},{7,9},{12,2},{13,3},{14,10},{15,11},{16,20},{17,... | collective-permute-start | bytes 1179656 | tf_op jit(solution)/shard_map/ppermute | solution.py:511
  6.3 34.6 %collective-permute-start = (bf16[384,1024]{1,0:T(8,128)(2,1)S(1)}, bf16[384,1024]{1,0:T(8,128)(2,1)S(1)}, u32[]{:S(2)}, u32[]{:S(2)}) collective-permute-start(bf16[384,1024]{1,0:T(8,128)(2,1)S(1)} %mask.1.grad_ref), channel_id=1, source_target_pairs={{0,0},{1,1},{2,8},{3,9},{8,2},{9,3},{10,10},{11,11},{20,20},{21,21... | collective-permute-start | bytes 2359304 | tf_op jit(solution)/shard_map/ppermute | solution.py:499
  48.8 23.0 %collective-permute-start.11 = (bf16[128,3328]{1,0:T(8,128)(2,1)}, bf16[128,3328]{1,0:T(8,128)(2,1)}, u32[]{:S(2)}, u32[]{:S(2)}) collective-permute-start(bf16[128,3328]{1,0:T(8,128)(2,1)} %slice.47), channel_id=1, source_target_pairs={{0,16},{8,24},{16,0},{24,8},{1,17},{9,25},{17,1},{25,9},{2,18},{10... | collective-permute-start | bytes 2555912 | tf_op jit(solution)/shard_map/ppermute | solution.py:487
  48.8 22.9 %collective-permute-start.10 = (bf16[384,1024]{1,0:T(8,128)(2,1)S(1)}, bf16[384,1024]{1,0:T(8,128)(2,1)}, u32[]{:S(2)}, u32[]{:S(2)}) collective-permute-start(bf16[384,1024]{1,0:T(8,128)(2,1)S(1)} %maximum_add_fusion.refs_0_), channel_id=1, source_target_pairs={{2,0},{4,2},{6,4},{7,6},{5,7},{3,5},{1,3},{0,1},{10,8},{12,10},{14... | collective-permute-start | bytes 2359304 | tf_op jit(solution)/shard_map/ppermute | solution.py:525
  50.4 21.4 %collective-permute-start.9 = (bf16[384,1024]{1,0:T(8,128)(2,1)S(1)}, bf16[384,1024]{1,0:T(8,128)(2,1)}, u32[]{:S(2)}, u32[]{:S(2)}) collective-permute-start(bf16[384,1024]{1,0:T(8,128)(2,1)S(1)} %maximum_add_fusion.refs_0_), channel_id=1, source_target_pairs={{0,2},{2,4},{4,6},{6,7},{7,5},{5,3},{3,1},{1,0},{8,10},{10,12},{12... | collective-permute-start | bytes 2359304 | tf_op jit(solution)/shard_map/ppermute | solution.py:522
  53.2 18.5 %collective-permute-start.12 = (bf16[192,128]{1,0:T(8,128)(2,1)S(1)}, bf16[192,128]{1,0:T(8,128)(2,1)S(1)}, u32[]{:S(2)}, u32[]{:S(2)}) collective-permute-start(bf16[192,128]{1,0:T(8,128)(2,1)S(1)} %convert_element_type.63), channel_id=1, source_target_pairs={{0,4},{1,5},{2,6},{3,7},{4,0},{5,1},{6,2},{7,3},{8,12},{9,13},{10,... | collective-permute-start | bytes 147464 | tf_op jit(solution)/shard_map/ppermute | solution.py:487
  71.8 22.7 %collective-permute-start.15 = (bf16[128,3328]{1,0:T(8,128)(2,1)S(1)}, bf16[128,3328]{1,0:T(8,128)(2,1)S(1)}, u32[]{:S(2)}, u32[]{:S(2)}) collective-permute-start(bf16[128,3328]{1,0:T(8,128)(2,1)S(1)} %slice.48), channel_id=1, source_target_pairs={{0,16},{8,24},{16,0},{24,8},{1,17},{9,25},{17,1},{25,9},{2,18},{10... | collective-permute-start | bytes 2555912 | tf_op jit(solution)/shard_map/ppermute | solution.py:487
  72.6 22.0 %collective-permute-start.16 = (bf16[128,3328]{1,0:T(8,128)(2,1)}, bf16[128,3328]{1,0:T(8,128)(2,1)S(1)}, u32[]{:S(2)}, u32[]{:S(2)}) collective-permute-start(bf16[128,3328]{1,0:T(8,128)(2,1)} %collective-permute-done.11.refs_0_.refs_6_), channel_id=1, source_target_pairs={{0,8},{8,0},{16,24},{24,16},{1,9},{9,1},{17,25},{25,17},{2,10},{10... | collective-permute-start | bytes 2555912 | tf_op jit(solution)/shard_map/ppermute | solution.py:487
  72.6 21.9 %collective-permute-start.13 = (bf16[384,1024]{1,0:T(8,128)(2,1)}, bf16[384,1024]{1,0:T(8,128)(2,1)S(1)}, u32[]{:S(2)}, u32[]{:S(2)}) collective-permute-start(bf16[384,1024]{1,0:T(8,128)(2,1)} %collective-permute-done.9.refs_1_), channel_id=1, source_target_pairs={{0,2},{2,4},{4,6},{6,7},{7,5},{5,3},{3,1},{1,0},{8,10},{10,12},{12... | collective-permute-start | bytes 2359304 | tf_op jit(solution)/shard_map/ppermute | solution.py:522
  73.6 21.0 %collective-permute-start.14 = (bf16[384,1024]{1,0:T(8,128)(2,1)}, bf16[384,1024]{1,0:T(8,128)(2,1)S(1)}, u32[]{:S(2)}, u32[]{:S(2)}) collective-permute-start(bf16[384,1024]{1,0:T(8,128)(2,1)} %collective-permute-done.10.refs_2_), channel_id=1, source_target_pairs={{2,0},{4,2},{6,4},{7,6},{5,7},{3,5},{1,3},{0,1},{10,8},{12,10},{14... | collective-permute-start | bytes 2359304 | tf_op jit(solution)/shard_map/ppermute | solution.py:525
  74.8 19.7 %collective-permute-start.17 = (bf16[192,128]{1,0:T(8,128)(2,1)S(1)}, bf16[192,128]{1,0:T(8,128)(2,1)S(1)}, u32[]{:S(2)}, u32[]{:S(2)}) collective-permute-start(bf16[192,128]{1,0:T(8,128)(2,1)S(1)} %convert_element_type.65), channel_id=1, source_target_pairs={{0,2},{1,3},{2,0},{3,1},{4,6},{5,7},{6,4},{7,5},{8,10},{9,11},{10,... | collective-permute-start | bytes 147464 | tf_op jit(solution)/shard_map/ppermute | solution.py:487
  96.5 21.9 %collective-permute-start.20 = (bf16[128,3328]{1,0:T(8,128)(2,1)S(1)}, bf16[128,3328]{1,0:T(8,128)(2,1)S(1)}, u32[]{:S(2)}, u32[]{:S(2)}) collective-permute-start(bf16[128,3328]{1,0:T(8,128)(2,1)S(1)} %slice.49), channel_id=1, source_target_pairs={{0,16},{8,24},{16,0},{24,8},{1,17},{9,25},{17,1},{25,9},{2,18},{10... | collective-permute-start | bytes 2555912 | tf_op jit(solution)/shard_map/ppermute | solution.py:487
  97.4 21.0 %collective-permute-start.18 = (bf16[384,1024]{1,0:T(8,128)(2,1)S(1)}, bf16[384,1024]{1,0:T(8,128)(2,1)S(1)}, u32[]{:S(2)}, u32[]{:S(2)}) collective-permute-start(bf16[384,1024]{1,0:T(8,128)(2,1)S(1)} %collective-permute-done.13.refs_3_), channel_id=1, source_target_pairs={{0,2},{2,4},{4,6},{6,7},{7,5},{5,3},{3,1},{1,0},{8,10},{10,12},{12... | collective-permute-start | bytes 2359304 | tf_op jit(solution)/shard_map/ppermute | solution.py:522
  97.9 20.6 %collective-permute-start.19 = (bf16[384,1024]{1,0:T(8,128)(2,1)S(1)}, bf16[384,1024]{1,0:T(8,128)(2,1)S(1)}, u32[]{:S(2)}, u32[]{:S(2)}) collective-permute-start(bf16[384,1024]{1,0:T(8,128)(2,1)S(1)} %collective-permute-done.14.refs_4_), channel_id=1, source_target_pairs={{2,0},{4,2},{6,4},{7,6},{5,7},{3,5},{1,3},{0,1},{10,8},{12,10},{14... | collective-permute-start | bytes 2359304 | tf_op jit(solution)/shard_map/ppermute | solution.py:525
  156.1 23.8 %collective-permute-start.33 = (bf16[384,1024]{1,0:T(8,128)(2,1)}, bf16[384,1024]{1,0:T(8,128)(2,1)S(1)}, u32[]{:S(2)}, u32[]{:S(2)}) collective-permute-start(bf16[384,1024]{1,0:T(8,128)(2,1)} %get-tuple-element.261), channel_id=1, source_target_pairs={{0,2},{2,4},{4,6},{6,7},{7,5},{5,3},{3,1},{1,0},{8,10},{10,12},{12... | collective-permute-start | bytes 2359304 | tf_op jit(solution)/shard_map/ppermute | solution.py:522
  157.2 22.7 %collective-permute-start.34 = (bf16[384,1024]{1,0:T(8,128)(2,1)}, bf16[384,1024]{1,0:T(8,128)(2,1)S(1)}, u32[]{:S(2)}, u32[]{:S(2)}) collective-permute-start(bf16[384,1024]{1,0:T(8,128)(2,1)} %get-tuple-element.262), channel_id=1, source_target_pairs={{2,0},{4,2},{6,4},{7,6},{5,7},{3,5},{1,3},{0,1},{10,8},{12,10},{14... | collective-permute-start | bytes 2359304 | tf_op jit(solution)/shard_map/ppermute | solution.py:525
  179.9 23.7 %collective-permute-start.39 = (bf16[144,3328]{1,0:T(8,128)(2,1)}, bf16[144,3328]{1,0:T(8,128)(2,1)}, u32[]{:S(2)}, u32[]{:S(2)}) collective-permute-start(bf16[144,3328]{1,0:T(8,128)(2,1)} %get-tuple-element.287), channel_id=1, source_target_pairs={{0,16},{8,24},{16,0},{24,8},{1,17},{9,25},{17,1},{25,9},{2,18},{10... | collective-permute-start | bytes 2875400 | tf_op jit(solution)/shard_map/ppermute | solution.py:487
  184.3 19.1 %collective-permute-start.37 = (bf16[384,1024]{1,0:T(8,128)(2,1)S(1)}, bf16[384,1024]{1,0:T(8,128)(2,1)S(1)}, u32[]{:S(2)}, u32[]{:S(2)}) collective-permute-start(bf16[384,1024]{1,0:T(8,128)(2,1)S(1)} %get-tuple-element.284), channel_id=1, source_target_pairs={{0,2},{2,4},{4,6},{6,7},{7,5},{5,3},{3,1},{1,0},{8,10},{10,12},{12... | collective-permute-start | bytes 2359304 | tf_op jit(solution)/shard_map/ppermute | solution.py:522
  184.4 18.9 %collective-permute-start.38 = (bf16[384,1024]{1,0:T(8,128)(2,1)S(1)}, bf16[384,1024]{1,0:T(8,128)(2,1)S(1)}, u32[]{:S(2)}, u32[]{:S(2)}) collective-permute-start(bf16[384,1024]{1,0:T(8,128)(2,1)S(1)} %get-tuple-element.285), channel_id=1, source_target_pairs={{2,0},{4,2},{6,4},{7,6},{5,7},{3,5},{1,3},{0,1},{10,8},{12,10},{14... | collective-permute-start | bytes 2359304 | tf_op jit(solution)/shard_map/ppermute | solution.py:525
  186.4 16.9 %collective-permute-start.40 = (bf16[192,128]{1,0:T(8,128)(2,1)S(1)}, bf16[192,128]{1,0:T(8,128)(2,1)S(1)}, u32[]{:S(2)}, u32[]{:S(2)}) collective-permute-start(bf16[192,128]{1,0:T(8,128)(2,1)S(1)} %convert_element_type.78), channel_id=1, source_target_pairs={{0,2},{1,3},{2,0},{3,1},{4,6},{5,7},{6,4},{7,5},{8,10},{9,11},{10,... | collective-permute-start | bytes 147464 | tf_op jit(solution)/shard_map/ppermute | solution.py:487
  203.7 24.6 %collective-permute-start.43 = (bf16[384,3328]{1,0:T(8,128)(2,1)}, bf16[384,3328]{1,0:T(8,128)(2,1)}, u32[]{:S(2)}, u32[]{:S(2)}) collective-permute-start(bf16[384,3328]{1,0:T(8,128)(2,1)} %backward_part.6), channel_id=1, source_target_pairs={{0,8},{8,0},{16,24},{24,16},{1,9},{9,1},{17,25},{25,17},{2,10},{10... | collective-permute-start | bytes 7667720 | tf_op jit(solution)/shard_map/ppermute | solution.py:487
  203.7 24.6 %collective-permute-start.44 = (bf16[144,3328]{1,0:T(8,128)(2,1)}, bf16[144,3328]{1,0:T(8,128)(2,1)}, u32[]{:S(2)}, u32[]{:S(2)}) collective-permute-start(bf16[144,3328]{1,0:T(8,128)(2,1)} %get-tuple-element.306), channel_id=1, source_target_pairs={{0,16},{8,24},{16,0},{24,8},{1,17},{9,25},{17,1},{25,9},{2,18},{10... | collective-permute-start | bytes 2875400 | tf_op jit(solution)/shard_map/ppermute | solution.py:487
  206.4 21.8 %collective-permute-start.41 = (bf16[384,1024]{1,0:T(8,128)(2,1)S(1)}, bf16[384,1024]{1,0:T(8,128)(2,1)S(1)}, u32[]{:S(2)}, u32[]{:S(2)}) collective-permute-start(bf16[384,1024]{1,0:T(8,128)(2,1)S(1)} %get-tuple-element.302), channel_id=1, source_target_pairs={{0,2},{2,4},{4,6},{6,7},{7,5},{5,3},{3,1},{1,0},{8,10},{10,12},{12... | collective-permute-start | bytes 2359304 | tf_op jit(solution)/shard_map/ppermute | solution.py:522
  207.2 21.1 %collective-permute-start.42 = (bf16[384,1024]{1,0:T(8,128)(2,1)S(1)}, bf16[384,1024]{1,0:T(8,128)(2,1)S(1)}, u32[]{:S(2)}, u32[]{:S(2)}) collective-permute-start(bf16[384,1024]{1,0:T(8,128)(2,1)S(1)} %get-tuple-element.303), channel_id=1, source_target_pairs={{2,0},{4,2},{6,4},{7,6},{5,7},{3,5},{1,3},{0,1},{10,8},{12,10},{14... | collective-permute-start | bytes 2359304 | tf_op jit(solution)/shard_map/ppermute | solution.py:525
  209.3 18.9 %collective-permute-start.45 = (bf16[192,128]{1,0:T(8,128)(2,1)S(1)}, bf16[192,128]{1,0:T(8,128)(2,1)S(1)}, u32[]{:S(2)}, u32[]{:S(2)}) collective-permute-start(bf16[192,128]{1,0:T(8,128)(2,1)S(1)} %convert_element_type.80), channel_id=1, source_target_pairs={{0,1},{1,0},{2,3},{3,2},{4,5},{5,4},{6,7},{7,6},{8,9},{9,8},{10,11... | collective-permute-start | bytes 147464 | tf_op jit(solution)/shard_map/ppermute | solution.py:487
  234.4 24.0 %collective-permute-start.49 = (bf16[192,1024]{1,0:T(8,128)(2,1)S(1)}, bf16[192,1024]{1,0:T(8,128)(2,1)}, u32[]{:S(2)}, u32[]{:S(2)}) collective-permute-start(bf16[192,1024]{1,0:T(8,128)(2,1)S(1)} %get-tuple-element.355), channel_id=1, source_target_pairs={{4,0},{5,1},{6,8},{7,9},{12,2},{13,3},{14,10},{15,11},{16,20},{17,... | collective-permute-start | bytes 1179656 | tf_op jit(solution)/shard_map/ppermute | solution.py:511
  235.7 40.9 %collective-permute-start.46 = (bf16[384,1024]{1,0:T(8,128)(2,1)}, bf16[384,1024]{1,0:T(8,128)(2,1)}, u32[]{:S(2)}, u32[]{:S(2)}) collective-permute-start(bf16[384,1024]{1,0:T(8,128)(2,1)} %last_add.1), channel_id=1, source_target_pairs={{0,0},{1,1},{2,8},{3,9},{8,2},{9,3},{10,10},{11,11},{20,20},{21,21... | collective-permute-start | bytes 2359304 | tf_op jit(solution)/shard_map/ppermute | solution.py:499
  245.9 28.4 %collective-permute-start.48 = (bf16[192,1024]{1,0:T(8,128)(2,1)}, bf16[192,1024]{1,0:T(8,128)(2,1)}, u32[]{:S(2)}, u32[]{:S(2)}) collective-permute-start(bf16[192,1024]{1,0:T(8,128)(2,1)} %collective-permute-done.47), channel_id=1, source_target_pairs={{20,16},{21,17},{22,24},{23,25},{28,18},{29,19},{30,26},{31,27},{0... | collective-permute-start | bytes 1179656 | tf_op jit(solution)/shard_map/ppermute | solution.py:510
  258.5 17.9 %collective-permute-start.50 = (bf16[192,1024]{1,0:T(8,128)(2,1)}, bf16[192,1024]{1,0:T(8,128)(2,1)}, u32[]{:S(2)}, u32[]{:S(2)}) collective-permute-start(bf16[192,1024]{1,0:T(8,128)(2,1)} %collective-permute-done.49), channel_id=1, source_target_pairs={{0,16},{1,17},{8,24},{9,25},{2,18},{3,19},{10,26},{11,27},{20,4},{... | collective-permute-start | bytes 1179656 | tf_op jit(solution)/shard_map/ppermute | solution.py:510
  260.5 22.7 %collective-permute-start.54 = (bf16[96,3328]{1,0:T(8,128)(2,1)}, bf16[96,3328]{1,0:T(8,128)(2,1)}, u32[]{:S(2)}, u32[]{:S(2)}) collective-permute-start(bf16[96,3328]{1,0:T(8,128)(2,1)} %get-tuple-element.333), channel_id=1, source_target_pairs={{0,16},{8,24},{16,0},{24,8},{1,17},{9,25},{17,1},{25,9},{2,18},{10... | collective-permute-start | bytes 1916936 | tf_op jit(solution)/shard_map/ppermute | solution.py:487
  260.5 17.7 %collective-permute-start.51 = (bf16[64,1024]{1,0:T(8,128)(2,1)}, bf16[64,1024]{1,0:T(8,128)(2,1)S(1)}, u32[]{:S(2)}, u32[]{:S(2)}) collective-permute-start(bf16[64,1024]{1,0:T(8,128)(2,1)} %copy-done.49), channel_id=1, source_target_pairs={{0,8},{8,0},{16,24},{24,16},{1,9},{9,1},{17,25},{25,17},{2,10},{10... | collective-permute-start | bytes 393224 | tf_op jit(solution)/shard_map/ppermute | solution.py:487
  (75 other events, 815.6 us)

commit v5 on v4

--- a/solution.py
+++ b/solution.py
@@ -487,32 +487,12 @@
         return lax.ppermute(value, axis, [(i, i ^ bit) for i in range(count)])
 
     def swap_places(value):
-        index = lambda j, m: j * n_mp + m
-        near_pairs, far = [], []
-        for j in range(n_dp):
-            for m in range(n_mp):
-                c, h = m // q, m % q
-                if c // 2 == j // 2 or n_dp != 4:
-                    near_pairs.append((index(j, m), index(c, j * q + h)))
-                else:
-                    far.append((j, c, h))
-        swapped = lax.ppermute(value, ("dp", "mp"), near_pairs)
-        if far:
-            routes = (
-                lambda j, c, h: index(j ^ 2, c * q + h),
-                lambda j, c, h: index(c ^ 2, j * q + h),
-            )
-            halves = []
-            for route, half_rows in zip(routes, (value[:top], value[top:])):
-                first = [(index(j, c * q + h), route(j, c, h)) for j, c, h in far]
-                second = [(route(j, c, h), index(c, j * q + h)) for j, c, h in far]
-                halves.append(
-                    lax.ppermute(
-                        lax.ppermute(half_rows, ("dp", "mp"), first), ("dp", "mp"), second
-                    )
-                )
-            swapped = swapped + jnp.concatenate(halves, axis=0)
-        return swapped
+        pairs = [
+            (j * n_mp + m, (m // q) * n_mp + j * q + m % q)
+            for j in range(n_dp)
+            for m in range(n_mp)
+        ]
+        return lax.ppermute(value, ("dp", "mp"), pairs)
 
     ring = list(range(0, n_mp, 2)) + list(range(n_mp - 1, 0, -2))
     up_ring = [(ring[i], ring[(i + 1) % n_mp]) for i in range(n_mp)]
@@ -527,8 +507,8 @@
     evens = range(2, n_dp, 2)
     cuts = list(range(0, rows + 1, BLK))
 
-    def fetch(hidden, piece):
-        held = {0: hidden[cuts[piece] : cuts[piece + 1]]}
+    def fetch(hidden_cut, piece):
+        held = {0: hidden_cut[piece]}
         bit = 2
         while bit < n_dp:
             for r in list(held):
@@ -563,8 +543,9 @@
     arrived_up = [exchange(chosen[r], r) if r else chosen[0] for r in range(n_dp)]
     turned_factor = jnp.transpose(adapter_down, (0, 2, 1)).reshape(owned * rank, units)
     factor = turned_factor.T
-    swapped, near, arrived_up, factor, masks, hidden = fence(
-        swapped, near, arrived_up, factor, masks, hidden
+    hidden_cut = [hidden[a:b] for a, b in zip(cuts, cuts[1:])]
+    swapped, near, arrived_up, factor, masks, hidden, hidden_cut = fence(
+        swapped, near, arrived_up, factor, masks, hidden, hidden_cut
     )
 
     def forward(groups, span, hids, total):
@@ -583,7 +564,7 @@
     ring_blocks = [swapped]
     picked = {}
     ahead, behind = onward(ahead), backward_on(behind)
-    fetched = [fetch(hidden, 0)]
+    fetched = [fetch(hidden_cut, 0)]
     up_sum, block_up = call(
         functools.partial(up_kernel, n_dp, owned),
         "up_part",
@@ -595,24 +576,24 @@
     up_sum = sum_step(up_sum, 0)
     total, own = forward((0, 1), (0, blocks), [hidden], None)
     picked[0] = [own[0]]
-    ahead, behind, fetched[0], total, up_sum, hidden = fence(
-        ahead, behind, fetched[0], total, up_sum, hidden
+    ahead, behind, fetched[0], total, up_sum, hidden_cut = fence(
+        ahead, behind, fetched[0], total, up_sum, hidden_cut
     )
     ring_blocks += [ahead, behind]
     ahead, behind = onward(ahead), backward_on(behind)
-    fetched.append(fetch(hidden, 1))
+    fetched.append(fetch(hidden_cut, 1))
     passed = [pass_on(fetched[0])]
     up_sum = sum_step(up_sum, 1)
     total, own = forward((1, 1), (0, blocks), [near], total)
     picked[1] = [own[0]]
-    ahead, behind, fetched[1], passed, total, up_sum, hidden = fence(
-        ahead, behind, fetched[1], passed, total, up_sum, hidden
+    ahead, behind, fetched[1], passed, total, up_sum, hidden_cut = fence(
+        ahead, behind, fetched[1], passed, total, up_sum, hidden_cut
     )
     ring_blocks += [ahead, behind]
     for _ in range(3, half):
         ahead, behind = onward(ahead), backward_on(behind)
         ring_blocks += [ahead, behind]
-    fetched.append(fetch(hidden, 2))
+    fetched.append(fetch(hidden_cut, 2))
     passed.append(pass_on(fetched[1]))
     total = forward_pairs((0, 2), (0, 1), total)
     total, up_sum = fence(total, up_sum)
@@ -653,7 +634,7 @@
     ends = [0, 3 * rows // 8, 3 * rows // 4, rows]
     pieces = [b - a for a, b in zip(ends, ends[1:])]
 
-    def partial_gradient(piece):
+    def partial_gradient(piece, parts):
         held = {r: parts[r][piece] for r in evens}
         sent = []
         bit = n_dp // 2
@@ -693,14 +674,14 @@
     parts, down_sum = fence(parts, down_sum)
     down_sum = sum_step(down_sum, 0)
     ahead, behind, parts, down_sum, acts = fence(ahead, behind, parts, down_sum, acts)
-    arriving = [partial_gradient(0)]
+    arriving = [partial_gradient(0, parts)]
     ahead, behind, acts = add_and_send(half - 2, ahead, behind, acts)
     down_sum = sum_step(down_sum, 1)
     (parts[1],) = backward(1, acts)
     ahead, behind, parts, arriving, down_sum, acts = fence(
         ahead, behind, parts, arriving, down_sum, acts
     )
-    arriving.append(partial_gradient(1))
+    arriving.append(partial_gradient(1, parts))
     for step in range(half - 3, 0, -1):
         ahead, behind, acts = add_and_send(step, ahead, behind, acts)
     down_sum = sum_step(down_sum, 2)
@@ -711,6 +692,8 @@
     )
 
     base_out = last_add(at, live_rows, total, ahead, behind, n_mp)
+    base_out, down_sum, parts, acts = fence(base_out, down_sum, parts, acts)
+    base_out = swap_places(base_out)
     branch, *terms = call(
         functools.partial(term_kernel, n_dp, owned),
         "term_up",
@@ -718,10 +701,8 @@
         [down_sum, masked_grad, block_up],
         [like((rows, width), F32)] + [like((rank, width), BF16)] * n_dp,
     )
-    base_out, terms, parts, acts = fence(base_out, terms, parts, acts)
-    base_out = swap_places(base_out)
     terms = [exchange(terms[r], r) if r else terms[0] for r in range(n_dp)]
-    arriving.append(partial_gradient(2))
+    arriving.append(partial_gradient(2, parts))
     hidden_gradient = blank((rows, units), BF16)
     for piece in range(2):
         hidden_gradient = combine(
@@ -732,9 +713,7 @@
         groups += [piece[r] for piece in fetched] + [piece[r + 1] for piece in passed]
     down_grad = factor_grad(masks, acts, groups)
     down_grad = jnp.transpose(down_grad.reshape(owned, rank, units), (0, 2, 1))
-    base_out, terms, arriving[2], hidden_gradient, down_grad, branch = fence(
-        base_out, terms, arriving[2], hidden_gradient, down_grad, branch
-    )
+    terms, hidden_gradient, down_grad, branch = fence(terms, hidden_gradient, down_grad, branch)
     (up_grad,) = call(
         functools.partial(up_grad_kernel, n_dp, blocks),
         "up_grad",
@@ -742,8 +721,9 @@
         terms,
         [like((owned, rank, width), BF16)],
     )
+    base_out, arriving[2], up_grad = fence(base_out, arriving[2], up_grad)
+    hidden_gradient = combine(ends[2], parts[0], parts[1], arriving[2], hidden_gradient)
     layer_out = (base_out.astype(F32) + branch).astype(BF16)
-    hidden_gradient = combine(ends[2], parts[0], parts[1], arriving[2], hidden_gradient)
     return layer_out, hidden_gradient, down_grad, up_grad
 
 

time: 293 us -> 284 us (0.969); the launches traced: 288 us -> 283 us
  waiting for transfers between devices: 65 us -> 52.5 us
  local copies, waits for them, and re-layouts: 18.5 us -> 29.2 us
  starting transfers between devices: 75 us -> 70.1 us
    ppermute x10 -> x2, waiting for transfers between devices: 29.7 us -> 0.01 us  [swap_places(): return lax.ppermute(value, ('dp', 'mp'), pairs)]
    ppermute x10 -> x2, starting transfers between devices: 25.2 us -> 8.26 us  [swap_places(): return lax.ppermute(value, ('dp', 'mp'), pairs)]
    ppermute x29, waiting for transfers between devices: 35.3 us -> 51.5 us  [exchange(): return lax.ppermute(value, axis, [(i, i ^ bit) for i in range(count)])]
    ppermute x29, starting transfers between devices: 31.4 us -> 45.5 us  [exchange(): return lax.ppermute(value, axis, [(i, i ^ bit) for i in range(count)])]
    unnamed x104 -> x122, local copies, waits for them, and re-layouts: 10.8 us -> 23.6 us
  transfers between devices with their start and end apart: 55 -> 47, of which waited for: 17 -> 14; matrix products, arithmetic and copies ran while one was open for 2% -> 2% of each run, Pallas kernels for 40% -> 43%
where the time goes in v5:
time: 284 us; the launch traced here: 283 us
  Pallas kernels  127 us (45%)
  starting transfers between devices  70.1 us (25%)
  waiting for transfers between devices  52.5 us (18%)
  local copies, waits for them, and re-layouts  29.2 us (10%)
    pallas_call x4, Pallas kernels, backward_part(): pl.pallas_call(functools.partial(backward_kernel, group, n_mp, offsets, l...  52.6 us
    ppermute x29, waiting for transfers between devices, exchange(): return lax.ppermute(value, axis, [(i, i ^ bit) for i in range(count)])  51.5 us
    ppermute x29, starting transfers between devices, exchange(): return lax.ppermute(value, axis, [(i, i ^ bit) for i in range(count)])  45.5 us
    pallas_call x4, Pallas kernels, forward_part(): pl.pallas_call(functools.partial(forward_kernel, len(hids)), grid=(cols /...  43.9 us
    unnamed x122, local copies, waits for them, and re-layouts  23.6 us
    ppermute x8, starting transfers between devices, backward_on(): return lax.ppermute(value, 'mp', down_ring)  11.5 us
    pallas_call x3, Pallas kernels, combine(): pl.pallas_call(combine_kernel, grid=(arrived[0].shape[0] // tile,), in_sp...  9.53 us
    ppermute x2, starting transfers between devices, swap_places(): return lax.ppermute(value, ('dp', 'mp'), pairs)  8.26 us
  transfers between devices with their start and end apart: 47, of which 14 were waited for; matrix products, arithmetic and copies ran while one was open for 2% of the time, Pallas kernels for 43%

profile of v5, /device:TPU:0, one launch (start us, length us, event | category | flops | bytes accessed | tf_op | source)
XLA Modules:
  0.0 282.6 jit_solution(323134275025448976)
XLA Ops:
  6.7 4.0 %collective-permute-start.2 = (bf16[64,1024]{1,0:T(8,128)(2,1)S(1)}, bf16[64,1024]{1,0:T(8,128)(2,1)S(1)}, u32[]{:S(2)}, u32[]{:S(2)}) collective-permute-start(bf16[64,1024]{1,0:T(8,128)(2,1)S(1)} %get-tuple-element.184), channel_id=1, source_target_pairs={{0,8},{8,0},{16,24},{24,16},{1,9},{9,1},{17,25},{25,17},{2,10},{10... | collective-permute-start | bytes 393224 | tf_op jit(solution)/shard_map/ppermute | solution.py:487
  10.7 3.5 %collective-permute-start.3 = (bf16[64,1024]{1,0:T(8,128)(2,1)S(1)}, bf16[64,1024]{1,0:T(8,128)(2,1)S(1)}, u32[]{:S(2)}, u32[]{:S(2)}) collective-permute-start(bf16[64,1024]{1,0:T(8,128)(2,1)S(1)} %get-tuple-element.185), channel_id=1, source_target_pairs={{0,16},{8,24},{16,0},{24,8},{1,17},{9,25},{17,1},{25,9},{2,18},{10... | collective-permute-start | bytes 393224 | tf_op jit(solution)/shard_map/ppermute | solution.py:487
  14.2 3.3 %fusion = (bf16[128,3328]{1,0:T(8,128)(2,1)}, bf16[128,3328]{1,0:T(8,128)(2,1)}, bf16[128,3328]{1,0:T(8,128)(2,1)}) fusion(bf16[384,3328]{1,0:T(8,128)(2,1)} %refs_4_.2), kind=kLoop, calls=%fused_computation.15 | loop fusion | bytes 5111808 | tf_op jit(solution)/shard_map/slice | solution.py:546
  17.5 2.9 %collective-permute-done.3.refs_2_ = bf16[64,1024]{1,0:T(8,128)(2,1)S(1)} collective-permute-done((bf16[64,1024]{1,0:T(8,128)(2,1)S(1)}, bf16[64,1024]{1,0:T(8,128)(2,1)S(1)}, u32[]{:S(2)}, u32[]{:S(2)}) %collective-permute-start.3) | collective-permute-done | bytes 131104 | tf_op jit(solution)/shard_map/ppermute | solution.py:487
  20.3 5.1 %collective-permute-done.4.refs_3_ = bf16[64,1024]{1,0:T(8,128)(2,1)S(1)} collective-permute-done((bf16[64,1024]{1,0:T(8,128)(2,1)S(1)}, bf16[64,1024]{1,0:T(8,128)(2,1)S(1)}, u32[]{:S(2)}, u32[]{:S(2)}) %collective-permute-start.4) | collective-permute-done | bytes 131104 | tf_op jit(solution)/shard_map/ppermute | solution.py:487
  25.5 21.3 %collective-permute-start.7 = (bf16[128,3328]{1,0:T(8,128)(2,1)}, bf16[128,3328]{1,0:T(8,128)(2,1)}, u32[]{:S(2)}, u32[]{:S(2)}) collective-permute-start(bf16[128,3328]{1,0:T(8,128)(2,1)} %get-tuple-element.189), channel_id=1, source_target_pairs={{0,16},{8,24},{16,0},{24,8},{1,17},{9,25},{17,1},{25,9},{2,18},{10... | collective-permute-start | bytes 2555912 | tf_op jit(solution)/shard_map/ppermute | solution.py:487
  50.6 2.3 copy.17.refs_2_.refs_5_.refs_3_
  56.1 10.7 %forward_part.4 = (bf16[4,2,3,128,1024]{4,3,2,1,0:T(8,128)(2,1)}, bf16[1,192,128]{2,1,0:T(8,128)(2,1)S(1)}) custom-call(bf16[384,3328]{1,0:T(8,128)(2,1)S(1)} %copy-done.6, bf16[3328,2048]{1,0:T(8,128)(2,1)} %refs_11_.7, bf16[3328,256]{1,0:T(8,128)(2,1)S(1)} %copy-done.4, bf16[4,3,128,256]{3,2,1,0:T(8,128)(2,1)S(1)} %get-tuple-element.199.refs_3_.refs_6_.refs_4_.refs_10_.m_ref), custom_call_target="tpu_custom_call" | custom-call | flops 5234491392 | tf_op jit(solution)/shard_map/forward_part/pallas_call | solution.py:328
  71.6 11.4 %forward_part.5 = (bf16[4,2,3,128,1024]{4,3,2,1,0:T(8,128)(2,1)}, bf16[1,192,128]{2,1,0:T(8,128)(2,1)S(1)}) custom-call(bf16[384,3328]{1,0:T(8,128)(2,1)} %collective-permute-done.1.refs_0_.refs_5_, bf16[3328,2048]{1,0:T(8,128)(2,1)} %refs_11_.7, bf16[3328,256]{1,0:T(8,128)(2,1)S(1)} %copy-done.5, ...), custom_call_target="tpu_custom_call", output_to_operand_aliasing={{0}: (4, {})} | custom-call | flops 5234491392 | tf_op jit(solution)/shard_map/forward_part/pallas_call | solution.py:328
  83.0 6.9 %collective-permute-done.13 = bf16[192,128]{1,0:T(8,128)(2,1)S(1)} collective-permute-done((bf16[192,128]{1,0:T(8,128)(2,1)S(1)}, bf16[192,128]{1,0:T(8,128)(2,1)S(1)}, u32[]{:S(2)}, u32[]{:S(2)}) %collective-permute-start.13) | collective-permute-done | bytes 49184 | tf_op jit(solution)/shard_map/ppermute | solution.py:487
  94.0 12.7 %forward_part.6 = (bf16[4,2,3,128,1024]{4,3,2,1,0:T(8,128)(2,1)}, bf16[2,128,128]{2,1,0:T(8,128)(2,1)S(1)}) custom-call(bf16[128,3328]{1,0:T(8,128)(2,1)} %collective-permute-done.7.refs_0_.refs_6_, bf16[128,3328]{1,0:T(8,128)(2,1)S(1)} %collective-permute-done.11.refs_1_.refs_7_, ...), custom_call_target="tpu_custom_call", output_to_operand_aliasing={{0}: (7, {})} | custom-call | flops 6979321856 | tf_op jit(solution)/shard_map/forward_part/pallas_call | solution.py:328
  108.2 4.5 %collective-permute-done.18 = bf16[192,128]{1,0:T(8,128)(2,1)S(1)} collective-permute-done((bf16[192,128]{1,0:T(8,128)(2,1)S(1)}, bf16[192,128]{1,0:T(8,128)(2,1)S(1)}, u32[]{:S(2)}, u32[]{:S(2)}) %collective-permute-start.18) | collective-permute-done | bytes 49184 | tf_op jit(solution)/shard_map/ppermute | solution.py:487
  117.4 9.1 %forward_part.7 = (bf16[4,2,3,128,1024]{4,3,2,1,0:T(8,128)(2,1)}, bf16[2,64,128]{2,1,0:T(8,128)(2,1)S(1)}) custom-call(bf16[128,3328]{1,0:T(8,128)(2,1)S(1)} %collective-permute-done.16.refs_0_.refs_8_, bf16[128,3328]{1,0:T(8,128)(2,1)S(1)} %collective-permute-done.21.refs_1_.refs_11_, bf16[3328,2048]{1,0:T(8,128)(2,1)} %refs_11_.7, ...), custom_call_target="tpu_custom_call", output_to_operand_aliasing={{0}: (5, {})} | custom-call | flops 3489660928 | tf_op jit(solution)/shard_map/forward_part/pallas_call | solution.py:328
  127.8 2.8 copy-done
  135.0 13.0 %backward_part.4 = bf16[384,3328]{1,0:T(8,128)(2,1)} custom-call(s32[2]{0:T(128)S(1)} %pad_add_fusion.at_ref, bf16[384,1024]{1,0:T(8,128)(2,1)S(1)} %copy-done.11, bf16[384,1024]{1,0:T(8,128)(2,1)} %collective-permute-done.5.refs_1_, bf16[384,1024]{1,0:T(8,128)(2,1)} %collective-permute-done.6.refs_2_, bf16[384,1024]{1,0:T(8,128)(2,1)S(1)} %copy-done.16, ...), custom_call_target="tpu_custom_call" | custom-call | flops 5234491392 | tf_op jit(solution)/shard_map/backward_part/pallas_call | solution.py:416
  151.7 3.1 %collective-permute-done.31.refs_13_ = bf16[384,3328]{1,0:T(8,128)(2,1)} collective-permute-done((bf16[384,3328]{1,0:T(8,128)(2,1)}, bf16[384,3328]{1,0:T(8,128)(2,1)}, u32[]{:S(2)}, u32[]{:S(2)}) %collective-permute-start.31) | collective-permute-done | bytes 2555936 | tf_op jit(solution)/shard_map/ppermute | solution.py:487
  154.9 13.2 %backward_part.5 = (bf16[144,3328]{1,0:T(8,128)(2,1)}, bf16[144,3328]{1,0:T(8,128)(2,1)}, bf16[96,3328]{1,0:T(8,128)(2,1)}) custom-call(s32[2]{0:T(128)S(1)} %pad_add_fusion.at_ref, bf16[384,1024]{1,0:T(8,128)(2,1)S(1)} %copy-done.12, bf16[384,1024]{1,0:T(8,128)(2,1)} %collective-permute-done.5.refs_1_, bf16[384,1024]{1,0:T(8,128)(2,1)} %collective-permute-done.6.refs_2_, ...), custom_call_target="tpu_custom_call" | custom-call | flops 20937965568 | tf_op jit(solution)/shard_map/backward_part/pallas_call | solution.py:416
  168.1 2.5 collective-permute-start.32
  170.6 3.1 %collective-permute-done.32 = bf16[192,128]{1,0:T(8,128)(2,1)S(1)} collective-permute-done((bf16[192,128]{1,0:T(8,128)(2,1)S(1)}, bf16[192,128]{1,0:T(8,128)(2,1)S(1)}, u32[]{:S(2)}, u32[]{:S(2)}) %collective-permute-start.32) | collective-permute-done | bytes 49184 | tf_op jit(solution)/shard_map/ppermute | solution.py:487
  175.5 3.0 %collective-permute-start.35 = (bf16[144,3328]{1,0:T(8,128)(2,1)}, bf16[144,3328]{1,0:T(8,128)(2,1)S(1)}, u32[]{:S(2)}, u32[]{:S(2)}) collective-permute-start(bf16[144,3328]{1,0:T(8,128)(2,1)} %get-tuple-element.293), channel_id=1, source_target_pairs={{0,16},{8,24},{16,0},{24,8},{1,17},{9,25},{17,1},{25,9},{2,18},{10... | collective-permute-start | bytes 2875400 | tf_op jit(solution)/shard_map/ppermute | solution.py:487
  184.6 13.2 %backward_part.6 = bf16[384,3328]{1,0:T(8,128)(2,1)} custom-call(s32[2]{0:T(128)S(1)} %pad_add_fusion.at_ref, bf16[384,1024]{1,0:T(8,128)(2,1)S(1)} %copy-done.12, bf16[384,1024]{1,0:T(8,128)(2,1)} %collective-permute-done.5.refs_1_, bf16[384,1024]{1,0:T(8,128)(2,1)} %collective-permute-done.6.refs_2_, bf16[384,1024]{1,0:T(8,128)(2,1)S(1)} %copy-done.17, ...), custom_call_target="tpu_custom_call" | custom-call | flops 5234491392 | tf_op jit(solution)/shard_map/backward_part/pallas_call | solution.py:416
  197.8 4.8 %collective-permute-done.36 = bf16[192,128]{1,0:T(8,128)(2,1)S(1)} collective-permute-done((bf16[192,128]{1,0:T(8,128)(2,1)S(1)}, bf16[192,128]{1,0:T(8,128)(2,1)S(1)}, u32[]{:S(2)}, u32[]{:S(2)}) %collective-permute-start.36) | collective-permute-done | bytes 49184 | tf_op jit(solution)/shard_map/ppermute | solution.py:487
  211.5 13.3 %backward_part.7.own_ref = bf16[384,3328]{1,0:T(8,128)(2,1)} custom-call(s32[2]{0:T(128)S(1)} %pad_add_fusion.at_ref, bf16[384,1024]{1,0:T(8,128)(2,1)S(1)} %copy-done.12, bf16[384,1024]{1,0:T(8,128)(2,1)} %collective-permute-done.5.refs_1_, bf16[384,1024]{1,0:T(8,128)(2,1)} %collective-permute-done.6.refs_2_, bf16[384,1024]{1,0:T(8,128)(2,1)S(1)} %copy-done.17, ...), custom_call_target="tpu_custom_call" | custom-call | flops 5234491392 | tf_op jit(solution)/shard_map/backward_part/pallas_call | solution.py:416
  224.8 4.7 %collective-permute-done.41 = bf16[192,128]{1,0:T(8,128)(2,1)S(1)} collective-permute-done((bf16[192,128]{1,0:T(8,128)(2,1)S(1)}, bf16[192,128]{1,0:T(8,128)(2,1)S(1)}, u32[]{:S(2)}, u32[]{:S(2)}) %collective-permute-start.41) | collective-permute-done | bytes 49184 | tf_op jit(solution)/shard_map/ppermute | solution.py:487
  231.9 7.5 %collective-permute-start.42 = (bf16[384,1024]{1,0:T(8,128)(2,1)}, bf16[384,1024]{1,0:T(8,128)(2,1)}, u32[]{:S(2)}, u32[]{:S(2)}) collective-permute-start(bf16[384,1024]{1,0:T(8,128)(2,1)} %last_add.1), channel_id=1, source_target_pairs={{0,0},{1,1},{2,8},{3,9},{4,16},{5,17},{6,24},{7,25},{8,2},{9,3},{1... | collective-permute-start | bytes 2359304 | tf_op jit(solution)/shard_map/ppermute | solution.py:495
  239.5 2.4 term_up.1
  247.1 3.1 %combine.3.refs_2_ = bf16[384,3328]{1,0:T(8,128)(2,1)} custom-call(bf16[384,3328]{1,0:T(8,128)(2,1)S(1)} %copy-done.1, bf16[384,3328]{1,0:T(8,128)(2,1)} %collective-permute-done.39.refs_0_, bf16[144,3328]{1,0:T(8,128)(2,1)S(1)} %copy-done.32, bf16[384,3328]{1,0:T(8,128)(2,1)} %blank.1.refs_2_), custom_call_target="tpu_custom_call", output_to_operand_aliasing={{}: (3, {})} | custom-call | tf_op jit(solution)/shard_map/combine/pallas_call | solution.py:253
  250.2 4.2 %combine.4.refs_2_ = bf16[384,3328]{1,0:T(8,128)(2,1)} custom-call(bf16[384,3328]{1,0:T(8,128)(2,1)S(1)} %copy-done.1, bf16[384,3328]{1,0:T(8,128)(2,1)} %collective-permute-done.39.refs_0_, bf16[144,3328]{1,0:T(8,128)(2,1)} %collective-permute-done.40.refs_1_, bf16[384,3328]{1,0:T(8,128)(2,1)} %combine.3.refs_2_), custom_call_target="tpu_custom_call", output_to_operand_aliasing={{}: (3, {})} | custom-call | tf_op jit(solution)/shard_map/combine/pallas_call | solution.py:253
  254.5 6.2 %factor_grad.1 = bf16[256,3328]{1,0:T(8,128)(2,1)} custom-call(bf16[4,3,128,256]{3,2,1,0:T(8,128)(2,1)S(1)} %get-tuple-element.199.refs_3_.refs_6_.refs_4_.refs_10_.m_ref, bf16[192,128]{1,0:T(8,128)(2,1)S(1)} %add_convert_fusion.2.refs_9_.refs_0_, bf16[192,128]{1,0:T(8,128)(2,1)S(1)} %collective-permute-done.22.refs_9_.refs_1_, ...), custom_call_target="tpu_custom_call" | custom-call | tf_op jit(solution)/shard_map/factor_grad/pallas_call | solution.py:456
  260.6 12.5 %collective-permute-done.45.refs_2_ = bf16[64,1024]{1,0:T(8,128)(2,1)} collective-permute-done((bf16[64,1024]{1,0:T(8,128)(2,1)}, bf16[64,1024]{1,0:T(8,128)(2,1)}, u32[]{:S(2)}, u32[]{:S(2)}) %collective-permute-start.45) | collective-permute-done | bytes 131104 | tf_op jit(solution)/shard_map/ppermute | solution.py:487
  275.3 2.8 up_grad.1
  280.4 2.3 add_convert_fusion
  (231 shorter events, 66.2 us)
Async XLA Ops:
  0.6 24.8 %collective-permute-start.1 = (bf16[384,3328]{1,0:T(8,128)(2,1)}, bf16[384,3328]{1,0:T(8,128)(2,1)}, u32[]{:S(2)}, u32[]{:S(2)}) collective-permute-start(bf16[384,3328]{1,0:T(8,128)(2,1)} %refs_4_.2), channel_id=1, source_target_pairs={{0,8},{8,0},{16,24},{24,16},{1,9},{9,1},{17,25},{25,17},{2,10},{10... | collective-permute-start | bytes 7667720 | tf_op jit(solution)/shard_map/ppermute | solution.py:487
  3.6 21.8 %collective-permute-start = (bf16[384,1024]{1,0:T(8,128)(2,1)S(1)}, bf16[384,1024]{1,0:T(8,128)(2,1)S(1)}, u32[]{:S(2)}, u32[]{:S(2)}) collective-permute-start(bf16[384,1024]{1,0:T(8,128)(2,1)S(1)} %mask.1.grad_ref), channel_id=1, source_target_pairs={{0,0},{1,1},{2,8},{3,9},{4,16},{5,17},{6,24},{7,25},{8,2},{9,3},{1... | collective-permute-start | bytes 2359304 | tf_op jit(solution)/shard_map/ppermute | solution.py:495
  25.5 43.0 %collective-permute-start.7 = (bf16[128,3328]{1,0:T(8,128)(2,1)}, bf16[128,3328]{1,0:T(8,128)(2,1)}, u32[]{:S(2)}, u32[]{:S(2)}) collective-permute-start(bf16[128,3328]{1,0:T(8,128)(2,1)} %get-tuple-element.189), channel_id=1, source_target_pairs={{0,16},{8,24},{16,0},{24,8},{1,17},{9,25},{17,1},{25,9},{2,18},{10... | collective-permute-start | bytes 2555912 | tf_op jit(solution)/shard_map/ppermute | solution.py:487
  46.8 21.6 %collective-permute-start.5 = (bf16[384,1024]{1,0:T(8,128)(2,1)S(1)}, bf16[384,1024]{1,0:T(8,128)(2,1)}, u32[]{:S(2)}, u32[]{:S(2)}) collective-permute-start(bf16[384,1024]{1,0:T(8,128)(2,1)S(1)} %collective-permute-done.refs_0_), channel_id=1, source_target_pairs={{0,2},{2,4},{4,6},{6,7},{7,5},{5,3},{3,1},{1,0},{8,10},{10,12},{12... | collective-permute-start | bytes 2359304 | tf_op jit(solution)/shard_map/ppermute | solution.py:502
  46.8 21.6 %collective-permute-start.6 = (bf16[384,1024]{1,0:T(8,128)(2,1)S(1)}, bf16[384,1024]{1,0:T(8,128)(2,1)}, u32[]{:S(2)}, u32[]{:S(2)}) collective-permute-start(bf16[384,1024]{1,0:T(8,128)(2,1)S(1)} %collective-permute-done.refs_0_), channel_id=1, source_target_pairs={{2,0},{4,2},{6,4},{7,6},{5,7},{3,5},{1,3},{0,1},{10,8},{12,10},{14... | collective-permute-start | bytes 2359304 | tf_op jit(solution)/shard_map/ppermute | solution.py:505
  50.6 17.8 %collective-permute-start.8 = (bf16[192,128]{1,0:T(8,128)(2,1)S(1)}, bf16[192,128]{1,0:T(8,128)(2,1)S(1)}, u32[]{:S(2)}, u32[]{:S(2)}) collective-permute-start(bf16[192,128]{1,0:T(8,128)(2,1)S(1)} %convert_element_type.63), channel_id=1, source_target_pairs={{0,4},{1,5},{2,6},{3,7},{4,0},{5,1},{6,2},{7,3},{8,12},{9,13},{10,... | collective-permute-start | bytes 147464 | tf_op jit(solution)/shard_map/ppermute | solution.py:487
  68.4 21.5 %collective-permute-start.11 = (bf16[128,3328]{1,0:T(8,128)(2,1)S(1)}, bf16[128,3328]{1,0:T(8,128)(2,1)S(1)}, u32[]{:S(2)}, u32[]{:S(2)}) collective-permute-start(bf16[128,3328]{1,0:T(8,128)(2,1)S(1)} %copy-done.58), channel_id=1, source_target_pairs={{0,16},{8,24},{16,0},{24,8},{1,17},{9,25},{17,1},{25,9},{2,18},{10... | collective-permute-start | bytes 2555912 | tf_op jit(solution)/shard_map/ppermute | solution.py:487
  68.7 21.3 %collective-permute-start.12 = (bf16[128,3328]{1,0:T(8,128)(2,1)}, bf16[128,3328]{1,0:T(8,128)(2,1)S(1)}, u32[]{:S(2)}, u32[]{:S(2)}) collective-permute-start(bf16[128,3328]{1,0:T(8,128)(2,1)} %collective-permute-done.7.refs_0_.refs_6_), channel_id=1, source_target_pairs={{0,8},{8,0},{16,24},{24,16},{1,9},{9,1},{17,25},{25,17},{2,10},{10... | collective-permute-start | bytes 2555912 | tf_op jit(solution)/shard_map/ppermute | solution.py:487
  69.0 20.9 %collective-permute-start.10 = (bf16[384,1024]{1,0:T(8,128)(2,1)}, bf16[384,1024]{1,0:T(8,128)(2,1)S(1)}, u32[]{:S(2)}, u32[]{:S(2)}) collective-permute-start(bf16[384,1024]{1,0:T(8,128)(2,1)} %collective-permute-done.6.refs_2_), channel_id=1, source_target_pairs={{2,0},{4,2},{6,4},{7,6},{5,7},{3,5},{1,3},{0,1},{10,8},{12,10},{14... | collective-permute-start | bytes 2359304 | tf_op jit(solution)/shard_map/ppermute | solution.py:505
  70.1 19.9 %collective-permute-start.9 = (bf16[384,1024]{1,0:T(8,128)(2,1)}, bf16[384,1024]{1,0:T(8,128)(2,1)S(1)}, u32[]{:S(2)}, u32[]{:S(2)}) collective-permute-start(bf16[384,1024]{1,0:T(8,128)(2,1)} %collective-permute-done.5.refs_1_), channel_id=1, source_target_pairs={{0,2},{2,4},{4,6},{6,7},{7,5},{5,3},{3,1},{1,0},{8,10},{10,12},{12... | collective-permute-start | bytes 2359304 | tf_op jit(solution)/shard_map/ppermute | solution.py:502
  71.0 18.9 %collective-permute-start.13 = (bf16[192,128]{1,0:T(8,128)(2,1)S(1)}, bf16[192,128]{1,0:T(8,128)(2,1)S(1)}, u32[]{:S(2)}, u32[]{:S(2)}) collective-permute-start(bf16[192,128]{1,0:T(8,128)(2,1)S(1)} %convert_element_type.65), channel_id=1, source_target_pairs={{0,2},{1,3},{2,0},{3,1},{4,6},{5,7},{6,4},{7,5},{8,10},{9,11},{10,... | collective-permute-start | bytes 147464 | tf_op jit(solution)/shard_map/ppermute | solution.py:487
  90.1 23.0 %collective-permute-start.16 = (bf16[128,3328]{1,0:T(8,128)(2,1)S(1)}, bf16[128,3328]{1,0:T(8,128)(2,1)S(1)}, u32[]{:S(2)}, u32[]{:S(2)}) collective-permute-start(bf16[128,3328]{1,0:T(8,128)(2,1)S(1)} %copy-done.57), channel_id=1, source_target_pairs={{0,16},{8,24},{16,0},{24,8},{1,17},{9,25},{17,1},{25,9},{2,18},{10... | collective-permute-start | bytes 2555912 | tf_op jit(solution)/shard_map/ppermute | solution.py:487
  92.0 20.7 %collective-permute-start.14 = (bf16[384,1024]{1,0:T(8,128)(2,1)S(1)}, bf16[384,1024]{1,0:T(8,128)(2,1)S(1)}, u32[]{:S(2)}, u32[]{:S(2)}) collective-permute-start(bf16[384,1024]{1,0:T(8,128)(2,1)S(1)} %collective-permute-done.9.refs_3_), channel_id=1, source_target_pairs={{0,2},{2,4},{4,6},{6,7},{7,5},{5,3},{3,1},{1,0},{8,10},{10,12},{12... | collective-permute-start | bytes 2359304 | tf_op jit(solution)/shard_map/ppermute | solution.py:502
  93.8 19.3 %collective-permute-start.15 = (bf16[384,1024]{1,0:T(8,128)(2,1)S(1)}, bf16[384,1024]{1,0:T(8,128)(2,1)S(1)}, u32[]{:S(2)}, u32[]{:S(2)}) collective-permute-start(bf16[384,1024]{1,0:T(8,128)(2,1)S(1)} %collective-permute-done.10.refs_4_), channel_id=1, source_target_pairs={{2,0},{4,2},{6,4},{7,6},{5,7},{3,5},{1,3},{0,1},{10,8},{12,10},{14... | collective-permute-start | bytes 2359304 | tf_op jit(solution)/shard_map/ppermute | solution.py:505
  131.2 16.8 %collective-permute-start.25 = (bf16[192,1024]{1,0:T(8,128)(2,1)S(1)}, bf16[192,1024]{1,0:T(8,128)(2,1)S(1)}, u32[]{:S(2)}, u32[]{:S(2)}) collective-permute-start(bf16[192,1024]{1,0:T(8,128)(2,1)S(1)} %get-tuple-element.244), channel_id=1, source_target_pairs={{0,2},{2,4},{4,6},{6,7},{7,5},{5,3},{3,1},{1,0},{8,10},{10,12},{12... | collective-permute-start | bytes 1179656 | tf_op jit(solution)/shard_map/ppermute | solution.py:502
  131.6 16.4 %collective-permute-start.26 = (bf16[192,1024]{1,0:T(8,128)(2,1)S(1)}, bf16[192,1024]{1,0:T(8,128)(2,1)S(1)}, u32[]{:S(2)}, u32[]{:S(2)}) collective-permute-start(bf16[192,1024]{1,0:T(8,128)(2,1)S(1)} %get-tuple-element.245), channel_id=1, source_target_pairs={{2,0},{4,2},{6,4},{7,6},{5,7},{3,5},{1,3},{0,1},{10,8},{12,10},{14... | collective-permute-start | bytes 1179656 | tf_op jit(solution)/shard_map/ppermute | solution.py:505
  149.7 24.0 %collective-permute-start.29 = (bf16[384,1024]{1,0:T(8,128)(2,1)}, bf16[384,1024]{1,0:T(8,128)(2,1)S(1)}, u32[]{:S(2)}, u32[]{:S(2)}) collective-permute-start(bf16[384,1024]{1,0:T(8,128)(2,1)} %get-tuple-element.267), channel_id=1, source_target_pairs={{0,2},{2,4},{4,6},{6,7},{7,5},{5,3},{3,1},{1,0},{8,10},{10,12},{12... | collective-permute-start | bytes 2359304 | tf_op jit(solution)/shard_map/ppermute | solution.py:502
  151.1 23.5 %collective-permute-start.30 = (bf16[384,1024]{1,0:T(8,128)(2,1)S(1)}, bf16[384,1024]{1,0:T(8,128)(2,1)S(1)}, u32[]{:S(2)}, u32[]{:S(2)}) collective-permute-start(bf16[384,1024]{1,0:T(8,128)(2,1)S(1)} %get-tuple-element.268), channel_id=1, source_target_pairs={{2,0},{4,2},{6,4},{7,6},{5,7},{3,5},{1,3},{0,1},{10,8},{12,10},{14... | collective-permute-start | bytes 2359304 | tf_op jit(solution)/shard_map/ppermute | solution.py:505
  175.5 28.9 %collective-permute-start.35 = (bf16[144,3328]{1,0:T(8,128)(2,1)}, bf16[144,3328]{1,0:T(8,128)(2,1)S(1)}, u32[]{:S(2)}, u32[]{:S(2)}) collective-permute-start(bf16[144,3328]{1,0:T(8,128)(2,1)} %get-tuple-element.293), channel_id=1, source_target_pairs={{0,16},{8,24},{16,0},{24,8},{1,17},{9,25},{17,1},{25,9},{2,18},{10... | collective-permute-start | bytes 2875400 | tf_op jit(solution)/shard_map/ppermute | solution.py:487
  182.5 20.1 %collective-permute-start.33 = (bf16[384,1024]{1,0:T(8,128)(2,1)S(1)}, bf16[384,1024]{1,0:T(8,128)(2,1)S(1)}, u32[]{:S(2)}, u32[]{:S(2)}) collective-permute-start(bf16[384,1024]{1,0:T(8,128)(2,1)S(1)} %get-tuple-element.290), channel_id=1, source_target_pairs={{0,2},{2,4},{4,6},{6,7},{7,5},{5,3},{3,1},{1,0},{8,10},{10,12},{12... | collective-permute-start | bytes 2359304 | tf_op jit(solution)/shard_map/ppermute | solution.py:502
  182.5 21.0 %collective-permute-start.34 = (bf16[384,1024]{1,0:T(8,128)(2,1)}, bf16[384,1024]{1,0:T(8,128)(2,1)S(1)}, u32[]{:S(2)}, u32[]{:S(2)}) collective-permute-start(bf16[384,1024]{1,0:T(8,128)(2,1)} %get-tuple-element.291), channel_id=1, source_target_pairs={{2,0},{4,2},{6,4},{7,6},{5,7},{3,5},{1,3},{0,1},{10,8},{12,10},{14... | collective-permute-start | bytes 2359304 | tf_op jit(solution)/shard_map/ppermute | solution.py:505
  184.5 18.1 %collective-permute-start.36 = (bf16[192,128]{1,0:T(8,128)(2,1)S(1)}, bf16[192,128]{1,0:T(8,128)(2,1)S(1)}, u32[]{:S(2)}, u32[]{:S(2)}) collective-permute-start(bf16[192,128]{1,0:T(8,128)(2,1)S(1)} %convert_element_type.78), channel_id=1, source_target_pairs={{0,2},{1,3},{2,0},{3,1},{4,6},{5,7},{6,4},{7,5},{8,10},{9,11},{10,... | collective-permute-start | bytes 147464 | tf_op jit(solution)/shard_map/ppermute | solution.py:487
  204.4 25.7 %collective-permute-start.39 = (bf16[384,3328]{1,0:T(8,128)(2,1)}, bf16[384,3328]{1,0:T(8,128)(2,1)}, u32[]{:S(2)}, u32[]{:S(2)}) collective-permute-start(bf16[384,3328]{1,0:T(8,128)(2,1)} %backward_part.6), channel_id=1, source_target_pairs={{0,8},{8,0},{16,24},{24,16},{1,9},{9,1},{17,25},{25,17},{2,10},{10... | collective-permute-start | bytes 7667720 | tf_op jit(solution)/shard_map/ppermute | solution.py:487
  204.4 25.7 %collective-permute-start.40 = (bf16[144,3328]{1,0:T(8,128)(2,1)}, bf16[144,3328]{1,0:T(8,128)(2,1)}, u32[]{:S(2)}, u32[]{:S(2)}) collective-permute-start(bf16[144,3328]{1,0:T(8,128)(2,1)} %get-tuple-element.312), channel_id=1, source_target_pairs={{0,16},{8,24},{16,0},{24,8},{1,17},{9,25},{17,1},{25,9},{2,18},{10... | collective-permute-start | bytes 2875400 | tf_op jit(solution)/shard_map/ppermute | solution.py:487
  208.9 20.7 %collective-permute-start.37 = (bf16[384,1024]{1,0:T(8,128)(2,1)S(1)}, bf16[384,1024]{1,0:T(8,128)(2,1)S(1)}, u32[]{:S(2)}, u32[]{:S(2)}) collective-permute-start(bf16[384,1024]{1,0:T(8,128)(2,1)S(1)} %get-tuple-element.308), channel_id=1, source_target_pairs={{0,2},{2,4},{4,6},{6,7},{7,5},{5,3},{3,1},{1,0},{8,10},{10,12},{12... | collective-permute-start | bytes 2359304 | tf_op jit(solution)/shard_map/ppermute | solution.py:502
  209.0 21.2 %collective-permute-start.38 = (bf16[384,1024]{1,0:T(8,128)(2,1)}, bf16[384,1024]{1,0:T(8,128)(2,1)S(1)}, u32[]{:S(2)}, u32[]{:S(2)}) collective-permute-start(bf16[384,1024]{1,0:T(8,128)(2,1)} %get-tuple-element.309), channel_id=1, source_target_pairs={{2,0},{4,2},{6,4},{7,6},{5,7},{3,5},{1,3},{0,1},{10,8},{12,10},{14... | collective-permute-start | bytes 2359304 | tf_op jit(solution)/shard_map/ppermute | solution.py:505
  210.9 18.6 %collective-permute-start.41 = (bf16[192,128]{1,0:T(8,128)(2,1)S(1)}, bf16[192,128]{1,0:T(8,128)(2,1)S(1)}, u32[]{:S(2)}, u32[]{:S(2)}) collective-permute-start(bf16[192,128]{1,0:T(8,128)(2,1)S(1)} %convert_element_type.80), channel_id=1, source_target_pairs={{0,1},{1,0},{2,3},{3,2},{4,5},{5,4},{6,7},{7,6},{8,9},{9,8},{10,11... | collective-permute-start | bytes 147464 | tf_op jit(solution)/shard_map/ppermute | solution.py:487
  231.9 46.2 %collective-permute-start.42 = (bf16[384,1024]{1,0:T(8,128)(2,1)}, bf16[384,1024]{1,0:T(8,128)(2,1)}, u32[]{:S(2)}, u32[]{:S(2)}) collective-permute-start(bf16[384,1024]{1,0:T(8,128)(2,1)} %last_add.1), channel_id=1, source_target_pairs={{0,0},{1,1},{2,8},{3,9},{4,16},{5,17},{6,24},{7,25},{8,2},{9,3},{1... | collective-permute-start | bytes 2359304 | tf_op jit(solution)/shard_map/ppermute | solution.py:495
  239.4 38.7 %collective-permute-start.43 = (bf16[96,3328]{1,0:T(8,128)(2,1)}, bf16[96,3328]{1,0:T(8,128)(2,1)}, u32[]{:S(2)}, u32[]{:S(2)}) collective-permute-start(bf16[96,3328]{1,0:T(8,128)(2,1)} %get-tuple-element.330), channel_id=1, source_target_pairs={{0,16},{8,24},{16,0},{24,8},{1,17},{9,25},{17,1},{25,9},{2,18},{10... | collective-permute-start | bytes 1916936 | tf_op jit(solution)/shard_map/ppermute | solution.py:487
  243.7 16.9 %collective-permute-start.44 = (bf16[64,1024]{1,0:T(8,128)(2,1)}, bf16[64,1024]{1,0:T(8,128)(2,1)}, u32[]{:S(2)}, u32[]{:S(2)}) collective-permute-start(bf16[64,1024]{1,0:T(8,128)(2,1)} %get-tuple-element.334), channel_id=1, source_target_pairs={{0,8},{8,0},{16,24},{24,16},{1,9},{9,1},{17,25},{25,17},{2,10},{10... | collective-permute-start | bytes 393224 | tf_op jit(solution)/shard_map/ppermute | solution.py:487
  243.7 29.4 %collective-permute-start.45 = (bf16[64,1024]{1,0:T(8,128)(2,1)}, bf16[64,1024]{1,0:T(8,128)(2,1)}, u32[]{:S(2)}, u32[]{:S(2)}) collective-permute-start(bf16[64,1024]{1,0:T(8,128)(2,1)} %get-tuple-element.335), channel_id=1, source_target_pairs={{0,16},{8,24},{16,0},{24,8},{1,17},{9,25},{17,1},{25,9},{2,18},{10... | collective-permute-start | bytes 393224 | tf_op jit(solution)/shard_map/ppermute | solution.py:487
  245.7 29.6 %collective-permute-start.46 = (bf16[64,1024]{1,0:T(8,128)(2,1)}, bf16[64,1024]{1,0:T(8,128)(2,1)}, u32[]{:S(2)}, u32[]{:S(2)}) collective-permute-start(bf16[64,1024]{1,0:T(8,128)(2,1)} %get-tuple-element.336), channel_id=1, source_target_pairs={{0,24},{8,16},{16,8},{24,0},{1,25},{9,17},{17,9},{25,1},{2,26},{10... | collective-permute-start | bytes 393224 | tf_op jit(solution)/shard_map/ppermute | solution.py:487
  (76 other events, 744.5 us)

commit v6 on v5

--- a/solution.py
+++ b/solution.py
@@ -101,7 +101,7 @@
         rows = slice(b * BLK, (b + 1) * BLK)
         act = down_act[b * rank : (b + 1) * rank]
         branch = lax.dot_general(act, block_ref[b], FIRSTS, preferred_element_type=F32)
-        branch_ref[rows, :] = jnp.where(row + b * BLK < live_ref[dp], branch, 0.0)
+        branch_ref[rows, :] = jnp.where(row + b * BLK < live_ref[dp], branch, 0.0).astype(BF16)
         term = jnp.dot(act, grad_ref[rows, :], preferred_element_type=F32).astype(BF16)
         owner = (id_ref[dp * blocks + b] // owned) ^ dp
         for r in range(n_dp):
@@ -246,7 +246,7 @@
 
 def combine(start, own, near, arrived, out):
     rows, units = own.shape
-    tile = 48
+    tile = 32
     first = start // tile
     placed = pl.BlockSpec((tile, units), lambda i: (i + first, 0))
     piece = pl.BlockSpec((tile, units), lambda i: (i, 0))
@@ -544,12 +544,14 @@
     turned_factor = jnp.transpose(adapter_down, (0, 2, 1)).reshape(owned * rank, units)
     factor = turned_factor.T
     hidden_cut = [hidden[a:b] for a, b in zip(cuts, cuts[1:])]
-    swapped, near, arrived_up, factor, masks, hidden, hidden_cut = fence(
-        swapped, near, arrived_up, factor, masks, hidden, hidden_cut
-    )
-
     def forward(groups, span, hids, total):
         return forward_part(groups, span, hids, down_weight, factor, masks, total, q, rank)
+
+    total, own = forward((0, 1), (0, blocks), [hidden], None)
+    picked = {0: [own[0]]}
+    swapped, near, arrived_up, hidden, hidden_cut, total, picked = fence(
+        swapped, near, arrived_up, hidden, hidden_cut, total, picked
+    )
 
     def forward_pairs(span, piece, total):
         for r in evens:
@@ -562,7 +564,6 @@
     offsets = [0] + [sign * step for step in range(1, half) for sign in (-1, 1)] + [half]
     ahead = behind = swapped
     ring_blocks = [swapped]
-    picked = {}
     ahead, behind = onward(ahead), backward_on(behind)
     fetched = [fetch(hidden_cut, 0)]
     up_sum, block_up = call(
@@ -572,12 +573,9 @@
         [masked_grad, *arrived_up],
         [like((blocks * rank, BLK), F32), like((blocks, rank, width), BF16)],
     )
-    up_sum, hidden = fence(up_sum, hidden)
     up_sum = sum_step(up_sum, 0)
-    total, own = forward((0, 1), (0, blocks), [hidden], None)
-    picked[0] = [own[0]]
-    ahead, behind, fetched[0], total, up_sum, hidden_cut = fence(
-        ahead, behind, fetched[0], total, up_sum, hidden_cut
+    ahead, behind, fetched[0], total, near, up_sum, hidden_cut = fence(
+        ahead, behind, fetched[0], total, near, up_sum, hidden_cut
     )
     ring_blocks += [ahead, behind]
     ahead, behind = onward(ahead), backward_on(behind)
@@ -631,7 +629,7 @@
         ahead, behind, *others = fence(ahead, behind, *others)
         return onward(ahead), backward_on(behind), *others
 
-    ends = [0, 3 * rows // 8, 3 * rows // 4, rows]
+    ends = [0, 5 * rows // 12, 5 * rows // 6, rows]
     pieces = [b - a for a, b in zip(ends, ends[1:])]
 
     def partial_gradient(piece, parts):
@@ -699,7 +697,7 @@
         "term_up",
         [at, adapter_per_block, live_rows],
         [down_sum, masked_grad, block_up],
-        [like((rows, width), F32)] + [like((rank, width), BF16)] * n_dp,
+        [like((rows, width), BF16)] + [like((rank, width), BF16)] * n_dp,
     )
     terms = [exchange(terms[r], r) if r else terms[0] for r in range(n_dp)]
     arriving.append(partial_gradient(2, parts))
@@ -723,7 +721,7 @@
     )
     base_out, arriving[2], up_grad = fence(base_out, arriving[2], up_grad)
     hidden_gradient = combine(ends[2], parts[0], parts[1], arriving[2], hidden_gradient)
-    layer_out = (base_out.astype(F32) + branch).astype(BF16)
+    layer_out = (base_out.astype(F32) + branch.astype(F32)).astype(BF16)
     return layer_out, hidden_gradient, down_grad, up_grad
 
 

time: 284 us -> 278 us (0.979)
  starting transfers between devices: 70.1 us -> 59.5 us
  waiting for transfers between devices: 52.5 us -> 60.9 us
  local copies, waits for them, and re-layouts: 29.2 us -> 22.6 us
  Pallas kernels: 127 us -> 130 us
    ppermute x29, starting transfers between devices: 45.5 us -> 33.7 us  [exchange(): return lax.ppermute(value, axis, [(i, i ^ bit) for i in range(count)])]
    ppermute x29, waiting for transfers between devices: 51.5 us -> 60.5 us  [exchange(): return lax.ppermute(value, axis, [(i, i ^ bit) for i in range(count)])]
    unnamed x122 -> x114, local copies, waits for them, and re-layouts: 23.6 us -> 16.9 us
    pallas_call x5, Pallas kernels: 7.46 us -> 11.4 us  [call(): pl.pallas_call(kernel, grid_spec=pltpu.PrefetchScalarGridSpec(num_scalar_...]
  transfers between devices with their start and end apart: 47 -> 47, of which waited for: 14 -> 13; matrix products, arithmetic and copies ran while one was open for 2% -> 2% of each run, Pallas kernels for 43% -> 45%
where the time goes in v6:
time: 278 us; the launch traced here: 277 us
  Pallas kernels  130 us (47%)
  waiting for transfers between devices  60.9 us (22%)
  starting transfers between devices  59.5 us (21%)
  local copies, waits for them, and re-layouts  22.6 us (8%)
    ppermute x29, waiting for transfers between devices, exchange(): return lax.ppermute(value, axis, [(i, i ^ bit) for i in range(count)])  60.5 us
    pallas_call x4, Pallas kernels, backward_part(): pl.pallas_call(functools.partial(backward_kernel, group, n_mp, offsets, l...  51 us
    pallas_call x4, Pallas kernels, forward_part(): pl.pallas_call(functools.partial(forward_kernel, len(hids)), grid=(cols /...  43.7 us
    ppermute x29, starting transfers between devices, exchange(): return lax.ppermute(value, axis, [(i, i ^ bit) for i in range(count)])  33.7 us
    unnamed x114, local copies, waits for them, and re-layouts  16.9 us
    ppermute x8, starting transfers between devices, backward_on(): return lax.ppermute(value, 'mp', down_ring)  11.6 us
    pallas_call x5, Pallas kernels, call(): pl.pallas_call(kernel, grid_spec=pltpu.PrefetchScalarGridSpec(num_scalar_...  11.4 us
    pallas_call x3, Pallas kernels, combine(): pl.pallas_call(combine_kernel, grid=(arrived[0].shape[0] // tile,), in_sp...  11.3 us
  transfers between devices with their start and end apart: 47, of which 13 were waited for; matrix products, arithmetic and copies ran while one was open for 2% of the time, Pallas kernels for 45%

profile of v6, /device:TPU:0, one launch (start us, length us, event | category | flops | bytes accessed | tf_op | source)
XLA Modules:
  0.0 276.5 jit_solution(16999596341712033966)
XLA Ops:
  9.3 2.8 %collective-permute-start.2 = (bf16[64,1024]{1,0:T(8,128)(2,1)}, bf16[64,1024]{1,0:T(8,128)(2,1)}, u32[]{:S(2)}, u32[]{:S(2)}) collective-permute-start(bf16[64,1024]{1,0:T(8,128)(2,1)} %get-tuple-element.183), channel_id=1, source_target_pairs={{0,8},{8,0},{16,24},{24,16},{1,9},{9,1},{17,25},{25,17},{2,10},{10... | collective-permute-start | bytes 393224 | tf_op jit(solution)/shard_map/ppermute | solution.py:487
  12.1 3.5 %collective-permute-start.3 = (bf16[64,1024]{1,0:T(8,128)(2,1)}, bf16[64,1024]{1,0:T(8,128)(2,1)}, u32[]{:S(2)}, u32[]{:S(2)}) collective-permute-start(bf16[64,1024]{1,0:T(8,128)(2,1)} %get-tuple-element.184), channel_id=1, source_target_pairs={{0,16},{8,24},{16,0},{24,8},{1,17},{9,25},{17,1},{25,9},{2,18},{10... | collective-permute-start | bytes 393224 | tf_op jit(solution)/shard_map/ppermute | solution.py:487
  15.6 3.3 %fusion = (bf16[128,3328]{1,0:T(8,128)(2,1)}, bf16[128,3328]{1,0:T(8,128)(2,1)}, bf16[128,3328]{1,0:T(8,128)(2,1)}) fusion(bf16[384,3328]{1,0:T(8,128)(2,1)} %refs_4_.2), kind=kLoop, calls=%fused_computation.15 | loop fusion | bytes 5111808 | tf_op jit(solution)/shard_map/slice | solution.py:546
  19.0 2.2 copy.17.refs_2_.refs_5_.refs_3_
  24.4 10.7 %forward_part.4 = (bf16[4,2,3,128,1024]{4,3,2,1,0:T(8,128)(2,1)}, bf16[1,192,128]{2,1,0:T(8,128)(2,1)S(1)}) custom-call(bf16[384,3328]{1,0:T(8,128)(2,1)S(1)} %copy-done.6, bf16[3328,2048]{1,0:T(8,128)(2,1)} %refs_11_.7, bf16[3328,256]{1,0:T(8,128)(2,1)S(1)} %copy-done.4, bf16[4,3,128,256]{3,2,1,0:T(8,128)(2,1)S(1)} %get-tuple-element.186.refs_3_.refs_6_.refs_4_.refs_10_.m_ref), custom_call_target="tpu_custom_call" | custom-call | flops 5234491392 | tf_op jit(solution)/shard_map/forward_part/pallas_call | solution.py:328
  35.2 12.7 %collective-permute-start.7 = (bf16[128,3328]{1,0:T(8,128)(2,1)S(1)}, bf16[128,3328]{1,0:T(8,128)(2,1)S(1)}, u32[]{:S(2)}, u32[]{:S(2)}) collective-permute-start(bf16[128,3328]{1,0:T(8,128)(2,1)S(1)} %copy-done.54), channel_id=1, source_target_pairs={{0,16},{8,24},{16,0},{24,8},{1,17},{9,25},{17,1},{25,9},{2,18},{10... | collective-permute-start | bytes 2555912 | tf_op jit(solution)/shard_map/ppermute | solution.py:487
  52.3 17.2 %collective-permute-done.8 = bf16[192,128]{1,0:T(8,128)(2,1)S(1)} collective-permute-done((bf16[192,128]{1,0:T(8,128)(2,1)S(1)}, bf16[192,128]{1,0:T(8,128)(2,1)S(1)}, u32[]{:S(2)}, u32[]{:S(2)}) %collective-permute-start.8) | collective-permute-done | bytes 49184 | tf_op jit(solution)/shard_map/ppermute | solution.py:487
  72.3 11.5 %forward_part.5 = (bf16[4,2,3,128,1024]{4,3,2,1,0:T(8,128)(2,1)}, bf16[1,192,128]{2,1,0:T(8,128)(2,1)S(1)}) custom-call(bf16[384,3328]{1,0:T(8,128)(2,1)} %collective-permute-done.1.refs_0_.refs_5_, bf16[3328,2048]{1,0:T(8,128)(2,1)} %refs_11_.7, bf16[3328,256]{1,0:T(8,128)(2,1)S(1)} %copy-done.5, ...), custom_call_target="tpu_custom_call", output_to_operand_aliasing={{0}: (4, {})} | custom-call | flops 5234491392 | tf_op jit(solution)/shard_map/forward_part/pallas_call | solution.py:328
  83.8 7.2 %collective-permute-done.13 = bf16[192,128]{1,0:T(8,128)(2,1)S(1)} collective-permute-done((bf16[192,128]{1,0:T(8,128)(2,1)S(1)}, bf16[192,128]{1,0:T(8,128)(2,1)S(1)}, u32[]{:S(2)}, u32[]{:S(2)}) %collective-permute-start.13) | collective-permute-done | bytes 49184 | tf_op jit(solution)/shard_map/ppermute | solution.py:487
  95.0 12.5 %forward_part.6 = (bf16[4,2,3,128,1024]{4,3,2,1,0:T(8,128)(2,1)}, bf16[2,128,128]{2,1,0:T(8,128)(2,1)S(1)}) custom-call(bf16[128,3328]{1,0:T(8,128)(2,1)S(1)} %collective-permute-done.7.refs_0_.refs_6_, bf16[128,3328]{1,0:T(8,128)(2,1)S(1)} %collective-permute-done.11.refs_1_.refs_7_, ...), custom_call_target="tpu_custom_call", output_to_operand_aliasing={{0}: (7, {})} | custom-call | flops 6979321856 | tf_op jit(solution)/shard_map/forward_part/pallas_call | solution.py:328
  107.6 6.0 %collective-permute-done.18 = bf16[192,128]{1,0:T(8,128)(2,1)S(1)} collective-permute-done((bf16[192,128]{1,0:T(8,128)(2,1)S(1)}, bf16[192,128]{1,0:T(8,128)(2,1)S(1)}, u32[]{:S(2)}, u32[]{:S(2)}) %collective-permute-start.18) | collective-permute-done | bytes 49184 | tf_op jit(solution)/shard_map/ppermute | solution.py:487
  118.4 9.1 %forward_part.7 = (bf16[4,2,3,128,1024]{4,3,2,1,0:T(8,128)(2,1)}, bf16[2,64,128]{2,1,0:T(8,128)(2,1)S(1)}) custom-call(bf16[128,3328]{1,0:T(8,128)(2,1)S(1)} %collective-permute-done.16.refs_0_.refs_8_, bf16[128,3328]{1,0:T(8,128)(2,1)S(1)} %collective-permute-done.21.refs_1_.refs_11_, bf16[3328,2048]{1,0:T(8,128)(2,1)} %refs_11_.7, ...), custom_call_target="tpu_custom_call", output_to_operand_aliasing={{0}: (5, {})} | custom-call | flops 3489660928 | tf_op jit(solution)/shard_map/forward_part/pallas_call | solution.py:328
  128.9 2.8 %copy-done = bf16[4,2,3,128,1024]{4,3,2,1,0:T(8,128)(2,1)S(1)} copy-done((bf16[4,2,3,128,1024]{4,3,2,1,0:T(8,128)(2,1)S(1)}, bf16[4,2,3,128,1024]{4,3,2,1,0:T(8,128)(2,1)}, u32[]{:S(2)}) %copy-start) | copy-done | bytes 6291480
  138.5 12.8 %backward_part.4 = bf16[384,3328]{1,0:T(8,128)(2,1)} custom-call(s32[2]{0:T(128)S(1)} %pad_add_fusion.at_ref, bf16[384,1024]{1,0:T(8,128)(2,1)S(1)} %copy-done.11, bf16[384,1024]{1,0:T(8,128)(2,1)S(1)} %collective-permute-done.5.refs_1_, bf16[384,1024]{1,0:T(8,128)(2,1)S(1)} %copy-done.16, bf16[384,1024]{1,0:T(8,128)(2,1)S(1)} %copy-done.20, ...), custom_call_target="tpu_custom_call" | custom-call | flops 5234491392 | tf_op jit(solution)/shard_map/backward_part/pallas_call | solution.py:416
  155.1 3.1 %collective-permute-done.31.refs_13_ = bf16[384,3328]{1,0:T(8,128)(2,1)} collective-permute-done((bf16[384,3328]{1,0:T(8,128)(2,1)}, bf16[384,3328]{1,0:T(8,128)(2,1)}, u32[]{:S(2)}, u32[]{:S(2)}) %collective-permute-start.31) | collective-permute-done | bytes 2555936 | tf_op jit(solution)/shard_map/ppermute | solution.py:487
  158.2 13.1 %backward_part.5 = (bf16[160,3328]{1,0:T(8,128)(2,1)}, bf16[160,3328]{1,0:T(8,128)(2,1)}, bf16[64,3328]{1,0:T(8,128)(2,1)}) custom-call(s32[2]{0:T(128)S(1)} %pad_add_fusion.at_ref, bf16[384,1024]{1,0:T(8,128)(2,1)S(1)} %copy-done.12, bf16[384,1024]{1,0:T(8,128)(2,1)S(1)} %copy-done.14, bf16[384,1024]{1,0:T(8,128)(2,1)S(1)} %copy-done.16, ...), custom_call_target="tpu_custom_call" | custom-call | flops 20937965568 | tf_op jit(solution)/shard_map/backward_part/pallas_call | solution.py:416
  173.2 3.8 %collective-permute-done.32 = bf16[192,128]{1,0:T(8,128)(2,1)S(1)} collective-permute-done((bf16[192,128]{1,0:T(8,128)(2,1)S(1)}, bf16[192,128]{1,0:T(8,128)(2,1)S(1)}, u32[]{:S(2)}, u32[]{:S(2)}) %collective-permute-start.32) | collective-permute-done | bytes 49184 | tf_op jit(solution)/shard_map/ppermute | solution.py:487
  181.9 12.5 %backward_part.6 = bf16[384,3328]{1,0:T(8,128)(2,1)} custom-call(s32[2]{0:T(128)S(1)} %pad_add_fusion.at_ref, bf16[384,1024]{1,0:T(8,128)(2,1)S(1)} %copy-done.12, bf16[384,1024]{1,0:T(8,128)(2,1)S(1)} %copy-done.14, bf16[384,1024]{1,0:T(8,128)(2,1)S(1)} %copy-done.16, bf16[384,1024]{1,0:T(8,128)(2,1)S(1)} %copy-done.20, bf16[384,1024]{1,0:T(8,128)(2,1)S(1)} %copy-done.18, ...), custom_call_target="tpu_custom_call" | custom-call | flops 5234491392 | tf_op jit(solution)/shard_map/backward_part/pallas_call | solution.py:416
  194.4 5.5 %collective-permute-done.36 = bf16[192,128]{1,0:T(8,128)(2,1)S(1)} collective-permute-done((bf16[192,128]{1,0:T(8,128)(2,1)S(1)}, bf16[192,128]{1,0:T(8,128)(2,1)S(1)}, u32[]{:S(2)}, u32[]{:S(2)}) %collective-permute-start.36) | collective-permute-done | bytes 49184 | tf_op jit(solution)/shard_map/ppermute | solution.py:487
  200.0 2.5 collective-permute-done.35.refs_1_
  208.5 12.6 %backward_part.7.own_ref = bf16[384,3328]{1,0:T(8,128)(2,1)} custom-call(s32[2]{0:T(128)S(1)} %pad_add_fusion.at_ref, bf16[384,1024]{1,0:T(8,128)(2,1)S(1)} %copy-done.12, bf16[384,1024]{1,0:T(8,128)(2,1)S(1)} %copy-done.14, bf16[384,1024]{1,0:T(8,128)(2,1)S(1)} %copy-done.16, bf16[384,1024]{1,0:T(8,128)(2,1)S(1)} %copy-done.20, ...), custom_call_target="tpu_custom_call" | custom-call | flops 5234491392 | tf_op jit(solution)/shard_map/backward_part/pallas_call | solution.py:416
  221.1 4.9 %collective-permute-done.41 = bf16[192,128]{1,0:T(8,128)(2,1)S(1)} collective-permute-done((bf16[192,128]{1,0:T(8,128)(2,1)S(1)}, bf16[192,128]{1,0:T(8,128)(2,1)S(1)}, u32[]{:S(2)}, u32[]{:S(2)}) %collective-permute-start.41) | collective-permute-done | bytes 49184 | tf_op jit(solution)/shard_map/ppermute | solution.py:487
  226.1 2.7 collective-permute-done.40.refs_1_
  230.5 7.6 %collective-permute-start.42 = (bf16[384,1024]{1,0:T(8,128)(2,1)}, bf16[384,1024]{1,0:T(8,128)(2,1)}, u32[]{:S(2)}, u32[]{:S(2)}) collective-permute-start(bf16[384,1024]{1,0:T(8,128)(2,1)} %last_add.1), channel_id=1, source_target_pairs={{0,0},{1,1},{2,8},{3,9},{4,16},{5,17},{6,24},{7,25},{8,2},{9,3},{1... | collective-permute-start | bytes 2359304 | tf_op jit(solution)/shard_map/ppermute | solution.py:495
  238.1 3.6 %term_up.1 = (bf16[384,1024]{1,0:T(8,128)(2,1)S(1)}, bf16[64,1024]{1,0:T(8,128)(2,1)S(1)}, bf16[64,1024]{1,0:T(8,128)(2,1)}, bf16[64,1024]{1,0:T(8,128)(2,1)}, bf16[64,1024]{1,0:T(8,128)(2,1)}) custom-call(s32[2]{0:T(128)S(1)} %pad_add_fusion.at_ref, s32[12]{0:T(128)S(1)} %copy-done.49, s32[4]{0:T(128)S(1)} %copy-done.51, ...), custom_call_target="tpu_custom_call" | custom-call | tf_op jit(solution)/shard_map/term_up/pallas_call | solution.py:34
  246.6 4.0 %combine.3.refs_2_ = bf16[384,3328]{1,0:T(8,128)(2,1)} custom-call(bf16[384,3328]{1,0:T(8,128)(2,1)S(1)} %copy-done.1, bf16[384,3328]{1,0:T(8,128)(2,1)} %collective-permute-done.39.refs_0_, bf16[160,3328]{1,0:T(8,128)(2,1)S(1)} %copy-done.31, bf16[384,3328]{1,0:T(8,128)(2,1)} %blank.1.refs_2_), custom_call_target="tpu_custom_call", output_to_operand_aliasing={{}: (3, {})} | custom-call | tf_op jit(solution)/shard_map/combine/pallas_call | solution.py:253
  250.6 5.3 %combine.4.refs_2_ = bf16[384,3328]{1,0:T(8,128)(2,1)} custom-call(bf16[384,3328]{1,0:T(8,128)(2,1)S(1)} %copy-done.1, bf16[384,3328]{1,0:T(8,128)(2,1)} %collective-permute-done.39.refs_0_, bf16[160,3328]{1,0:T(8,128)(2,1)} %collective-permute-done.40.refs_1_, bf16[384,3328]{1,0:T(8,128)(2,1)} %combine.3.refs_2_), custom_call_target="tpu_custom_call", output_to_operand_aliasing={{}: (3, {})} | custom-call | tf_op jit(solution)/shard_map/combine/pallas_call | solution.py:253
  255.9 6.0 %factor_grad.1 = bf16[256,3328]{1,0:T(8,128)(2,1)} custom-call(bf16[4,3,128,256]{3,2,1,0:T(8,128)(2,1)S(1)} %get-tuple-element.186.refs_3_.refs_6_.refs_4_.refs_10_.m_ref, bf16[192,128]{1,0:T(8,128)(2,1)S(1)} %add_convert_fusion.2.refs_9_.refs_0_, bf16[192,128]{1,0:T(8,128)(2,1)S(1)} %collective-permute-done.22.refs_9_.refs_1_, ...), custom_call_target="tpu_custom_call" | custom-call | tf_op jit(solution)/shard_map/factor_grad/pallas_call | solution.py:456
  262.0 3.2 %collective-permute-done.45.refs_2_ = bf16[64,1024]{1,0:T(8,128)(2,1)} collective-permute-done((bf16[64,1024]{1,0:T(8,128)(2,1)}, bf16[64,1024]{1,0:T(8,128)(2,1)}, u32[]{:S(2)}, u32[]{:S(2)}) %collective-permute-start.45) | collective-permute-done | bytes 131104 | tf_op jit(solution)/shard_map/ppermute | solution.py:487
  265.2 4.1 %collective-permute-done.46.refs_3_ = bf16[64,1024]{1,0:T(8,128)(2,1)} collective-permute-done((bf16[64,1024]{1,0:T(8,128)(2,1)}, bf16[64,1024]{1,0:T(8,128)(2,1)}, u32[]{:S(2)}, u32[]{:S(2)}) %collective-permute-start.46) | collective-permute-done | bytes 131104 | tf_op jit(solution)/shard_map/ppermute | solution.py:487
  269.3 2.8 %up_grad.1 = bf16[4,64,1024]{2,1,0:T(8,128)(2,1)} custom-call(s32[2]{0:T(128)S(1)} %pad_add_fusion.at_ref, s32[12]{0:T(128)S(1)} %copy-done.49, bf16[64,1024]{1,0:T(8,128)(2,1)S(1)} %copy-done.47, bf16[64,1024]{1,0:T(8,128)(2,1)} %collective-permute-done.44.refs_1_, bf16[64,1024]{1,0:T(8,128)(2,1)} %collective-permute-done.45.refs_2_, ...), custom_call_target="tpu_custom_call" | custom-call | tf_op jit(solution)/shard_map/up_grad/pallas_call | solution.py:34
  274.2 2.3 add_convert_fusion
  (223 shorter events, 61.1 us)
Async XLA Ops:
  0.6 34.5 %collective-permute-start.1 = (bf16[384,3328]{1,0:T(8,128)(2,1)}, bf16[384,3328]{1,0:T(8,128)(2,1)}, u32[]{:S(2)}, u32[]{:S(2)}) collective-permute-start(bf16[384,3328]{1,0:T(8,128)(2,1)} %refs_4_.2), channel_id=1, source_target_pairs={{0,8},{8,0},{16,24},{24,16},{1,9},{9,1},{17,25},{25,17},{2,10},{10... | collective-permute-start | bytes 7667720 | tf_op jit(solution)/shard_map/ppermute | solution.py:487
  4.5 30.6 %collective-permute-start = (bf16[384,1024]{1,0:T(8,128)(2,1)}, bf16[384,1024]{1,0:T(8,128)(2,1)S(1)}, u32[]{:S(2)}, u32[]{:S(2)}) collective-permute-start(bf16[384,1024]{1,0:T(8,128)(2,1)} %mask.1.grad_ref), channel_id=1, source_target_pairs={{0,0},{1,1},{2,8},{3,9},{4,16},{5,17},{6,24},{7,25},{8,2},{9,3},{1... | collective-permute-start | bytes 2359304 | tf_op jit(solution)/shard_map/ppermute | solution.py:495
  9.3 25.8 %collective-permute-start.2 = (bf16[64,1024]{1,0:T(8,128)(2,1)}, bf16[64,1024]{1,0:T(8,128)(2,1)}, u32[]{:S(2)}, u32[]{:S(2)}) collective-permute-start(bf16[64,1024]{1,0:T(8,128)(2,1)} %get-tuple-element.183), channel_id=1, source_target_pairs={{0,8},{8,0},{16,24},{24,16},{1,9},{9,1},{17,25},{25,17},{2,10},{10... | collective-permute-start | bytes 393224 | tf_op jit(solution)/shard_map/ppermute | solution.py:487
  12.1 23.0 %collective-permute-start.3 = (bf16[64,1024]{1,0:T(8,128)(2,1)}, bf16[64,1024]{1,0:T(8,128)(2,1)}, u32[]{:S(2)}, u32[]{:S(2)}) collective-permute-start(bf16[64,1024]{1,0:T(8,128)(2,1)} %get-tuple-element.184), channel_id=1, source_target_pairs={{0,16},{8,24},{16,0},{24,8},{1,17},{9,25},{17,1},{25,9},{2,18},{10... | collective-permute-start | bytes 393224 | tf_op jit(solution)/shard_map/ppermute | solution.py:487
  15.6 19.5 %collective-permute-start.4 = (bf16[64,1024]{1,0:T(8,128)(2,1)}, bf16[64,1024]{1,0:T(8,128)(2,1)}, u32[]{:S(2)}, u32[]{:S(2)}) collective-permute-start(bf16[64,1024]{1,0:T(8,128)(2,1)} %get-tuple-element.185), channel_id=1, source_target_pairs={{0,24},{8,16},{16,8},{24,0},{1,25},{9,17},{17,9},{25,1},{2,26},{10... | collective-permute-start | bytes 393224 | tf_op jit(solution)/shard_map/ppermute | solution.py:487
  35.2 34.4 %collective-permute-start.7 = (bf16[128,3328]{1,0:T(8,128)(2,1)S(1)}, bf16[128,3328]{1,0:T(8,128)(2,1)S(1)}, u32[]{:S(2)}, u32[]{:S(2)}) collective-permute-start(bf16[128,3328]{1,0:T(8,128)(2,1)S(1)} %copy-done.54), channel_id=1, source_target_pairs={{0,16},{8,24},{16,0},{24,8},{1,17},{9,25},{17,1},{25,9},{2,18},{10... | collective-permute-start | bytes 2555912 | tf_op jit(solution)/shard_map/ppermute | solution.py:487
  47.9 21.7 %collective-permute-start.5 = (bf16[384,1024]{1,0:T(8,128)(2,1)S(1)}, bf16[384,1024]{1,0:T(8,128)(2,1)S(1)}, u32[]{:S(2)}, u32[]{:S(2)}) collective-permute-start(bf16[384,1024]{1,0:T(8,128)(2,1)S(1)} %collective-permute-done.refs_0_), channel_id=1, source_target_pairs={{0,2},{2,4},{4,6},{6,7},{7,5},{5,3},{3,1},{1,0},{8,10},{10,12},{12... | collective-permute-start | bytes 2359304 | tf_op jit(solution)/shard_map/ppermute | solution.py:502
  48.0 21.6 %collective-permute-start.6 = (bf16[384,1024]{1,0:T(8,128)(2,1)S(1)}, bf16[384,1024]{1,0:T(8,128)(2,1)S(1)}, u32[]{:S(2)}, u32[]{:S(2)}) collective-permute-start(bf16[384,1024]{1,0:T(8,128)(2,1)S(1)} %collective-permute-done.refs_0_), channel_id=1, source_target_pairs={{2,0},{4,2},{6,4},{7,6},{5,7},{3,5},{1,3},{0,1},{10,8},{12,10},{14... | collective-permute-start | bytes 2359304 | tf_op jit(solution)/shard_map/ppermute | solution.py:505
  69.6 21.4 %collective-permute-start.11 = (bf16[128,3328]{1,0:T(8,128)(2,1)S(1)}, bf16[128,3328]{1,0:T(8,128)(2,1)S(1)}, u32[]{:S(2)}, u32[]{:S(2)}) collective-permute-start(bf16[128,3328]{1,0:T(8,128)(2,1)S(1)} %copy-done.53), channel_id=1, source_target_pairs={{0,16},{8,24},{16,0},{24,8},{1,17},{9,25},{17,1},{25,9},{2,18},{10... | collective-permute-start | bytes 2555912 | tf_op jit(solution)/shard_map/ppermute | solution.py:487
  69.9 21.1 %collective-permute-start.12 = (bf16[128,3328]{1,0:T(8,128)(2,1)S(1)}, bf16[128,3328]{1,0:T(8,128)(2,1)S(1)}, u32[]{:S(2)}, u32[]{:S(2)}) collective-permute-start(bf16[128,3328]{1,0:T(8,128)(2,1)S(1)} %collective-permute-done.7.refs_0_.refs_6_), channel_id=1, source_target_pairs={{0,8},{8,0},{16,24},{24,16},{1,9},{9,1},{17,25},{25,17},{2,10},{10... | collective-permute-start | bytes 2555912 | tf_op jit(solution)/shard_map/ppermute | solution.py:487
  70.2 20.8 %collective-permute-start.10 = (bf16[384,1024]{1,0:T(8,128)(2,1)S(1)}, bf16[384,1024]{1,0:T(8,128)(2,1)S(1)}, u32[]{:S(2)}, u32[]{:S(2)}) collective-permute-start(bf16[384,1024]{1,0:T(8,128)(2,1)S(1)} %collective-permute-done.6.refs_2_), channel_id=1, source_target_pairs={{2,0},{4,2},{6,4},{7,6},{5,7},{3,5},{1,3},{0,1},{10,8},{12,10},{14... | collective-permute-start | bytes 2359304 | tf_op jit(solution)/shard_map/ppermute | solution.py:505
  71.2 19.7 %collective-permute-start.9 = (bf16[384,1024]{1,0:T(8,128)(2,1)S(1)}, bf16[384,1024]{1,0:T(8,128)(2,1)S(1)}, u32[]{:S(2)}, u32[]{:S(2)}) collective-permute-start(bf16[384,1024]{1,0:T(8,128)(2,1)S(1)} %collective-permute-done.5.refs_1_), channel_id=1, source_target_pairs={{0,2},{2,4},{4,6},{6,7},{7,5},{5,3},{3,1},{1,0},{8,10},{10,12},{12... | collective-permute-start | bytes 2359304 | tf_op jit(solution)/shard_map/ppermute | solution.py:502
  72.2 18.7 %collective-permute-start.13 = (bf16[192,128]{1,0:T(8,128)(2,1)S(1)}, bf16[192,128]{1,0:T(8,128)(2,1)S(1)}, u32[]{:S(2)}, u32[]{:S(2)}) collective-permute-start(bf16[192,128]{1,0:T(8,128)(2,1)S(1)} %convert_element_type.68), channel_id=1, source_target_pairs={{0,2},{1,3},{2,0},{3,1},{4,6},{5,7},{6,4},{7,5},{8,10},{9,11},{10,... | collective-permute-start | bytes 147464 | tf_op jit(solution)/shard_map/ppermute | solution.py:487
  91.1 23.0 %collective-permute-start.16 = (bf16[128,3328]{1,0:T(8,128)(2,1)S(1)}, bf16[128,3328]{1,0:T(8,128)(2,1)S(1)}, u32[]{:S(2)}, u32[]{:S(2)}) collective-permute-start(bf16[128,3328]{1,0:T(8,128)(2,1)S(1)} %copy-done.52), channel_id=1, source_target_pairs={{0,16},{8,24},{16,0},{24,8},{1,17},{9,25},{17,1},{25,9},{2,18},{10... | collective-permute-start | bytes 2555912 | tf_op jit(solution)/shard_map/ppermute | solution.py:487
  93.0 20.7 %collective-permute-start.14 = (bf16[384,1024]{1,0:T(8,128)(2,1)S(1)}, bf16[384,1024]{1,0:T(8,128)(2,1)S(1)}, u32[]{:S(2)}, u32[]{:S(2)}) collective-permute-start(bf16[384,1024]{1,0:T(8,128)(2,1)S(1)} %collective-permute-done.9.refs_3_), channel_id=1, source_target_pairs={{0,2},{2,4},{4,6},{6,7},{7,5},{5,3},{3,1},{1,0},{8,10},{10,12},{12... | collective-permute-start | bytes 2359304 | tf_op jit(solution)/shard_map/ppermute | solution.py:502
  94.7 19.3 %collective-permute-start.15 = (bf16[384,1024]{1,0:T(8,128)(2,1)S(1)}, bf16[384,1024]{1,0:T(8,128)(2,1)S(1)}, u32[]{:S(2)}, u32[]{:S(2)}) collective-permute-start(bf16[384,1024]{1,0:T(8,128)(2,1)S(1)} %collective-permute-done.10.refs_4_), channel_id=1, source_target_pairs={{2,0},{4,2},{6,4},{7,6},{5,7},{3,5},{1,3},{0,1},{10,8},{12,10},{14... | collective-permute-start | bytes 2359304 | tf_op jit(solution)/shard_map/ppermute | solution.py:505
  132.3 19.1 %collective-permute-start.25 = (bf16[192,1024]{1,0:T(8,128)(2,1)S(1)}, bf16[192,1024]{1,0:T(8,128)(2,1)S(1)}, u32[]{:S(2)}, u32[]{:S(2)}) collective-permute-start(bf16[192,1024]{1,0:T(8,128)(2,1)S(1)} %get-tuple-element.241), channel_id=1, source_target_pairs={{0,2},{2,4},{4,6},{6,7},{7,5},{5,3},{3,1},{1,0},{8,10},{10,12},{12... | collective-permute-start | bytes 1179656 | tf_op jit(solution)/shard_map/ppermute | solution.py:502
  132.6 18.7 %collective-permute-start.26 = (bf16[192,1024]{1,0:T(8,128)(2,1)S(1)}, bf16[192,1024]{1,0:T(8,128)(2,1)S(1)}, u32[]{:S(2)}, u32[]{:S(2)}) collective-permute-start(bf16[192,1024]{1,0:T(8,128)(2,1)S(1)} %get-tuple-element.242), channel_id=1, source_target_pairs={{2,0},{4,2},{6,4},{7,6},{5,7},{3,5},{1,3},{0,1},{10,8},{12,10},{14... | collective-permute-start | bytes 1179656 | tf_op jit(solution)/shard_map/ppermute | solution.py:505
  153.0 24.0 %collective-permute-start.29 = (bf16[384,1024]{1,0:T(8,128)(2,1)}, bf16[384,1024]{1,0:T(8,128)(2,1)S(1)}, u32[]{:S(2)}, u32[]{:S(2)}) collective-permute-start(bf16[384,1024]{1,0:T(8,128)(2,1)} %get-tuple-element.264), channel_id=1, source_target_pairs={{0,2},{2,4},{4,6},{6,7},{7,5},{5,3},{3,1},{1,0},{8,10},{10,12},{12... | collective-permute-start | bytes 2359304 | tf_op jit(solution)/shard_map/ppermute | solution.py:502
  154.4 22.6 %collective-permute-start.30 = (bf16[384,1024]{1,0:T(8,128)(2,1)S(1)}, bf16[384,1024]{1,0:T(8,128)(2,1)S(1)}, u32[]{:S(2)}, u32[]{:S(2)}) collective-permute-start(bf16[384,1024]{1,0:T(8,128)(2,1)S(1)} %get-tuple-element.265), channel_id=1, source_target_pairs={{2,0},{4,2},{6,4},{7,6},{5,7},{3,5},{1,3},{0,1},{10,8},{12,10},{14... | collective-permute-start | bytes 2359304 | tf_op jit(solution)/shard_map/ppermute | solution.py:505
  177.0 25.4 %collective-permute-start.35 = (bf16[160,3328]{1,0:T(8,128)(2,1)}, bf16[160,3328]{1,0:T(8,128)(2,1)S(1)}, u32[]{:S(2)}, u32[]{:S(2)}) collective-permute-start(bf16[160,3328]{1,0:T(8,128)(2,1)} %get-tuple-element.290), channel_id=1, source_target_pairs={{0,16},{8,24},{16,0},{24,8},{1,17},{9,25},{17,1},{25,9},{2,18},{10... | collective-permute-start | bytes 3194888 | tf_op jit(solution)/shard_map/ppermute | solution.py:487
  179.8 20.2 %collective-permute-start.33 = (bf16[384,1024]{1,0:T(8,128)(2,1)S(1)}, bf16[384,1024]{1,0:T(8,128)(2,1)S(1)}, u32[]{:S(2)}, u32[]{:S(2)}) collective-permute-start(bf16[384,1024]{1,0:T(8,128)(2,1)S(1)} %get-tuple-element.287), channel_id=1, source_target_pairs={{0,2},{2,4},{4,6},{6,7},{7,5},{5,3},{3,1},{1,0},{8,10},{10,12},{12... | collective-permute-start | bytes 2359304 | tf_op jit(solution)/shard_map/ppermute | solution.py:502
  179.8 20.1 %collective-permute-start.34 = (bf16[384,1024]{1,0:T(8,128)(2,1)S(1)}, bf16[384,1024]{1,0:T(8,128)(2,1)S(1)}, u32[]{:S(2)}, u32[]{:S(2)}) collective-permute-start(bf16[384,1024]{1,0:T(8,128)(2,1)S(1)} %get-tuple-element.288), channel_id=1, source_target_pairs={{2,0},{4,2},{6,4},{7,6},{5,7},{3,5},{1,3},{0,1},{10,8},{12,10},{14... | collective-permute-start | bytes 2359304 | tf_op jit(solution)/shard_map/ppermute | solution.py:505
  202.5 26.2 %collective-permute-start.39 = (bf16[384,3328]{1,0:T(8,128)(2,1)}, bf16[384,3328]{1,0:T(8,128)(2,1)}, u32[]{:S(2)}, u32[]{:S(2)}) collective-permute-start(bf16[384,3328]{1,0:T(8,128)(2,1)} %backward_part.6), channel_id=1, source_target_pairs={{0,8},{8,0},{16,24},{24,16},{1,9},{9,1},{17,25},{25,17},{2,10},{10... | collective-permute-start | bytes 7667720 | tf_op jit(solution)/shard_map/ppermute | solution.py:487
  202.5 26.2 %collective-permute-start.40 = (bf16[160,3328]{1,0:T(8,128)(2,1)}, bf16[160,3328]{1,0:T(8,128)(2,1)}, u32[]{:S(2)}, u32[]{:S(2)}) collective-permute-start(bf16[160,3328]{1,0:T(8,128)(2,1)} %get-tuple-element.309), channel_id=1, source_target_pairs={{0,16},{8,24},{16,0},{24,8},{1,17},{9,25},{17,1},{25,9},{2,18},{10... | collective-permute-start | bytes 3194888 | tf_op jit(solution)/shard_map/ppermute | solution.py:487
  205.2 20.8 %collective-permute-start.37 = (bf16[384,1024]{1,0:T(8,128)(2,1)S(1)}, bf16[384,1024]{1,0:T(8,128)(2,1)S(1)}, u32[]{:S(2)}, u32[]{:S(2)}) collective-permute-start(bf16[384,1024]{1,0:T(8,128)(2,1)S(1)} %get-tuple-element.305), channel_id=1, source_target_pairs={{0,2},{2,4},{4,6},{6,7},{7,5},{5,3},{3,1},{1,0},{8,10},{10,12},{12... | collective-permute-start | bytes 2359304 | tf_op jit(solution)/shard_map/ppermute | solution.py:502
  205.3 20.8 %collective-permute-start.38 = (bf16[384,1024]{1,0:T(8,128)(2,1)S(1)}, bf16[384,1024]{1,0:T(8,128)(2,1)S(1)}, u32[]{:S(2)}, u32[]{:S(2)}) collective-permute-start(bf16[384,1024]{1,0:T(8,128)(2,1)S(1)} %get-tuple-element.306), channel_id=1, source_target_pairs={{2,0},{4,2},{6,4},{7,6},{5,7},{3,5},{1,3},{0,1},{10,8},{12,10},{14... | collective-permute-start | bytes 2359304 | tf_op jit(solution)/shard_map/ppermute | solution.py:505
  230.5 41.6 %collective-permute-start.42 = (bf16[384,1024]{1,0:T(8,128)(2,1)}, bf16[384,1024]{1,0:T(8,128)(2,1)}, u32[]{:S(2)}, u32[]{:S(2)}) collective-permute-start(bf16[384,1024]{1,0:T(8,128)(2,1)} %last_add.1), channel_id=1, source_target_pairs={{0,0},{1,1},{2,8},{3,9},{4,16},{5,17},{6,24},{7,25},{8,2},{9,3},{1... | collective-permute-start | bytes 2359304 | tf_op jit(solution)/shard_map/ppermute | solution.py:495
  238.0 34.0 %collective-permute-start.43 = (bf16[64,3328]{1,0:T(8,128)(2,1)}, bf16[64,3328]{1,0:T(8,128)(2,1)}, u32[]{:S(2)}, u32[]{:S(2)}) collective-permute-start(bf16[64,3328]{1,0:T(8,128)(2,1)} %get-tuple-element.327), channel_id=1, source_target_pairs={{0,16},{8,24},{16,0},{24,8},{1,17},{9,25},{17,1},{25,9},{2,18},{10... | collective-permute-start | bytes 1277960 | tf_op jit(solution)/shard_map/ppermute | solution.py:487
  243.2 18.8 %collective-permute-start.44 = (bf16[64,1024]{1,0:T(8,128)(2,1)}, bf16[64,1024]{1,0:T(8,128)(2,1)}, u32[]{:S(2)}, u32[]{:S(2)}) collective-permute-start(bf16[64,1024]{1,0:T(8,128)(2,1)} %get-tuple-element.331), channel_id=1, source_target_pairs={{0,8},{8,0},{16,24},{24,16},{1,9},{9,1},{17,25},{25,17},{2,10},{10... | collective-permute-start | bytes 393224 | tf_op jit(solution)/shard_map/ppermute | solution.py:487
  243.2 22.0 %collective-permute-start.45 = (bf16[64,1024]{1,0:T(8,128)(2,1)}, bf16[64,1024]{1,0:T(8,128)(2,1)}, u32[]{:S(2)}, u32[]{:S(2)}) collective-permute-start(bf16[64,1024]{1,0:T(8,128)(2,1)} %get-tuple-element.332), channel_id=1, source_target_pairs={{0,16},{8,24},{16,0},{24,8},{1,17},{9,25},{17,1},{25,9},{2,18},{10... | collective-permute-start | bytes 393224 | tf_op jit(solution)/shard_map/ppermute | solution.py:487
  245.2 24.1 %collective-permute-start.46 = (bf16[64,1024]{1,0:T(8,128)(2,1)}, bf16[64,1024]{1,0:T(8,128)(2,1)}, u32[]{:S(2)}, u32[]{:S(2)}) collective-permute-start(bf16[64,1024]{1,0:T(8,128)(2,1)} %get-tuple-element.333), channel_id=1, source_target_pairs={{0,24},{8,16},{16,8},{24,0},{1,25},{9,17},{17,9},{25,1},{2,26},{10... | collective-permute-start | bytes 393224 | tf_op jit(solution)/shard_map/ppermute | solution.py:487
  (72 other events, 843.1 us)
